TPU v7x, 32 devices: a whole 2x2x4 slice. The times are simulated.
32 devices in a mesh: row: 4 (over z), col: 8 (over y, x, core).
Axes of the slice: x: 2, y: 2, z: 4, core: 2. Of those that a mesh axis runs over, the one named last changes fastest.
Arguments:
- gate_pre: bfloat16 [512, 16384], P('row', 'col'), may hold values from -6 to 6
- up_pre: bfloat16 [512, 16384], P('row', 'col'), may hold values from -6 to 6
- down_weight: bfloat16 [8192, 16384], P('row', 'col'), may hold values from -0.09375 to 0.09375
- block_mask: int32 [64, 128], P('row', 'col'), may hold values from 0 to 1, as said below
- cotangent: bfloat16 [512, 8192], P('row', 'col'), may hold values from -6 to 6
Outputs:
- output: bfloat16 [512, 8192], P('row', 'col')
- d_gate: bfloat16 [512, 16384], P('row', 'col')
- d_up: bfloat16 [512, 16384], P('row', 'col')
- d_down: bfloat16 [8192, 16384], P('row', 'col')
Inputs may be any that keep to these rules, and one draw needn't show every extreme that they name: `block_mask`: each device's tile of 16 x 16 blocks keeps between 64 and 192 blocks; in every draw some tile keeps exactly 192.
All inputs are finite; a program needn't handle non-finite values.
Results may differ from a plain program's by a relative error of at most 0.015.
Values may be sent and summed in bfloat16 or wider, within the bound.
No kernel may reach another device: no remote copies, remote signals or barrier semaphores. Data moves between devices by JAX's collectives and lax.ppermute only.
A program may use at most 128 MiB of HBM per device.

v0:
```python
import jax
import jax.numpy as jnp
from jax import lax
from jax.sharding import PartitionSpec as P


def rounded_f32(values):
    return lax.optimization_barrier(values.astype(jnp.bfloat16)).astype(jnp.float32)


def body(gate_pre, up_pre, down_weight, block_mask, cotangent):
    tok_rows, ff_cols = gate_pre.shape
    d_rows = down_weight.shape[0]
    tile_r, tile_c = block_mask.shape
    block_size = d_rows // tile_r
    gate_wide = gate_pre.astype(jnp.float32)
    up_wide = up_pre.astype(jnp.float32)
    activated = jax.nn.silu(gate_wide)
    hidden = (activated * up_wide).astype(jnp.bfloat16)
    expand = jnp.repeat(jnp.repeat(block_mask, block_size, axis=0), block_size, axis=1)
    masked = jnp.where(expand > 0, down_weight, jnp.zeros_like(down_weight))
    cot_row = lax.all_gather(cotangent, "col", axis=1, tiled=True)
    cot_all = lax.all_to_all(cot_row, "row", split_axis=1, concat_axis=0, tiled=True)
    panel = lax.all_gather(masked, "row", axis=0, tiled=True)
    columns = lax.dot_general(
        hidden, panel, (((1,), (1,)), ((), ())), preferred_element_type=jnp.float32
    )
    y_partial = columns
    shards = panel.shape[0] // d_rows
    per_shard = jnp.einsum(
        "tnd,ndf->ntf",
        cot_row.reshape(tok_rows, shards, d_rows),
        panel.reshape(shards, d_rows, ff_cols),
        preferred_element_type=jnp.float32,
    )
    d_hidden = jnp.sum(rounded_f32(per_shard), axis=0)
    y_partial, d_hidden = (y_partial, d_hidden)
    y_summand = rounded_f32(y_partial)
    hidden_all = lax.all_gather(hidden, "row", axis=0, tiled=True)
    grad_full = lax.dot_general(
        cot_all, hidden_all, (((0,), (0,)), ((), ())), preferred_element_type=jnp.float32
    )
    output = lax.psum_scatter(
        y_summand.astype(jnp.bfloat16), "col", scatter_dimension=1, tiled=True
    )
    sigmoid_g = jax.nn.sigmoid(gate_wide)
    d_gate = (d_hidden * up_wide * sigmoid_g * (1.0 + gate_wide * (1.0 - sigmoid_g))).astype(
        jnp.bfloat16
    )
    d_up = (d_hidden * activated).astype(jnp.bfloat16)
    d_down = jnp.where(expand > 0, grad_full, jnp.zeros_like(grad_full)).astype(jnp.bfloat16)
    return (output, d_gate, d_up, d_down)


def solution(mesh):
    in_specs = (P("row", "col"), P("row", "col"), P("row", "col"), P("row", "col"), P("row", "col"))
    out_specs = (P("row", "col"), P("row", "col"), P("row", "col"), P("row", "col"))
    return jax.shard_map(body, mesh=mesh, in_specs=in_specs, out_specs=out_specs, check_vma=False)
```

profile of v0, /device:TPU:16, one launch (start us, length us, event | category | flops | bytes accessed | tf_op | source)
XLA Modules:
  0.0 792.2 jit_solution(9814608847167343371)
XLA Ops:
  7.2 0.0 all-gather.4.cloned.1.call-start
  7.2 0.7 broadcast_compare_fusion
  7.9 0.1 copy.29
  8.0 0.1 broadcast_in_dim.12
  8.1 12.2 %copy.30 = bf16[2048,2048]{0,1:T(8,128)(2,1)} copy(bf16[2048,2048]{1,0:T(8,128)(2,1)} %param.7) | data formatting | bytes 16777216 | tf_op args[2]
  20.4 7.4 bitcast_select_fusion.1
  27.8 0.0 all-gather.4.cloned.1.call-update
  27.8 0.0 all-gather.6.cloned.1.call-start
  27.9 0.9 copy-done.4
  28.7 0.8 copy.32
  29.6 0.0 all-gather.6.cloned.1.call-update
  29.6 0.0 all-gather.8.cloned.1.call-start
  29.7 0.3 copy.27
  29.9 0.0 copy-done.3
  29.9 1.0 copy.28
  30.9 557.7 %all-gather.4.cloned.1.call-done = bf16[8192,2048]{0,1:T(8,128)(2,1)} async-done(((bf16[2048,2048]{0,1:T(8,128)(2,1)}), bf16[8192,2048]{0,1:T(8,128)(2,1)}) %all-gather.4.cloned.1.call-update) | async-done | bytes 33554448 | tf_op jit(solution)/shard_map/all_gather | solution.py:24
  588.7 40.7 %copy.31 = bf16[8192,2048]{1,0:T(8,128)(2,1)} copy(bf16[8192,2048]{0,1:T(8,128)(2,1)} %all-gather.4.cloned.1.call-done) | data formatting | bytes 67108864 | tf_op jit(solution)/shard_map/all_gather | solution.py:24
  629.4 17.8 %fusion.1 = bf16[4,128,2048]{1,2,0:T(8,128)(2,1)S(1)} fusion(bf16[4,2048,2048]{2,1,0:T(8,128)(2,1)} %bitcast.25, bf16[128,4,2048]{0,2,1:T(8,128)(2,1)} %bitcast.2), kind=kOutput, calls=%fused_computation.6 | convolution fusion | flops 4296015872 | bytes 37748736 | tf_op jit(solution)/shard_map/tnd,ndf->ntf/dot_general | solution.py:30
  647.2 0.3 convert_reduce_fusion
  647.6 2.6 multiply_convert_fusion
  650.2 0.0 all-gather.8.cloned.1.call-update
  650.2 7.7 all-to-all-start
  657.9 0.0 reduce-scatter.2.cloned.1.call-start
  657.9 17.2 %convolution_convert_fusion = bf16[128,8192]{1,0:T(8,128)(2,1)} fusion(bf16[128,2048]{0,1:T(8,128)(2,1)S(1)} %copy-done, bf16[8192,2048]{0,1:T(8,128)(2,1)} %all-gather.4.cloned.1.call-done), kind=kOutput, calls=%fused_computation.3 | convolution fusion | flops 4296015872 | bytes 36175872 | tf_op jit(solution)/shard_map/dot_general | solution.py:25
  675.2 0.0 reduce-scatter.2.cloned.1.call-update
  675.2 61.7 %all-to-all-done = bf16[128,4,2048]{0,2,1:T(8,128)(2,1)S(1)} async-done(((bf16[128,4,2048]{0,2,1:T(8,128)(2,1)}), bf16[128,4,2048]{0,2,1:T(8,128)(2,1)S(1)}, u32[]{:S(2)}, u32[]{:S(2)}) %all-to-all-start) | async-done | bytes 2097184 | tf_op jit(solution)/shard_map/all_to_all | solution.py:23
  736.9 2.6 copy.35
  739.4 1.0 copy.36
  740.4 1.0 copy.37
  741.5 10.0 %fusion = bf16[2048,2048]{0,1:T(8,128)(2,1)} fusion(bf16[512,2048]{0,1:T(8,128)(2,1)} %all-gather.8.cloned.1.call-done, bf16[512,2048]{1,0:T(8,128)(2,1)} %bitcast.27, pred[2048,16]{0,1:T(8,128)(4,1)S(1)} %bitcast.29), kind=kOutput, calls=%fused_computation.2 | convolution fusion | flops 4303355904 | bytes 12615680 | tf_op jit(solution)/shard_map/dot_general | solution.py:40
  751.4 12.4 %copy.38 = bf16[2048,2048]{1,0:T(8,128)(2,1)} copy(bf16[2048,2048]{0,1:T(8,128)(2,1)} %fusion) | data formatting | bytes 16777216
  763.8 21.9 %reduce-scatter.2.cloned.1.call-done = bf16[128,1024]{1,0:T(8,128)(2,1)} async-done(((bf16[128,8192]{1,0:T(8,128)(2,1)}), bf16[128,1024]{1,0:T(8,128)(2,1)}) %reduce-scatter.2.cloned.1.call-update) | async-done | bytes 262160 | tf_op jit(solution)/shard_map/reduce_scatter | solution.py:43
  (11 shorter events, 0.0 us)
Async XLA Ops:
  7.2 581.5 %all-gather.4.cloned.1.call-start = ((), (), s32[]{:S(2)}) async-start(), calls=%async_computation.2 | async-start | bytes 41943040 | tf_op jit(solution)/shard_map/all_gather | solution.py:24
  27.8 0.9 copy-start.4
  27.8 1.9 copy-start.2
  27.8 2.1 copy-start.3
  27.8 601.6 %all-gather.6.cloned.1.call-start = ((), (), s32[]{:S(2)}) async-start(), calls=%async_computation.4 | async-start | bytes 2359296 | tf_op jit(solution)/shard_map/all_gather | solution.py:22
  29.6 711.9 %all-gather.8.cloned.1.call-start = ((), (), s32[]{:S(2)}) async-start(), calls=%async_computation.5 | async-start | bytes 2621440 | tf_op jit(solution)/shard_map/all_gather | solution.py:39
  650.2 7.7 copy-start
  650.2 86.6 %all-to-all-start = ((bf16[128,4,2048]{0,2,1:T(8,128)(2,1)}), bf16[128,4,2048]{0,2,1:T(8,128)(2,1)S(1)}, u32[]{:S(2)}, u32[]{:S(2)}) async-start(bf16[128,4,2048]{0,2,1:T(8,128)(2,1)} %bitcast.2), calls=%async_computation.1 | async-start | bytes 4194304 | tf_op jit(solution)/shard_map/all_to_all | solution.py:23
  657.9 127.7 %reduce-scatter.2.cloned.1.call-start = ((), (), s32[]{:S(2)}) async-start(), calls=%async_computation.3 | async-start | bytes 2359296 | tf_op jit(solution)/shard_map/reduce_scatter | solution.py:43
  675.2 64.3 %copy-start.1 = (bf16[128,2048]{0,1:T(8,128)(2,1)S(1)}, bf16[128,2048]{0,1:T(8,128)(2,1)}, u32[]{:S(2)}) copy-start(bf16[128,2048]{0,1:T(8,128)(2,1)} %get-tuple-element.21) | copy-start | bytes 1572868
Sparse Core Ops, SparseCore 0:
  27.9 560.7 all-gather.3
  591.1 27.8 all-gather.5
  650.3 84.5 all-gather.7
  738.7 46.9 reduce-scatter.1
where the time goes:
time: 796 us; the launch traced here: 792 us
  waiting for transfers between devices  641 us (81%)
  local copies, waits for them, and re-layouts  73.1 us (9%)
  matrix products  45 us (6%)
  between operations  13.8 us (2%)
  other arithmetic  11.1 us (1%)
    all_gather x1, waiting for transfers between devices, body(): panel = lax.all_gather(masked, 'row', axis=0, tiled=True)  558 us
    all_to_all x1, waiting for transfers between devices, body(): lax.all_to_all(cot_row, 'row', split_axis=1, concat_axis=0, tiled=True)  61.7 us
    all_gather x1, local copies, waits for them, and re-layouts, body(): panel = lax.all_gather(masked, 'row', axis=0, tiled=True)  40.7 us
    unnamed x18, local copies, waits for them, and re-layouts  29.6 us
    reduce_scatter x1, waiting for transfers between devices, body(): lax.psum_scatter(y_summand.astype(jnp.bfloat16), 'col', scatter_dimension...  21.9 us
    dot_general x1, matrix products, body(): jnp.einsum('tnd,ndf->ntf', cot_row.reshape(tok_rows, shards, d_rows), pan...  17.8 us
    dot_general x1, matrix products, body(): lax.dot_general(hidden, panel, (((1,), (1,)), ((), ())), preferred_elemen...  17.2 us
  transfers between devices with their start and end apart: 5, of which 3 were waited for; matrix products, arithmetic and copies ran while one was open for 11% of the time, Pallas kernels for 0%

commit v1 on v0

v1 whole, which is shorter than its diff:
```python
import jax
import jax.numpy as jnp
from jax import lax
from jax.experimental import pallas as pl
from jax.experimental.pallas import tpu as pltpu
from jax.sharding import PartitionSpec as P

F32 = jnp.float32
BF16 = jnp.bfloat16
VMEM = pl.BlockSpec(memory_space=pltpu.VMEM)
SMEM = pl.BlockSpec(memory_space=pltpu.SMEM)
PARAMS = pltpu.CompilerParams(vmem_limit_bytes=40 * 2**20)


def in_vmem(array):
    return pltpu.with_memory_space_constraint(array, pltpu.VMEM)


def place():
    col = lax.axis_index("col")
    return lax.axis_index("row"), col // 2, col % 2


def call(kernel, name, outs, *args, specs=None, scratch=(), flops=0):
    moved = sum(a.size * a.dtype.itemsize for a in args)
    return pl.pallas_call(
        kernel,
        in_specs=specs or [VMEM] * len(args),
        out_specs=[VMEM] * len(outs),
        out_shape=[pltpu.VMEM(shape, dtype) for shape, dtype in outs],
        scratch_shapes=list(scratch),
        compiler_params=PARAMS,
        cost_estimate=pl.CostEstimate(flops=flops, bytes_accessed=moved, transcendentals=0),
        name=name,
    )(*args)


def masked_weight(weight, mask):
    rows, cols = weight.shape
    tile_r, tile_c = mask.shape
    size_r, size_c = rows // tile_r, cols // tile_c

    def kernel(w_ref, m_ref, o_ref, sem):
        def copy(i):
            part = pl.ds(i * size_r, size_r)
            return pltpu.make_async_copy(w_ref.at[part], o_ref.at[part], sem.at[i])

        for i in range(tile_r):
            copy(i).start()
        for i in range(tile_r):
            copy(i).wait()
            for j in range(tile_c):

                @pl.when(m_ref[i, j] == 0)
                def _():
                    o_ref[i * size_r : (i + 1) * size_r, j * size_c : (j + 1) * size_c] = (
                        jnp.zeros((size_r, size_c), BF16)
                    )

    return call(
        kernel,
        "masked_weight",
        [((rows, cols), BF16)],
        weight,
        mask,
        specs=[pl.BlockSpec(memory_space=pl.ANY), SMEM],
        scratch=[pltpu.SemaphoreType.DMA((tile_r,))],
    )[0]


def quarters(cot, chips):
    tok, width = cot.shape
    part = tok // chips

    def kernel(x_ref, *outs):
        _, a, _ = place()
        for u in range(chips):
            outs[u][...] = x_ref[pl.ds(pl.multiple_of((a ^ u) * part, part), part), :]

    return call(kernel, "quarters", [((part, width), BF16)] * chips, in_vmem(cot))


def choose(pieces, order):
    n = len(pieces)

    def kernel(*refs):
        r, a, _ = place()
        for i, t in enumerate(order):
            for u in range(n):

                @pl.when((r ^ a ^ t) == u)
                def _():
                    refs[n + i][...] = refs[u][...]

    shape = (pieces[0].shape, BF16)
    return call(kernel, "choose", [shape] * len(order), *map(in_vmem, pieces))


def back_product(parts, weight, tok):
    chips = len(parts[0])
    flat = [piece for half in parts for piece in half]
    chunk, width = flat[0].shape
    part = tok // chips
    blocks = chunk // part
    dr, ff = weight.shape
    step = 512

    def kernel(*refs):
        w_ref = refs[len(flat)]
        c_ref, *outs = refs[len(flat) + 1 :]
        _, a, h = place()
        for w in range(2):
            lanes = pl.ds(pl.multiple_of((h ^ w) * width, width), width)
            for u in range(chips):
                for b in range(blocks):
                    rows = pl.ds(pl.multiple_of(b * tok + (a ^ u) * part, part), part)
                    c_ref[rows, lanes] = refs[w * chips + u][b * part : (b + 1) * part, :]
        for j in range(0, ff, step):
            product = jnp.dot(
                c_ref[...], w_ref[:, j : j + step], preferred_element_type=F32
            ).astype(BF16)
            for b in range(blocks):
                outs[b][:, j : j + step] = product[b * tok : (b + 1) * tok]

    return call(
        kernel,
        "back_product",
        [((blocks * tok, dr), BF16)] + [((tok, ff), BF16)] * blocks,
        *map(in_vmem, flat),
        in_vmem(weight),
        flops=2 * blocks * tok * dr * ff,
    )


def out_product(hidden, weight, own, dtype):
    tok, ff = hidden[0].shape
    half = weight.shape[0] // 2
    n = len(hidden)
    step = 512

    def kernel(*refs):
        w_ref, o_ref = refs[n:]
        _, _, h = place()
        first = (h if own else 1 - h) * half
        lhs = jnp.concatenate([ref[...] for ref in refs[:n]], axis=0)
        for j in range(0, half, step):
            rows = pl.ds(pl.multiple_of(first + j, step), step)
            o_ref[:, j : j + step] = lax.dot_general(
                lhs, w_ref[rows, :], (((1,), (1,)), ((), ())), preferred_element_type=F32
            ).astype(dtype)

    return call(
        kernel,
        "out_product",
        [((n * tok, half), dtype)],
        *map(in_vmem, hidden),
        in_vmem(weight),
        flops=2 * n * tok * half * ff,
    )[0]


def pair_sum(own, received, tok, chips):
    rows, width = own.shape
    blocks, part = rows // tok, tok // chips

    def kernel(x_ref, y_ref, *outs):
        _, a, _ = place()
        for u in range(chips):
            for b in range(blocks):
                at = pl.ds(pl.multiple_of(b * tok + (a ^ u) * part, part), part)
                outs[u][b * part : (b + 1) * part, :] = (
                    x_ref[at, :] + y_ref[at, :].astype(F32)
                ).astype(BF16)

    return call(
        kernel,
        "pair_sum",
        [((blocks * part, width), BF16)] * chips,
        in_vmem(own),
        in_vmem(received),
    )


def plane_sum(chunks, orders, part):
    flat = [piece for chunk in chunks for piece in chunk]
    chips = len(chunks[0])
    width = flat[0].shape[1]
    count = sum(map(len, orders))

    def kernel(*refs):
        outs = refs[len(flat) :]
        r, a, _ = place()
        for i, order in enumerate(orders):
            for b, t in enumerate(order):
                total = jnp.zeros((part, width), F32)
                for u in range(chips):
                    total += refs[i * chips + u][b * part : (b + 1) * part, :].astype(F32)
                total = total.astype(BF16)
                for k in range(count):

                    @pl.when((r ^ a ^ k) == t)
                    def _():
                        outs[k][...] = total

    return call(
        kernel, "plane_sum", [((part, width), BF16)] * count, *map(in_vmem, flat)
    )


def assemble(pieces):
    n = len(pieces)
    part, width = pieces[0].shape

    def kernel(*refs):
        r, _, _ = place()
        for k in range(n):
            refs[n][pl.ds(pl.multiple_of((r ^ k) * part, part), part), :] = refs[k][...]

    return pl.pallas_call(
        kernel,
        in_specs=[VMEM] * n,
        out_specs=VMEM,
        out_shape=jax.ShapeDtypeStruct((n * part, width), BF16),
        compiler_params=PARAMS,
        name="assemble",
    )(*map(in_vmem, pieces))


def down_gradient(cots, hidden, mask):
    tok, ff = hidden[0].shape
    dr = cots[0].shape[1]
    tokens = tok * len(hidden)
    tile_r, tile_c = mask.shape
    size_r, size_c = dr // tile_r, ff // tile_c
    step = 512
    nc, nh = len(cots), len(hidden)

    def kernel(*refs):
        m_ref, o_ref, h_all, c_all = refs[nc + nh :]
        i = pl.program_id(0)

        @pl.when(i == 0)
        def _():
            for t in range(nh):
                h_all[t * tok : (t + 1) * tok, :] = refs[nc + t][...]

        at = 0
        for c in range(nc):
            c_all[at : at + cots[c].shape[0], :] = refs[c][...]
            at += cots[c].shape[0]
        o_ref[...] = lax.dot_general(
            c_all[...], h_all[...], (((0,), (0,)), ((), ())), preferred_element_type=F32
        ).astype(BF16)
        for b in range(step // size_r):
            for j in range(tile_c):

                @pl.when(m_ref[i * (step // size_r) + b, j] == 0)
                def _():
                    o_ref[b * size_r : (b + 1) * size_r, j * size_c : (j + 1) * size_c] = (
                        jnp.zeros((size_r, size_c), BF16)
                    )

    return pl.pallas_call(
        kernel,
        grid=(dr // step,),
        in_specs=[pl.BlockSpec((c.shape[0], step), lambda i: (0, i)) for c in cots]
        + [VMEM] * nh
        + [SMEM],
        out_specs=pl.BlockSpec((step, ff), lambda i: (i, 0)),
        out_shape=jax.ShapeDtypeStruct((dr, ff), BF16),
        scratch_shapes=[pltpu.VMEM((tokens, ff), BF16), pltpu.VMEM((tokens, step), BF16)],
        compiler_params=PARAMS,
        cost_estimate=pl.CostEstimate(
            flops=2 * tokens * dr * ff, bytes_accessed=2 * dr * ff, transcendentals=0
        ),
        name="down_gradient",
    )(*map(in_vmem, cots), *map(in_vmem, hidden), mask)


def fast_body(gate_pre, up_pre, down_weight, block_mask, cotangent):
    rows, chips = 4, 4
    tok = gate_pre.shape[0]
    part = tok // chips

    def over_row(x, t):
        return lax.ppermute(x, "row", [(i, i ^ t) for i in range(rows)])

    def over_chips(x, u):
        return lax.ppermute(x, "col", [(j, j ^ (2 * u)) for j in range(2 * chips)])

    def over_core(x):
        return lax.ppermute(x, "col", [(j, j ^ 1) for j in range(2 * chips)])

    spread = quarters(cotangent, chips)
    spread = [spread[0]] + [over_chips(spread[u], u) for u in range(1, chips)]

    gate_wide = gate_pre.astype(F32)
    up_wide = up_pre.astype(F32)
    activated = jax.nn.silu(gate_wide)
    hidden = {0: (activated * up_wide).astype(BF16)}
    hidden[1] = over_row(hidden[0], 1)
    hidden[3] = over_row(hidden[0], 3)

    weight = masked_weight(down_weight, block_mask)

    ours = choose(spread, (2, 3, 1, 0))
    cot = {t: over_row(x, t) for t, x in zip((2, 3, 1), ours)}
    cot[0] = ours[3]

    chunk_cot, back = [], {}
    for order in ((2, 3), (1, 0)):
        mine = jnp.concatenate([cot[t] for t in order], axis=0)
        same = [mine] + [over_chips(mine, u) for u in range(1, chips)]
        other = [over_core(x) for x in same]
        gathered, *blocks = back_product([same, other], weight, tok)
        chunk_cot.append(gathered)
        back.update(zip(order, blocks))

    near = over_row(back[2], 1)
    paired = (back[3].astype(F32) + near.astype(F32)).astype(BF16)
    far = over_row(paired, 3)
    beside = over_row(back[1], 1)
    d_hidden = back[0].astype(F32) + beside.astype(F32) + far.astype(F32)
    sigmoid_g = jax.nn.sigmoid(gate_wide)
    d_gate = (d_hidden * up_wide * sigmoid_g * (1.0 + gate_wide * (1.0 - sigmoid_g))).astype(BF16)
    d_up = (d_hidden * activated).astype(BF16)

    hidden[2] = over_row(hidden[3], 1)

    orders = ((0, 1, 3), (2,))
    sums = []
    for order in orders:
        blocks = [hidden[t] for t in order]
        received = over_core(out_product(blocks, weight, False, BF16))
        pieces = pair_sum(out_product(blocks, weight, True, F32), received, tok, chips)
        sums.append([pieces[0]] + [over_chips(pieces[u], u) for u in range(1, chips)])
    ready = plane_sum(sums, orders, part)
    width = 2 * chips
    placed = [
        lax.ppermute(
            ready[k],
            ("row", "col"),
            [
                (r * width + 2 * a + h, (a ^ k) * width + 2 * r + h)
                for r in range(rows)
                for a in range(chips)
                for h in range(2)
            ],
        )
        for k in range(rows)
    ]
    output = assemble(placed)

    d_down = down_gradient(chunk_cot, [hidden[t] for t in (2, 3, 1, 0)], block_mask)
    return output, d_gate, d_up, d_down


def rounded_f32(values):
    return lax.optimization_barrier(values.astype(BF16)).astype(F32)


def general_body(gate_pre, up_pre, down_weight, block_mask, cotangent):
    tok_rows, ff_cols = gate_pre.shape
    d_rows = down_weight.shape[0]
    block_size = d_rows // block_mask.shape[0]
    gate_wide = gate_pre.astype(F32)
    up_wide = up_pre.astype(F32)
    activated = jax.nn.silu(gate_wide)
    hidden = (activated * up_wide).astype(BF16)
    expand = jnp.repeat(jnp.repeat(block_mask, block_size, axis=0), block_size, axis=1)
    masked = jnp.where(expand > 0, down_weight, jnp.zeros_like(down_weight))
    cot_row = lax.all_gather(cotangent, "col", axis=1, tiled=True)
    cot_all = lax.all_to_all(cot_row, "row", split_axis=1, concat_axis=0, tiled=True)
    panel = lax.all_gather(masked, "row", axis=0, tiled=True)
    y_partial = lax.dot_general(
        hidden, panel, (((1,), (1,)), ((), ())), preferred_element_type=F32
    )
    shards = panel.shape[0] // d_rows
    per_shard = jnp.einsum(
        "tnd,ndf->ntf",
        cot_row.reshape(tok_rows, shards, d_rows),
        panel.reshape(shards, d_rows, ff_cols),
        preferred_element_type=F32,
    )
    d_hidden = jnp.sum(rounded_f32(per_shard), axis=0)
    hidden_all = lax.all_gather(hidden, "row", axis=0, tiled=True)
    grad_full = lax.dot_general(
        cot_all, hidden_all, (((0,), (0,)), ((), ())), preferred_element_type=F32
    )
    output = lax.psum_scatter(y_partial.astype(BF16), "col", scatter_dimension=1, tiled=True)
    sigmoid_g = jax.nn.sigmoid(gate_wide)
    d_gate = (d_hidden * up_wide * sigmoid_g * (1.0 + gate_wide * (1.0 - sigmoid_g))).astype(BF16)
    d_up = (d_hidden * activated).astype(BF16)
    d_down = jnp.where(expand > 0, grad_full, jnp.zeros_like(grad_full)).astype(BF16)
    return output, d_gate, d_up, d_down


def solution(mesh):
    spec = P("row", "col")
    small = mesh.shape["row"] == 4 and mesh.shape["col"] == 8
    return jax.shard_map(
        fast_body if small else general_body,
        mesh=mesh,
        in_specs=(spec,) * 5,
        out_specs=(spec,) * 4,
        check_vma=False,
    )
```

time: 796 us -> 160 us (0.20)
  waiting for transfers between devices: 641 us -> 88.8 us
  local copies, waits for them, and re-layouts: 73.1 us -> 1.67 us
  matrix products: 45 us -> 0 us
  starting transfers between devices: 7.83 us -> 39.4 us
  Pallas kernels: 0 us -> 26.9 us
  between operations: 13.8 us -> 0.89 us
  other arithmetic: 11.1 us -> 1.9 us
    all_gather x3 -> x0, waiting for transfers between devices: 558 us -> none  [the longest x1 558 us: body(): panel = lax.all_gather(masked, 'row', axis=0, tiled=True)]
    ppermute x0 -> x38, waiting for transfers between devices: none -> 88.8 us  [the longest x9 64.7 us: over_row(): return lax.ppermute(x, 'row', [(i, i ^ t) for i in range(rows)])]
    all_to_all x1 -> x0, waiting for transfers between devices: 61.7 us -> none  [body(): lax.all_to_all(cot_row, 'row', split_axis=1, concat_axis=0, tiled=True)]
    dot_general x3 -> x0, matrix products: 45 us -> none  [the longest x1 17.8 us: body(): jnp.einsum('tnd,ndf->ntf', cot_row.reshape(tok_rows, shards, d_rows), pan...]
    all_gather x1 -> x0, local copies, waits for them, and re-layouts: 40.7 us -> none  [body(): panel = lax.all_gather(masked, 'row', axis=0, tiled=True)]
    ppermute x0 -> x38, starting transfers between devices: none -> 39.4 us  [the longest x15 17.1 us: over_chips(): return lax.ppermute(x, 'col', [(j, j ^ 2 * u) for j in range(2 * chips)])]
    unnamed x18 -> x10, local copies, waits for them, and re-layouts: 29.6 us -> 1.66 us
    pallas_call x0 -> x14, Pallas kernels: none -> 26.9 us  [the longest x12 16.5 us: call(): pl.pallas_call(kernel, in_specs=specs or [VMEM] * len(args), out_specs=[V...]
  transfers between devices with their start and end apart: 5 -> 38, of which waited for: 3 -> 18; matrix products, arithmetic and copies ran while one was open for 11% -> 0% of each run, Pallas kernels for 0% -> 14%
where the time goes in v1:
time: 160 us
  waiting for transfers between devices  88.8 us (56%)
  starting transfers between devices  39.4 us (25%)
  Pallas kernels  26.9 us (17%)
  other arithmetic  1.9 us (1%)
  local copies, waits for them, and re-layouts  1.67 us (1%)
    ppermute x9, waiting for transfers between devices, over_row(): return lax.ppermute(x, 'row', [(i, i ^ t) for i in range(rows)])  64.7 us
    ppermute x15, waiting for transfers between devices, over_chips(): return lax.ppermute(x, 'col', [(j, j ^ 2 * u) for j in range(2 * chips)])  23.1 us
    ppermute x15, starting transfers between devices, over_chips(): return lax.ppermute(x, 'col', [(j, j ^ 2 * u) for j in range(2 * chips)])  17.1 us
    pallas_call x12, Pallas kernels, call(): pl.pallas_call(kernel, in_specs=specs or [VMEM] * len(args), out_specs=[V...  16.5 us
    ppermute x4, starting transfers between devices, fast_body(): lax.ppermute(ready[k], ('row', 'col'), [(r * width + 2 * a + h, (a ^ k) *...  10.7 us
    ppermute x9, starting transfers between devices, over_row(): return lax.ppermute(x, 'row', [(i, i ^ t) for i in range(rows)])  10.5 us
    pallas_call x1, Pallas kernels, down_gradient(): pl.pallas_call(kernel, grid=(dr // step,), in_specs=[pl.BlockSpec((c.shap...  9.68 us
  transfers between devices with their start and end apart: 38, of which 18 were waited for; matrix products, arithmetic and copies ran while one was open for 0% of the time, Pallas kernels for 14%

profile of v1, /device:TPU:16, one launch (start us, length us, event | category | flops | bytes accessed | tf_op | source)
XLA Modules:
  0.0 159.5 jit_solution(13164065039416331999)
XLA Ops:
  1.6 1.6 collective-permute-start.15
  3.2 1.5 collective-permute-start.16
  5.9 1.5 collective-permute-done.16.refs_2_
  7.4 2.4 %collective-permute-done.17.refs_3_ = bf16[32,1024]{1,0:T(8,128)(2,1)S(1)} collective-permute-done((bf16[32,1024]{1,0:T(8,128)(2,1)S(1)}, bf16[32,1024]{1,0:T(8,128)(2,1)S(1)}, u32[]{:S(2)}, u32[]{:S(2)}) %collective-permute-start.17) | collective-permute-done | bytes 65568 | tf_op jit(solution)/shard_map/ppermute | solution.py:289
  10.3 2.7 %collective-permute-start.28 = (bf16[32,1024]{1,0:T(8,128)(2,1)S(1)}, bf16[32,1024]{1,0:T(8,128)(2,1)S(1)}, u32[]{:S(2)}, u32[]{:S(2)}) collective-permute-start(bf16[32,1024]{1,0:T(8,128)(2,1)S(1)} %get-tuple-element.51), channel_id=1, source_target_pairs={{0,24},{8,16},{16,8},{24,0},{1,25},{9,17},{17,9},{25,1},{2,26},{10... | collective-permute-start | bytes 196616 | tf_op jit(solution)/shard_map/ppermute | solution.py:286
  13.0 2.2 %collective-permute-done.27 = bf16[32,1024]{1,0:T(8,128)(2,1)S(1)} collective-permute-done((bf16[32,1024]{1,0:T(8,128)(2,1)S(1)}, bf16[32,1024]{1,0:T(8,128)(2,1)S(1)}, u32[]{:S(2)}, u32[]{:S(2)}) %collective-permute-start.27) | collective-permute-done | bytes 65568 | tf_op jit(solution)/shard_map/ppermute | solution.py:286
  15.2 2.0 %collective-permute-done.28 = bf16[32,1024]{1,0:T(8,128)(2,1)S(1)} collective-permute-done((bf16[32,1024]{1,0:T(8,128)(2,1)S(1)}, bf16[32,1024]{1,0:T(8,128)(2,1)S(1)}, u32[]{:S(2)}, u32[]{:S(2)}) %collective-permute-start.28) | collective-permute-done | bytes 65568 | tf_op jit(solution)/shard_map/ppermute | solution.py:286
  21.6 1.8 %collective-permute-done.31.refs_3_ = bf16[64,1024]{1,0:T(8,128)(2,1)S(1)} collective-permute-done((bf16[64,1024]{1,0:T(8,128)(2,1)S(1)}, bf16[64,1024]{1,0:T(8,128)(2,1)S(1)}, u32[]{:S(2)}, u32[]{:S(2)}) %collective-permute-start.31) | collective-permute-done | bytes 131104 | tf_op jit(solution)/shard_map/ppermute | solution.py:289
  25.8 4.5 %masked_weight.1.refs_3_.refs_1_.refs_8_ = bf16[2048,2048]{1,0:T(8,128)(2,1)S(1)} custom-call(bf16[2048,2048]{1,0:T(8,128)(2,1)} %w_ref.1, s32[16,16]{1,0:T(8,128)S(1)} %copy-done.1), custom_call_target="tpu_custom_call" | custom-call | bytes 8389632 | tf_op jit(solution)/shard_map/masked_weight/pallas_call | solution.py:26
  30.4 2.4 %back_product.3 = (bf16[256,2048]{1,0:T(8,128)(2,1)S(1)}, bf16[128,2048]{1,0:T(8,128)(2,1)S(1)}, bf16[128,2048]{1,0:T(8,128)(2,1)S(1)}) custom-call(bf16[64,1024]{1,0:T(8,128)(2,1)S(1)} %constant_dynamic-update-slice_fusion.2.refs_0_, bf16[64,1024]{1,0:T(8,128)(2,1)S(1)} %collective-permute-done.29.refs_1_, ...), custom_call_target="tpu_custom_call" | custom-call | flops 2147483648 | bytes 9437184 | tf_op jit(solution)/shard_map/back_product/pallas_call | solution.py:26
  34.6 1.4 collective-permute-start.20
  37.1 3.8 %collective-permute-done.21.refs_3_ = bf16[64,1024]{1,0:T(8,128)(2,1)S(1)} collective-permute-done((bf16[64,1024]{1,0:T(8,128)(2,1)S(1)}, bf16[64,1024]{1,0:T(8,128)(2,1)S(1)}, u32[]{:S(2)}, u32[]{:S(2)}) %collective-permute-start.21) | collective-permute-done | bytes 131104 | tf_op jit(solution)/shard_map/ppermute | solution.py:289
  40.9 1.5 collective-permute-done.20.refs_2_
  44.0 2.4 %back_product.2 = (bf16[256,2048]{1,0:T(8,128)(2,1)S(1)}, bf16[128,2048]{1,0:T(8,128)(2,1)S(1)}, bf16[128,2048]{1,0:T(8,128)(2,1)S(1)}) custom-call(bf16[64,1024]{1,0:T(8,128)(2,1)S(1)} %constant_dynamic-update-slice_fusion.refs_0_, bf16[64,1024]{1,0:T(8,128)(2,1)S(1)} %collective-permute-done.19.refs_1_, ...), custom_call_target="tpu_custom_call" | custom-call | flops 2147483648 | bytes 9437184 | tf_op jit(solution)/shard_map/back_product/pallas_call | solution.py:26
  48.2 13.0 %collective-permute-done.26 = bf16[128,2048]{1,0:T(8,128)(2,1)S(1)} collective-permute-done((bf16[128,2048]{1,0:T(8,128)(2,1)S(1)}, bf16[128,2048]{1,0:T(8,128)(2,1)S(1)}, u32[]{:S(2)}, u32[]{:S(2)}) %collective-permute-start.26) | collective-permute-done | bytes 524320 | tf_op jit(solution)/shard_map/ppermute | solution.py:286
  61.2 12.2 %collective-permute-done.37 = bf16[128,2048]{1,0:T(8,128)(2,1)S(1)} collective-permute-done((bf16[128,2048]{1,0:T(8,128)(2,1)S(1)}, bf16[128,2048]{1,0:T(8,128)(2,1)S(1)}, u32[]{:S(2)}, u32[]{:S(2)}) %collective-permute-start.37) | collective-permute-done | bytes 524320 | tf_op jit(solution)/shard_map/ppermute | solution.py:286
  73.4 1.8 %multiply_convert_fusion = (bf16[128,2048]{1,0:T(8,128)(2,1)}, bf16[128,2048]{1,0:T(8,128)(2,1)}, bf16[128,2048]{1,0:T(8,128)(2,1)S(1)}) fusion(bf16[128,2048]{1,0:T(8,128)(2,1)S(1)} %collective-permute-done.37, bf16[128,2048]{1,0:T(8,128)(2,1)S(1)} %collective-permute-done.26, bf16[128,2048]{1,0:T(8,128)(2,1)S(1)} %get-tuple-element.48, ...), kind=kLoop, calls=%fused_computation.13 | loop fusion | flops 5767168 | bytes 4194304 | tf_op jit(solution)/shard_map/convert_element_type | solution.py:326
  75.2 2.3 %collective-permute-start = (bf16[128,2048]{1,0:T(8,128)(2,1)S(1)}, bf16[128,2048]{1,0:T(8,128)(2,1)S(1)}, u32[]{:S(2)}, u32[]{:S(2)}) collective-permute-start(bf16[128,2048]{1,0:T(8,128)(2,1)S(1)} %get-tuple-element.58.refs_0_.refs_5_), channel_id=1, source_target_pairs={{0,8},{8,0},{16,24},{24,16},{1,9},{9,1},{17,25},{25,17},{2,10},{10... | collective-permute-start | bytes 1572872 | tf_op jit(solution)/shard_map/ppermute | solution.py:286
  77.5 18.0 %collective-permute-done.1.refs_2_.refs_3_ = bf16[128,2048]{1,0:T(8,128)(2,1)S(1)} collective-permute-done((bf16[128,2048]{1,0:T(8,128)(2,1)S(1)}, bf16[128,2048]{1,0:T(8,128)(2,1)S(1)}, u32[]{:S(2)}, u32[]{:S(2)}) %collective-permute-start.1) | collective-permute-done | bytes 524320 | tf_op jit(solution)/shard_map/ppermute | solution.py:286
  95.5 4.6 %collective-permute-done.refs_1_.refs_4_ = bf16[128,2048]{1,0:T(8,128)(2,1)S(1)} collective-permute-done((bf16[128,2048]{1,0:T(8,128)(2,1)S(1)}, bf16[128,2048]{1,0:T(8,128)(2,1)S(1)}, u32[]{:S(2)}, u32[]{:S(2)}) %collective-permute-start) | collective-permute-done | bytes 524320 | tf_op jit(solution)/shard_map/ppermute | solution.py:286
  100.1 1.8 %out_product.5 = bf16[384,1024]{1,0:T(8,128)(2,1)S(1)} custom-call(bf16[128,2048]{1,0:T(8,128)(2,1)S(1)} %get-tuple-element.58.refs_0_.refs_5_, bf16[128,2048]{1,0:T(8,128)(2,1)S(1)} %collective-permute-done.refs_1_.refs_4_, bf16[128,2048]{1,0:T(8,128)(2,1)S(1)} %collective-permute-done.1.refs_2_.refs_3_, ...), custom_call_target="tpu_custom_call" | custom-call | flops 1610612736 | bytes 9961472 | tf_op jit(solution)/shard_map/out_product/pallas_call | solution.py:26
  102.1 1.7 %collective-permute-start.6 = (bf16[128,2048]{1,0:T(8,128)(2,1)S(1)}, bf16[128,2048]{1,0:T(8,128)(2,1)S(1)}, u32[]{:S(2)}, u32[]{:S(2)}) collective-permute-start(bf16[128,2048]{1,0:T(8,128)(2,1)S(1)} %collective-permute-done.1.refs_2_.refs_3_), channel_id=1, source_target_pairs={{0,8},{8,0},{16,24},{24,16},{1,9},{9,1},{17,25},{25,17},{2,10},{10... | collective-permute-start | bytes 1572872 | tf_op jit(solution)/shard_map/ppermute | solution.py:286
  103.8 12.6 %collective-permute-done.6.refs_0_.refs_2_ = bf16[128,2048]{1,0:T(8,128)(2,1)S(1)} collective-permute-done((bf16[128,2048]{1,0:T(8,128)(2,1)S(1)}, bf16[128,2048]{1,0:T(8,128)(2,1)S(1)}, u32[]{:S(2)}, u32[]{:S(2)}) %collective-permute-start.6) | collective-permute-done | bytes 524320 | tf_op jit(solution)/shard_map/ppermute | solution.py:286
  116.4 1.5 out_product.7
  118.0 1.8 %out_product.4.x_ref = f32[384,1024]{1,0:T(8,128)S(1)} custom-call(bf16[128,2048]{1,0:T(8,128)(2,1)S(1)} %get-tuple-element.58.refs_0_.refs_5_, bf16[128,2048]{1,0:T(8,128)(2,1)S(1)} %collective-permute-done.refs_1_.refs_4_, bf16[128,2048]{1,0:T(8,128)(2,1)S(1)} %collective-permute-done.1.refs_2_.refs_3_, ...), custom_call_target="tpu_custom_call" | custom-call | flops 1610612736 | bytes 9961472 | tf_op jit(solution)/shard_map/out_product/pallas_call | solution.py:26
  121.8 1.8 %collective-permute-start.5 = (bf16[96,1024]{1,0:T(8,128)(2,1)S(1)}, bf16[96,1024]{1,0:T(8,128)(2,1)S(1)}, u32[]{:S(2)}, u32[]{:S(2)}) collective-permute-start(bf16[96,1024]{1,0:T(8,128)(2,1)S(1)} %get-tuple-element.33), channel_id=1, source_target_pairs={{0,6},{1,7},{2,4},{3,5},{4,2},{5,3},{6,0},{7,1},{8,14},{9,15},{10,... | collective-permute-start | bytes 589832 | tf_op jit(solution)/shard_map/ppermute | solution.py:289
  123.5 1.5 out_product.6.x_ref
  126.9 6.1 %collective-permute-done.8.refs_5_ = bf16[32,1024]{1,0:T(8,128)(2,1)S(1)} collective-permute-done((bf16[32,1024]{1,0:T(8,128)(2,1)S(1)}, bf16[32,1024]{1,0:T(8,128)(2,1)S(1)}, u32[]{:S(2)}, u32[]{:S(2)}) %collective-permute-start.8) | collective-permute-done | bytes 65568 | tf_op jit(solution)/shard_map/ppermute | solution.py:289
  134.2 4.0 %collective-permute-done.10.refs_7_ = bf16[32,1024]{1,0:T(8,128)(2,1)S(1)} collective-permute-done((bf16[32,1024]{1,0:T(8,128)(2,1)S(1)}, bf16[32,1024]{1,0:T(8,128)(2,1)S(1)}, u32[]{:S(2)}, u32[]{:S(2)}) %collective-permute-start.10) | collective-permute-done | bytes 65568 | tf_op jit(solution)/shard_map/ppermute | solution.py:289
  138.4 4.4 %collective-permute-start.11 = (bf16[32,1024]{1,0:T(8,128)(2,1)S(1)}, bf16[32,1024]{1,0:T(8,128)(2,1)S(1)}, u32[]{:S(2)}, u32[]{:S(2)}) collective-permute-start(bf16[32,1024]{1,0:T(8,128)(2,1)S(1)} %get-tuple-element.38), channel_id=1, source_target_pairs={{0,0},{1,1},{2,8},{3,9},{4,16},{5,17},{6,24},{7,25},{8,2},{9,3},{1... | collective-permute-start | bytes 196616 | tf_op jit(solution)/shard_map/ppermute | solution.py:340
  143.7 5.4 %collective-permute-start.14 = (bf16[32,1024]{1,0:T(8,128)(2,1)S(1)}, bf16[32,1024]{1,0:T(8,128)(2,1)S(1)}, u32[]{:S(2)}, u32[]{:S(2)}) collective-permute-start(bf16[32,1024]{1,0:T(8,128)(2,1)S(1)} %get-tuple-element.41), channel_id=1, source_target_pairs={{0,24},{1,25},{2,16},{3,17},{4,8},{5,9},{6,0},{7,1},{8,26},{9,27},... | collective-permute-start | bytes 196616 | tf_op jit(solution)/shard_map/ppermute | solution.py:340
  149.1 9.7 %down_gradient.1 = bf16[2048,2048]{1,0:T(8,128)(2,1)} custom-call(bf16[256,2048]{1,0:T(8,128)(2,1)S(1)} %get-tuple-element.54.refs_0_, bf16[256,2048]{1,0:T(8,128)(2,1)S(1)} %get-tuple-element.55.refs_1_, bf16[128,2048]{1,0:T(8,128)(2,1)S(1)} %collective-permute-done.6.refs_0_.refs_2_, bf16[128,2048]{1,0:T(8,128)(2,1)S(1)} %collective-permute-done.1.refs_2_.refs_3_, ...), custom_call_target="tpu_custom_call" | custom-call | flops 4294967296 | bytes 8388608 | tf_op jit(solution)/shard_map/down_gradient/pallas_call | solution.py:263
  (72 shorter events, 22.7 us)
Async XLA Ops:
  4.7 5.2 %collective-permute-start.17 = (bf16[32,1024]{1,0:T(8,128)(2,1)S(1)}, bf16[32,1024]{1,0:T(8,128)(2,1)S(1)}, u32[]{:S(2)}, u32[]{:S(2)}) collective-permute-start(bf16[32,1024]{1,0:T(8,128)(2,1)S(1)} %get-tuple-element.45), channel_id=1, source_target_pairs={{0,6},{1,7},{2,4},{3,5},{4,2},{5,3},{6,0},{7,1},{8,14},{9,15},{10,... | collective-permute-start | bytes 196616 | tf_op jit(solution)/shard_map/ppermute | solution.py:289
  9.9 5.3 %collective-permute-start.27 = (bf16[32,1024]{1,0:T(8,128)(2,1)S(1)}, bf16[32,1024]{1,0:T(8,128)(2,1)S(1)}, u32[]{:S(2)}, u32[]{:S(2)}) collective-permute-start(bf16[32,1024]{1,0:T(8,128)(2,1)S(1)} %get-tuple-element.50), channel_id=1, source_target_pairs={{0,16},{8,24},{16,0},{24,8},{1,17},{9,25},{17,1},{25,9},{2,18},{10... | collective-permute-start | bytes 196616 | tf_op jit(solution)/shard_map/ppermute | solution.py:286
  10.3 6.9 %collective-permute-start.28 = (bf16[32,1024]{1,0:T(8,128)(2,1)S(1)}, bf16[32,1024]{1,0:T(8,128)(2,1)S(1)}, u32[]{:S(2)}, u32[]{:S(2)}) collective-permute-start(bf16[32,1024]{1,0:T(8,128)(2,1)S(1)} %get-tuple-element.51), channel_id=1, source_target_pairs={{0,24},{8,16},{16,8},{24,0},{1,25},{9,17},{17,9},{25,1},{2,26},{10... | collective-permute-start | bytes 196616 | tf_op jit(solution)/shard_map/ppermute | solution.py:286
  17.3 6.1 %collective-permute-start.31 = (bf16[64,1024]{1,0:T(8,128)(2,1)S(1)}, bf16[64,1024]{1,0:T(8,128)(2,1)S(1)}, u32[]{:S(2)}, u32[]{:S(2)}) collective-permute-start(bf16[64,1024]{1,0:T(8,128)(2,1)S(1)} %constant_dynamic-update-slice_fusion.2.refs_0_), channel_id=1, source_target_pairs={{0,6},{1,7},{2,4},{3,5},{4,2},{5,3},{6,0},{7,1},{8,14},{9,15},{10,... | collective-permute-start | bytes 393224 | tf_op jit(solution)/shard_map/ppermute | solution.py:289
  18.2 6.4 %collective-permute-start.30 = (bf16[64,1024]{1,0:T(8,128)(2,1)S(1)}, bf16[64,1024]{1,0:T(8,128)(2,1)S(1)}, u32[]{:S(2)}, u32[]{:S(2)}) collective-permute-start(bf16[64,1024]{1,0:T(8,128)(2,1)S(1)} %constant_dynamic-update-slice_fusion.2.refs_0_), channel_id=1, source_target_pairs={{0,4},{1,5},{2,6},{3,7},{4,0},{5,1},{6,2},{7,3},{8,12},{9,13},{10,... | collective-permute-start | bytes 393224 | tf_op jit(solution)/shard_map/ppermute | solution.py:289
  20.7 9.5 %collective-permute-start.18 = (bf16[32,1024]{1,0:T(8,128)(2,1)S(1)}, bf16[32,1024]{1,0:T(8,128)(2,1)S(1)}, u32[]{:S(2)}, u32[]{:S(2)}) collective-permute-start(bf16[32,1024]{1,0:T(8,128)(2,1)S(1)} %get-tuple-element.46), channel_id=1, source_target_pairs={{0,8},{8,0},{16,24},{24,16},{1,9},{9,1},{17,25},{25,17},{2,10},{10... | collective-permute-start | bytes 196616 | tf_op jit(solution)/shard_map/ppermute | solution.py:286
  21.6 8.8 %collective-permute-start.32 = (bf16[64,1024]{1,0:T(8,128)(2,1)S(1)}, bf16[64,1024]{1,0:T(8,128)(2,1)S(1)}, u32[]{:S(2)}, u32[]{:S(2)}) collective-permute-start(bf16[64,1024]{1,0:T(8,128)(2,1)S(1)} %constant_dynamic-update-slice_fusion.2.refs_0_), channel_id=1, source_target_pairs={{0,1},{1,0},{2,3},{3,2},{4,5},{5,4},{6,7},{7,6},{8,9},{9,8},{10,11... | collective-permute-start | bytes 393224 | tf_op jit(solution)/shard_map/ppermute | solution.py:292
  23.3 7.0 %collective-permute-start.35 = (bf16[64,1024]{1,0:T(8,128)(2,1)S(1)}, bf16[64,1024]{1,0:T(8,128)(2,1)S(1)}, u32[]{:S(2)}, u32[]{:S(2)}) collective-permute-start(bf16[64,1024]{1,0:T(8,128)(2,1)S(1)} %collective-permute-done.31.refs_3_), channel_id=1, source_target_pairs={{0,1},{1,0},{2,3},{3,2},{4,5},{5,4},{6,7},{7,6},{8,9},{9,8},{10,11... | collective-permute-start | bytes 393224 | tf_op jit(solution)/shard_map/ppermute | solution.py:292
  24.6 5.8 %collective-permute-start.34 = (bf16[64,1024]{1,0:T(8,128)(2,1)S(1)}, bf16[64,1024]{1,0:T(8,128)(2,1)S(1)}, u32[]{:S(2)}, u32[]{:S(2)}) collective-permute-start(bf16[64,1024]{1,0:T(8,128)(2,1)S(1)} %collective-permute-done.30.refs_2_), channel_id=1, source_target_pairs={{0,1},{1,0},{2,3},{3,2},{4,5},{5,4},{6,7},{7,6},{8,9},{9,8},{10,11... | collective-permute-start | bytes 393224 | tf_op jit(solution)/shard_map/ppermute | solution.py:292
  24.6 5.8 %collective-permute-start.33 = (bf16[64,1024]{1,0:T(8,128)(2,1)S(1)}, bf16[64,1024]{1,0:T(8,128)(2,1)S(1)}, u32[]{:S(2)}, u32[]{:S(2)}) collective-permute-start(bf16[64,1024]{1,0:T(8,128)(2,1)S(1)} %collective-permute-done.29.refs_1_), channel_id=1, source_target_pairs={{0,1},{1,0},{2,3},{3,2},{4,5},{5,4},{6,7},{7,6},{8,9},{9,8},{10,11... | collective-permute-start | bytes 393224 | tf_op jit(solution)/shard_map/ppermute | solution.py:292
  32.8 14.9 %collective-permute-start.36 = (bf16[128,2048]{1,0:T(8,128)(2,1)S(1)}, bf16[128,2048]{1,0:T(8,128)(2,1)S(1)}, u32[]{:S(2)}, u32[]{:S(2)}) collective-permute-start(bf16[128,2048]{1,0:T(8,128)(2,1)S(1)} %get-tuple-element.53), channel_id=1, source_target_pairs={{0,8},{8,0},{16,24},{24,16},{1,9},{9,1},{17,25},{25,17},{2,10},{10... | collective-permute-start | bytes 1572872 | tf_op jit(solution)/shard_map/ppermute | solution.py:286
  33.6 7.3 %collective-permute-start.21 = (bf16[64,1024]{1,0:T(8,128)(2,1)S(1)}, bf16[64,1024]{1,0:T(8,128)(2,1)S(1)}, u32[]{:S(2)}, u32[]{:S(2)}) collective-permute-start(bf16[64,1024]{1,0:T(8,128)(2,1)S(1)} %constant_dynamic-update-slice_fusion.refs_0_), channel_id=1, source_target_pairs={{0,6},{1,7},{2,4},{3,5},{4,2},{5,3},{6,0},{7,1},{8,14},{9,15},{10,... | collective-permute-start | bytes 393224 | tf_op jit(solution)/shard_map/ppermute | solution.py:289
  34.6 7.8 %collective-permute-start.20 = (bf16[64,1024]{1,0:T(8,128)(2,1)S(1)}, bf16[64,1024]{1,0:T(8,128)(2,1)S(1)}, u32[]{:S(2)}, u32[]{:S(2)}) collective-permute-start(bf16[64,1024]{1,0:T(8,128)(2,1)S(1)} %constant_dynamic-update-slice_fusion.refs_0_), channel_id=1, source_target_pairs={{0,4},{1,5},{2,6},{3,7},{4,0},{5,1},{6,2},{7,3},{8,12},{9,13},{10,... | collective-permute-start | bytes 393224 | tf_op jit(solution)/shard_map/ppermute | solution.py:289
  36.0 6.4 %collective-permute-start.19 = (bf16[64,1024]{1,0:T(8,128)(2,1)S(1)}, bf16[64,1024]{1,0:T(8,128)(2,1)S(1)}, u32[]{:S(2)}, u32[]{:S(2)}) collective-permute-start(bf16[64,1024]{1,0:T(8,128)(2,1)S(1)} %constant_dynamic-update-slice_fusion.refs_0_), channel_id=1, source_target_pairs={{0,2},{1,3},{2,0},{3,1},{4,6},{5,7},{6,4},{7,5},{8,10},{9,11},{10,... | collective-permute-start | bytes 393224 | tf_op jit(solution)/shard_map/ppermute | solution.py:289
  37.1 5.8 %collective-permute-start.22 = (bf16[64,1024]{1,0:T(8,128)(2,1)S(1)}, bf16[64,1024]{1,0:T(8,128)(2,1)S(1)}, u32[]{:S(2)}, u32[]{:S(2)}) collective-permute-start(bf16[64,1024]{1,0:T(8,128)(2,1)S(1)} %constant_dynamic-update-slice_fusion.refs_0_), channel_id=1, source_target_pairs={{0,1},{1,0},{2,3},{3,2},{4,5},{5,4},{6,7},{7,6},{8,9},{9,8},{10,11... | collective-permute-start | bytes 393224 | tf_op jit(solution)/shard_map/ppermute | solution.py:292
  46.4 14.8 %collective-permute-start.26 = (bf16[128,2048]{1,0:T(8,128)(2,1)S(1)}, bf16[128,2048]{1,0:T(8,128)(2,1)S(1)}, u32[]{:S(2)}, u32[]{:S(2)}) collective-permute-start(bf16[128,2048]{1,0:T(8,128)(2,1)S(1)} %get-tuple-element.49), channel_id=1, source_target_pairs={{0,8},{8,0},{16,24},{24,16},{1,9},{9,1},{17,25},{25,17},{2,10},{10... | collective-permute-start | bytes 1572872 | tf_op jit(solution)/shard_map/ppermute | solution.py:286
  47.9 25.6 %collective-permute-start.37 = (bf16[128,2048]{1,0:T(8,128)(2,1)S(1)}, bf16[128,2048]{1,0:T(8,128)(2,1)S(1)}, u32[]{:S(2)}, u32[]{:S(2)}) collective-permute-start(bf16[128,2048]{1,0:T(8,128)(2,1)S(1)} %add_convert_fusion), channel_id=1, source_target_pairs={{0,24},{8,16},{16,8},{24,0},{1,25},{9,17},{17,9},{25,1},{2,26},{10... | collective-permute-start | bytes 1572872 | tf_op jit(solution)/shard_map/ppermute | solution.py:286
  75.2 20.3 %collective-permute-start.1 = (bf16[128,2048]{1,0:T(8,128)(2,1)S(1)}, bf16[128,2048]{1,0:T(8,128)(2,1)S(1)}, u32[]{:S(2)}, u32[]{:S(2)}) collective-permute-start(bf16[128,2048]{1,0:T(8,128)(2,1)S(1)} %get-tuple-element.58.refs_0_.refs_5_), channel_id=1, source_target_pairs={{0,24},{8,16},{16,8},{24,0},{1,25},{9,17},{17,9},{25,1},{2,26},{10... | collective-permute-start | bytes 1572872 | tf_op jit(solution)/shard_map/ppermute | solution.py:286
  75.2 24.9 %collective-permute-start = (bf16[128,2048]{1,0:T(8,128)(2,1)S(1)}, bf16[128,2048]{1,0:T(8,128)(2,1)S(1)}, u32[]{:S(2)}, u32[]{:S(2)}) collective-permute-start(bf16[128,2048]{1,0:T(8,128)(2,1)S(1)} %get-tuple-element.58.refs_0_.refs_5_), channel_id=1, source_target_pairs={{0,8},{8,0},{16,24},{24,16},{1,9},{9,1},{17,25},{25,17},{2,10},{10... | collective-permute-start | bytes 1572872 | tf_op jit(solution)/shard_map/ppermute | solution.py:286
  102.0 17.8 %collective-permute-start.2 = (bf16[384,1024]{1,0:T(8,128)(2,1)S(1)}, bf16[384,1024]{1,0:T(8,128)(2,1)S(1)}, u32[]{:S(2)}, u32[]{:S(2)}) collective-permute-start(bf16[384,1024]{1,0:T(8,128)(2,1)S(1)} %out_product.5), channel_id=1, source_target_pairs={{0,1},{1,0},{2,3},{3,2},{4,5},{5,4},{6,7},{7,6},{8,9},{9,8},{10,11... | collective-permute-start | bytes 2359304 | tf_op jit(solution)/shard_map/ppermute | solution.py:292
  102.1 14.3 %collective-permute-start.6 = (bf16[128,2048]{1,0:T(8,128)(2,1)S(1)}, bf16[128,2048]{1,0:T(8,128)(2,1)S(1)}, u32[]{:S(2)}, u32[]{:S(2)}) collective-permute-start(bf16[128,2048]{1,0:T(8,128)(2,1)S(1)} %collective-permute-done.1.refs_2_.refs_3_), channel_id=1, source_target_pairs={{0,8},{8,0},{16,24},{24,16},{1,9},{9,1},{17,25},{25,17},{2,10},{10... | collective-permute-start | bytes 1572872 | tf_op jit(solution)/shard_map/ppermute | solution.py:286
  117.9 7.1 %collective-permute-start.7 = (bf16[128,1024]{1,0:T(8,128)(2,1)S(1)}, bf16[128,1024]{1,0:T(8,128)(2,1)S(1)}, u32[]{:S(2)}, u32[]{:S(2)}) collective-permute-start(bf16[128,1024]{1,0:T(8,128)(2,1)S(1)} %out_product.7), channel_id=1, source_target_pairs={{0,1},{1,0},{2,3},{3,2},{4,5},{5,4},{6,7},{7,6},{8,9},{9,8},{10,11... | collective-permute-start | bytes 786440 | tf_op jit(solution)/shard_map/ppermute | solution.py:292
  120.0 18.2 %collective-permute-start.3 = (bf16[96,1024]{1,0:T(8,128)(2,1)S(1)}, bf16[96,1024]{1,0:T(8,128)(2,1)S(1)}, u32[]{:S(2)}, u32[]{:S(2)}) collective-permute-start(bf16[96,1024]{1,0:T(8,128)(2,1)S(1)} %get-tuple-element.31), channel_id=1, source_target_pairs={{0,2},{1,3},{2,0},{3,1},{4,6},{5,7},{6,4},{7,5},{8,10},{9,11},{10,... | collective-permute-start | bytes 589832 | tf_op jit(solution)/shard_map/ppermute | solution.py:289
  121.1 17.1 %collective-permute-start.4 = (bf16[96,1024]{1,0:T(8,128)(2,1)S(1)}, bf16[96,1024]{1,0:T(8,128)(2,1)S(1)}, u32[]{:S(2)}, u32[]{:S(2)}) collective-permute-start(bf16[96,1024]{1,0:T(8,128)(2,1)S(1)} %get-tuple-element.32), channel_id=1, source_target_pairs={{0,4},{1,5},{2,6},{3,7},{4,0},{5,1},{6,2},{7,3},{8,12},{9,13},{10,... | collective-permute-start | bytes 589832 | tf_op jit(solution)/shard_map/ppermute | solution.py:289
  121.8 16.4 %collective-permute-start.5 = (bf16[96,1024]{1,0:T(8,128)(2,1)S(1)}, bf16[96,1024]{1,0:T(8,128)(2,1)S(1)}, u32[]{:S(2)}, u32[]{:S(2)}) collective-permute-start(bf16[96,1024]{1,0:T(8,128)(2,1)S(1)} %get-tuple-element.33), channel_id=1, source_target_pairs={{0,6},{1,7},{2,4},{3,5},{4,2},{5,3},{6,0},{7,1},{8,14},{9,15},{10,... | collective-permute-start | bytes 589832 | tf_op jit(solution)/shard_map/ppermute | solution.py:289
  125.1 7.9 %collective-permute-start.8 = (bf16[32,1024]{1,0:T(8,128)(2,1)S(1)}, bf16[32,1024]{1,0:T(8,128)(2,1)S(1)}, u32[]{:S(2)}, u32[]{:S(2)}) collective-permute-start(bf16[32,1024]{1,0:T(8,128)(2,1)S(1)} %get-tuple-element.35), channel_id=1, source_target_pairs={{0,2},{1,3},{2,0},{3,1},{4,6},{5,7},{6,4},{7,5},{8,10},{9,11},{10,... | collective-permute-start | bytes 196616 | tf_op jit(solution)/shard_map/ppermute | solution.py:289
  126.2 8.0 %collective-permute-start.9 = (bf16[32,1024]{1,0:T(8,128)(2,1)S(1)}, bf16[32,1024]{1,0:T(8,128)(2,1)S(1)}, u32[]{:S(2)}, u32[]{:S(2)}) collective-permute-start(bf16[32,1024]{1,0:T(8,128)(2,1)S(1)} %get-tuple-element.36), channel_id=1, source_target_pairs={{0,4},{1,5},{2,6},{3,7},{4,0},{5,1},{6,2},{7,3},{8,12},{9,13},{10,... | collective-permute-start | bytes 196616 | tf_op jit(solution)/shard_map/ppermute | solution.py:289
  133.0 5.2 %collective-permute-start.10 = (bf16[32,1024]{1,0:T(8,128)(2,1)S(1)}, bf16[32,1024]{1,0:T(8,128)(2,1)S(1)}, u32[]{:S(2)}, u32[]{:S(2)}) collective-permute-start(bf16[32,1024]{1,0:T(8,128)(2,1)S(1)} %get-tuple-element.37), channel_id=1, source_target_pairs={{0,6},{1,7},{2,4},{3,5},{4,2},{5,3},{6,0},{7,1},{8,14},{9,15},{10,... | collective-permute-start | bytes 196616 | tf_op jit(solution)/shard_map/ppermute | solution.py:289
  138.4 20.4 %collective-permute-start.11 = (bf16[32,1024]{1,0:T(8,128)(2,1)S(1)}, bf16[32,1024]{1,0:T(8,128)(2,1)S(1)}, u32[]{:S(2)}, u32[]{:S(2)}) collective-permute-start(bf16[32,1024]{1,0:T(8,128)(2,1)S(1)} %get-tuple-element.38), channel_id=1, source_target_pairs={{0,0},{1,1},{2,8},{3,9},{4,16},{5,17},{6,24},{7,25},{8,2},{9,3},{1... | collective-permute-start | bytes 196616 | tf_op jit(solution)/shard_map/ppermute | solution.py:340
  142.8 15.9 %collective-permute-start.12 = (bf16[32,1024]{1,0:T(8,128)(2,1)S(1)}, bf16[32,1024]{1,0:T(8,128)(2,1)S(1)}, u32[]{:S(2)}, u32[]{:S(2)}) collective-permute-start(bf16[32,1024]{1,0:T(8,128)(2,1)S(1)} %get-tuple-element.39), channel_id=1, source_target_pairs={{0,8},{1,9},{2,0},{3,1},{4,24},{5,25},{6,16},{7,17},{8,10},{9,11},... | collective-permute-start | bytes 196616 | tf_op jit(solution)/shard_map/ppermute | solution.py:340
  143.7 15.0 %collective-permute-start.13 = (bf16[32,1024]{1,0:T(8,128)(2,1)S(1)}, bf16[32,1024]{1,0:T(8,128)(2,1)S(1)}, u32[]{:S(2)}, u32[]{:S(2)}) collective-permute-start(bf16[32,1024]{1,0:T(8,128)(2,1)S(1)} %get-tuple-element.40), channel_id=1, source_target_pairs={{0,16},{1,17},{2,24},{3,25},{4,0},{5,1},{6,8},{7,9},{8,18},{9,19},... | collective-permute-start | bytes 196616 | tf_op jit(solution)/shard_map/ppermute | solution.py:340
  143.7 15.0 %collective-permute-start.14 = (bf16[32,1024]{1,0:T(8,128)(2,1)S(1)}, bf16[32,1024]{1,0:T(8,128)(2,1)S(1)}, u32[]{:S(2)}, u32[]{:S(2)}) collective-permute-start(bf16[32,1024]{1,0:T(8,128)(2,1)S(1)} %get-tuple-element.41), channel_id=1, source_target_pairs={{0,24},{1,25},{2,16},{3,17},{4,8},{5,9},{6,0},{7,1},{8,26},{9,27},... | collective-permute-start | bytes 196616 | tf_op jit(solution)/shard_map/ppermute | solution.py:340
  (10 other events, 106.4 us)

commit v2 on v1

v2 whole, which is shorter than its diff:
```python
import jax
import jax.numpy as jnp
from jax import lax
from jax.experimental import pallas as pl
from jax.experimental.pallas import tpu as pltpu
from jax.sharding import PartitionSpec as P

F32 = jnp.float32
BF16 = jnp.bfloat16
VMEM = pl.BlockSpec(memory_space=pltpu.VMEM)
SMEM = pl.BlockSpec(memory_space=pltpu.SMEM)
PARAMS = pltpu.CompilerParams(vmem_limit_bytes=16 * 2**20)


ANY = pl.BlockSpec(memory_space=pl.ANY)


def in_vmem(array):
    return pltpu.with_memory_space_constraint(array, pltpu.VMEM)


def in_hbm(array):
    return pltpu.with_memory_space_constraint(array, pltpu.HBM)


def place():
    col = lax.axis_index("col")
    return lax.axis_index("row"), col // 2, col % 2


def call(kernel, name, outs, *args, specs=None, scratch=(), flops=0, moved=0, after=()):
    n, m = len(args), len(args) + len(after)

    def body(*refs):
        kernel(*refs[:n], *refs[m:])

    return pl.pallas_call(
        body,
        in_specs=(specs or [VMEM] * n) + [pl.BlockSpec(memory_space=pl.ANY)] * len(after),
        out_specs=[VMEM] * len(outs),
        out_shape=[pltpu.VMEM(shape, dtype) for shape, dtype in outs],
        scratch_shapes=list(scratch),
        compiler_params=PARAMS,
        cost_estimate=pl.CostEstimate(flops=flops, bytes_accessed=moved, transcendentals=0),
        name=name,
    )(*args, *after)


def masked_weight(weight, mask, after=()):
    rows, cols = weight.shape
    tile_r, tile_c = mask.shape
    size_r, size_c = rows // tile_r, cols // tile_c

    def kernel(w_ref, m_ref, o_ref, sem):
        def copy(i):
            part = pl.ds(i * size_r, size_r)
            return pltpu.make_async_copy(w_ref.at[part], o_ref.at[part], sem.at[i])

        for i in range(tile_r):
            copy(i).start()
        for i in range(tile_r):
            copy(i).wait()
            for j in range(tile_c):

                @pl.when(m_ref[i, j] == 0)
                def _():
                    o_ref[i * size_r : (i + 1) * size_r, j * size_c : (j + 1) * size_c] = (
                        jnp.zeros((size_r, size_c), BF16)
                    )

    return call(
        kernel,
        "masked_weight",
        [((rows, cols), BF16)],
        in_hbm(weight),
        mask,
        specs=[ANY, SMEM],
        scratch=[pltpu.SemaphoreType.DMA((tile_r,))],
        after=after,
    )[0]


def gated(gate, up, after=()):
    def kernel(g_hbm, u_hbm, o_ref, dg_ref, du_ref, g_ref, u_ref, sem):
        copies = [
            pltpu.make_async_copy(g_hbm, g_ref, sem.at[0]),
            pltpu.make_async_copy(u_hbm, u_ref, sem.at[1]),
        ]
        for copy in copies:
            copy.start()
        for copy in copies:
            copy.wait()
        g = g_ref[...].astype(F32)
        u = u_ref[...].astype(F32)
        s = 1.0 / (1.0 + jnp.exp(-g))
        o_ref[...] = (g * s * u).astype(BF16)
        dg_ref[...] = u * s * (1.0 + g * (1.0 - s))
        du_ref[...] = g * s

    return call(
        kernel,
        "gated",
        [(gate.shape, BF16), (gate.shape, F32), (gate.shape, F32)],
        in_hbm(gate),
        in_hbm(up),
        specs=[ANY] * 2,
        scratch=[pltpu.VMEM(gate.shape, BF16)] * 2 + [pltpu.SemaphoreType.DMA((2,))],
        after=after,
    )


def gradients(shares, dg, du, after=()):
    rows, cols = dg.shape
    n = len(shares)
    step = rows // 4

    def kernel(*refs):
        dg_ref, du_ref = refs[n : n + 2]
        out_g, out_u = refs[-2:]
        total = refs[0][...].astype(F32)
        for ref in refs[1:n]:
            total += ref[...].astype(F32)
        out_g[...] = (total * dg_ref[...]).astype(BF16)
        out_u[...] = (total * du_ref[...]).astype(BF16)

    block = pl.BlockSpec((step, cols), lambda i: (i, 0))
    return pl.pallas_call(
        kernel,
        grid=(rows // step,),
        in_specs=[block] * (n + 2) + [ANY] * len(after),
        out_specs=[block] * 2,
        out_shape=[jax.ShapeDtypeStruct((rows, cols), BF16)] * 2,
        compiler_params=PARAMS,
        name="gradients",
    )(*map(in_vmem, shares), in_vmem(dg), in_vmem(du), *after)


def stack(pieces, after=()):
    part, width = pieces[0].shape

    def kernel(*refs):
        for i in range(len(pieces)):
            refs[-1][i * part : (i + 1) * part, :] = refs[i][...]

    shape = (len(pieces) * part, width)
    return call(kernel, "stack", [(shape, BF16)], *map(in_vmem, pieces), after=after)[0]


def quarters(cot, chips):
    tok, width = cot.shape
    part = tok // chips

    def kernel(x_ref, *rest):
        outs, sem = rest[:chips], rest[chips]
        _, a, _ = place()
        copies = [
            pltpu.make_async_copy(
                x_ref.at[pl.ds(pl.multiple_of((a ^ u) * part, part), part)], outs[u], sem.at[u]
            )
            for u in range(chips)
        ]
        for copy in copies:
            copy.start()
        for copy in copies:
            copy.wait()

    return call(
        kernel,
        "quarters",
        [((part, width), BF16)] * chips,
        in_hbm(cot),
        specs=[ANY],
        scratch=[pltpu.SemaphoreType.DMA((chips,))],
    )


def choose(pieces, order, after=()):
    n = len(pieces)

    def kernel(*refs):
        r, a, _ = place()
        for i, t in enumerate(order):
            for u in range(n):

                @pl.when((r ^ a ^ t) == u)
                def _():
                    refs[n + i][...] = refs[u][...]

    shape = (pieces[0].shape, BF16)
    return call(kernel, "choose", [shape] * len(order), *map(in_vmem, pieces), after=after)


def back_product(own, other, weight, tok, after=()):
    chips = len(own)
    chunk, width = own[0].shape
    part = tok // chips
    blocks = chunk // part
    dr, ff = weight.shape
    step = 512

    def kernel(*refs):
        x_ref, w_ref, c_ref, out2, out3 = refs[chips:]
        _, a, h = place()
        for w in range(2):
            lanes = pl.ds(pl.multiple_of((h ^ w) * width, width), width)
            for u in range(chips):
                for t in range(blocks):
                    rows = pl.ds(pl.multiple_of(t * tok + (a ^ u) * part, part), part)
                    if w == 0:
                        c_ref[rows, lanes] = refs[u][t * part : (t + 1) * part, :]
                    else:
                        at = u * chunk + t * part
                        c_ref[rows, lanes] = x_ref[at : at + part, :]
        for j in range(0, ff, step):
            product = jnp.dot(
                c_ref[2 * tok : 4 * tok, :], w_ref[:, j : j + step], preferred_element_type=F32
            ).astype(BF16)
            out2[:, j : j + step] = product[:tok]
            out3[:, j : j + step] = product[tok:]

    return call(
        kernel,
        "back_product",
        [((blocks * tok, dr), BF16)] + [((tok, ff), BF16)] * 2,
        *map(in_vmem, own),
        in_vmem(other),
        in_vmem(weight),
        flops=4 * tok * dr * ff,
        after=after,
    )


def back_rest(cot, weight, tok, passed, after=()):
    dr, ff = weight.shape
    step = 512

    def kernel(c_ref, w_ref, p_ref, out0, out1, out_p):
        out_p[...] = p_ref[...]
        for j in range(0, ff, step):
            product = jnp.dot(
                c_ref[: 2 * tok, :], w_ref[:, j : j + step], preferred_element_type=F32
            ).astype(BF16)
            out0[:, j : j + step] = product[:tok]
            out1[:, j : j + step] = product[tok:]

    return call(
        kernel,
        "back_rest",
        [((tok, ff), BF16)] * 3,
        in_vmem(cot),
        in_vmem(weight),
        in_vmem(passed),
        flops=4 * tok * dr * ff,
        after=after,
    )


def out_product(hidden, pair, weight, after=()):
    tok, ff = pair[0].shape
    half = weight.shape[0] // 2
    n = len(hidden)
    step = 512

    def kernel(*refs):
        x_ref, y_ref, w_ref, *sent, own_ref, block_ref = refs[n:]
        _, _, h = place()
        block_ref[...] = x_ref[...] + y_ref[...]
        lhs = jnp.concatenate([ref[...] for ref in refs[:n]] + [block_ref[...]], axis=0)
        for j in range(0, half, step):
            for own, first in ((False, (1 - h) * half), (True, h * half)):
                at = pl.ds(pl.multiple_of(first + j, step), step)
                product = lax.dot_general(
                    lhs, w_ref[at, :], (((1,), (1,)), ((), ())), preferred_element_type=F32
                )
                if own:
                    own_ref[:, j : j + step] = product
                else:
                    sent[j // step][...] = product.astype(BF16)

    rows = (n + 1) * tok
    return call(
        kernel,
        "out_product",
        [((rows, step), BF16)] * (half // step) + [((rows, half), F32), ((tok, ff), BF16)],
        *map(in_vmem, hidden),
        *map(in_vmem, pair),
        in_vmem(weight),
        flops=4 * max(rows, 256) * half * ff,
        after=after,
    )


def add_and_pass(pairs, passed=(), after=()):
    flat = [x for pair in pairs for x in pair]

    def kernel(*refs):
        outs = refs[len(flat) + len(passed) :]
        for i in range(len(pairs)):
            outs[i][...] = (
                refs[2 * i][...].astype(F32) + refs[2 * i + 1][...].astype(F32)
            ).astype(BF16)
        for i in range(len(passed)):
            outs[len(pairs) + i][...] = refs[len(flat) + i][...]

    shapes = [(pair[0].shape, BF16) for pair in pairs] + [(x.shape, BF16) for x in passed]
    return call(
        kernel, "add_and_pass", shapes, *map(in_vmem, flat), *map(in_vmem, passed), after=after
    )


def pair_sum(own, received, tok, chips, after=()):
    rows, width = own.shape
    blocks, part = rows // tok, tok // chips

    step = received[0].shape[1]

    def kernel(x_ref, *refs):
        outs = refs[len(received) :]
        _, a, _ = place()
        for u in range(chips):
            for b in range(blocks):
                at = pl.ds(pl.multiple_of(b * tok + (a ^ u) * part, part), part)
                for i in range(len(received)):
                    lanes = slice(i * step, (i + 1) * step)
                    outs[u][b * part : (b + 1) * part, lanes] = (
                        x_ref[at, lanes] + refs[i][at, :].astype(F32)
                    ).astype(BF16)

    return call(
        kernel,
        "pair_sum",
        [((blocks * part, width), BF16)] * chips,
        in_vmem(own),
        *map(in_vmem, received),
        after=after,
    )


def early_sum(pieces, after=()):
    def kernel(*refs):
        total = refs[0][...].astype(F32)
        for ref in refs[1:-1]:
            total += ref[...].astype(F32)
        refs[-1][...] = total.astype(BF16)

    shape = (pieces[0].shape, BF16)
    return call(kernel, "early_sum", [shape], *map(in_vmem, pieces), after=after)[0]


def plane_sum(early, pieces, part, after=()):
    n = len(pieces)
    blocks = early.shape[0] // part + 1

    def kernel(*refs):
        outs = refs[n + 1 :]
        r, a, _ = place()
        total = refs[1][...].astype(F32)
        for ref in refs[2 : n + 1]:
            total += ref[...].astype(F32)
        sums = [refs[0][t * part : (t + 1) * part, :] for t in range(blocks - 1)]
        for t, value in enumerate(sums + [total.astype(BF16)]):
            for k in range(blocks):

                @pl.when((r ^ a ^ k) == t)
                def _():
                    outs[k][...] = value

    return call(
        kernel,
        "plane_sum",
        [(pieces[0].shape, BF16)] * blocks,
        in_vmem(early),
        *map(in_vmem, pieces),
        after=after,
    )


def assemble(pieces):
    n = len(pieces)
    part, width = pieces[0].shape

    def kernel(*refs):
        r, _, _ = place()
        for k in range(n):
            refs[n][pl.ds(pl.multiple_of((r ^ k) * part, part), part), :] = refs[k][...]

    return pl.pallas_call(
        kernel,
        in_specs=[VMEM] * n,
        out_specs=VMEM,
        out_shape=jax.ShapeDtypeStruct((n * part, width), BF16),
        compiler_params=PARAMS,
        name="assemble",
    )(*map(in_vmem, pieces))


def down_gradient(cots, hidden, mask, steps, begun=None, after=()):
    tok, ff = hidden[0].shape
    dr = cots[0].shape[1]
    tokens = tok * len(hidden)
    tile_r, tile_c = mask.shape
    size_r, size_c = dr // tile_r, ff // tile_c
    step = dr // 4
    first, count = steps
    nc, nh = len(cots), len(hidden)
    extra = ([] if begun is None else [begun]) + list(after)

    def kernel(*refs):
        m_ref = refs[nc + nh]
        o_ref, t_ref, h_all, c_all = refs[nc + nh + 1 + len(extra) :]
        t_ref[...] = jnp.zeros(t_ref.shape, BF16)
        i = pl.program_id(0)

        @pl.when(i == 0)
        def _():
            for t in range(nh):
                h_all[t * tok : (t + 1) * tok, :] = refs[nc + t][...]

        at = 0
        for c in range(nc):
            c_all[at : at + cots[c].shape[0], :] = refs[c][...]
            at += cots[c].shape[0]
        o_ref[...] = lax.dot_general(
            c_all[...], h_all[...], (((0,), (0,)), ((), ())), preferred_element_type=F32
        ).astype(BF16)
        for b in range(step // size_r):
            for j in range(tile_c):

                @pl.when(m_ref[(first + i) * (step // size_r) + b, j] == 0)
                def _():
                    o_ref[b * size_r : (b + 1) * size_r, j * size_c : (j + 1) * size_c] = (
                        jnp.zeros((size_r, size_c), BF16)
                    )

    return pl.pallas_call(
        kernel,
        grid=(count,),
        in_specs=[pl.BlockSpec((c.shape[0], step), lambda i: (0, first + i)) for c in cots]
        + [VMEM] * nh
        + [SMEM]
        + [pl.BlockSpec(memory_space=pl.ANY)] * len(extra),
        out_specs=[pl.BlockSpec((step, ff), lambda i: (first + i, 0)), VMEM],
        out_shape=[jax.ShapeDtypeStruct((dr, ff), BF16), pltpu.VMEM((16, 128), BF16)],
        scratch_shapes=[pltpu.VMEM((tokens, ff), BF16), pltpu.VMEM((tokens, step), BF16)],
        input_output_aliases={} if begun is None else {nc + nh + 1: 0},
        compiler_params=PARAMS,
        cost_estimate=pl.CostEstimate(
            flops=2 * tokens * step * count * ff,
            bytes_accessed=2 * step * count * ff,
            transcendentals=0,
        ),
        name="down_gradient",
    )(*map(in_vmem, cots), *map(in_vmem, hidden), mask, *extra)


def fast_body(gate_pre, up_pre, down_weight, block_mask, cotangent):
    rows, chips = 4, 4
    tok = gate_pre.shape[0]
    part = tok // chips

    def over_row(x, t, senders=range(4)):
        return lax.ppermute(x, "row", [(i, i ^ t) for i in senders])

    def over_chips(x, u):
        return lax.ppermute(x, "col", [(j, j ^ (2 * u)) for j in range(2 * chips)])

    def over_core(x):
        return lax.ppermute(x, "col", [(j, j ^ 1) for j in range(2 * chips)])

    ends, inner = (0, 3), (1, 2)

    mine = quarters(cotangent, chips)
    spread = [mine[0]] + [over_chips(mine[u], u) for u in range(1, chips)]
    first, dg, du = gated(gate_pre, up_pre, after=[mine[0]])
    ours = choose(spread, (3, 2, 1, 0), after=[first])
    cot = {t: over_row(x, t) for t, x in zip((3, 2, 1), ours)}
    cot[0] = ours[3]

    weight = masked_weight(down_weight, block_mask, after=[ours[0]])
    hidden = {0: add_and_pass([], [first], after=[weight, cot[1], cot[2], cot[3]])[0]}
    hidden[1] = over_row(hidden[0], 1)
    inner3 = over_row(hidden[0], 3, inner)
    inner2 = over_row(hidden[1], 3, inner)
    ends2 = over_row(inner3, 1, inner)


    mine = stack([cot[t] for t in range(rows)], after=[hidden[0]])
    same = [mine] + [over_chips(mine, u) for u in range(1, chips)]
    other = over_core(stack(same, after=[hidden[1], inner3]))
    cot, back2, back3 = back_product(same, other, weight, tok)

    first3 = over_row(back3, 1, ends)
    first2 = over_row(back2, 1, ends)
    back0, back1, inner2 = back_rest(cot, weight, tok, inner2, after=[back3])
    ends3 = over_row(inner2, 1, inner)

    def to_plane(own, received, after=()):
        pieces = pair_sum(own, received, tok, chips, after=after)
        return [pieces[0]] + [over_chips(pieces[u], u) for u in range(1, chips)]

    *sent, own, hidden[2] = out_product(
        [hidden[0], hidden[1]], [inner2, ends2], weight, after=[back1]
    )
    received = [over_core(x) for x in sent]
    (to_pass,) = add_and_pass([(back2, first3)], after=[own])
    second = over_row(to_pass, 3, inner)
    early = to_plane(own, received, after=[to_pass])

    *sent, own, hidden[3] = out_product([], [inner3, ends3], weight, after=[early[0]])
    received = [over_core(x) for x in sent]
    to_inner, to_near = add_and_pass([(back3, first2), (back1, second)], after=[own])
    across = over_row(to_inner, 3, inner)
    beside = over_row(to_near, 1)
    early = early_sum(early, after=[to_inner])
    late = to_plane(own, received, after=[early])

    tokens = [hidden[t] for t in range(rows)]
    d_down, done = down_gradient([cot], tokens, block_mask, (0, 2), after=[late[0]])
    ready = plane_sum(early, late, part, after=[done])
    d_down, done = down_gradient([cot], tokens, block_mask, (2, 2), d_down, after=[ready[0]])

    d_gate, d_up = gradients([back0, beside, across], dg, du, after=[done])

    width = 2 * chips
    placed = [
        lax.ppermute(
            ready[k],
            ("row", "col"),
            [
                (r * width + 2 * a + h, (a ^ k) * width + 2 * r + h)
                for r in range(rows)
                for a in range(chips)
                for h in range(2)
            ],
        )
        for k in range(rows)
    ]
    output = assemble(placed)

    return output, d_gate, d_up, d_down


def rounded_f32(values):
    return lax.optimization_barrier(values.astype(BF16)).astype(F32)


def general_body(gate_pre, up_pre, down_weight, block_mask, cotangent):
    tok_rows, ff_cols = gate_pre.shape
    d_rows = down_weight.shape[0]
    block_size = d_rows // block_mask.shape[0]
    gate_wide = gate_pre.astype(F32)
    up_wide = up_pre.astype(F32)
    activated = jax.nn.silu(gate_wide)
    hidden = (activated * up_wide).astype(BF16)
    expand = jnp.repeat(jnp.repeat(block_mask, block_size, axis=0), block_size, axis=1)
    masked = jnp.where(expand > 0, down_weight, jnp.zeros_like(down_weight))
    cot_row = lax.all_gather(cotangent, "col", axis=1, tiled=True)
    cot_all = lax.all_to_all(cot_row, "row", split_axis=1, concat_axis=0, tiled=True)
    panel = lax.all_gather(masked, "row", axis=0, tiled=True)
    y_partial = lax.dot_general(
        hidden, panel, (((1,), (1,)), ((), ())), preferred_element_type=F32
    )
    shards = panel.shape[0] // d_rows
    per_shard = jnp.einsum(
        "tnd,ndf->ntf",
        cot_row.reshape(tok_rows, shards, d_rows),
        panel.reshape(shards, d_rows, ff_cols),
        preferred_element_type=F32,
    )
    d_hidden = jnp.sum(rounded_f32(per_shard), axis=0)
    hidden_all = lax.all_gather(hidden, "row", axis=0, tiled=True)
    grad_full = lax.dot_general(
        cot_all, hidden_all, (((0,), (0,)), ((), ())), preferred_element_type=F32
    )
    output = lax.psum_scatter(y_partial.astype(BF16), "col", scatter_dimension=1, tiled=True)
    sigmoid_g = jax.nn.sigmoid(gate_wide)
    d_gate = (d_hidden * up_wide * sigmoid_g * (1.0 + gate_wide * (1.0 - sigmoid_g))).astype(BF16)
    d_up = (d_hidden * activated).astype(BF16)
    d_down = jnp.where(expand > 0, grad_full, jnp.zeros_like(grad_full)).astype(BF16)
    return output, d_gate, d_up, d_down


def solution(mesh):
    spec = P("row", "col")
    small = mesh.shape["row"] == 4 and mesh.shape["col"] == 8
    return jax.shard_map(
        fast_body if small else general_body,
        mesh=mesh,
        in_specs=(spec,) * 5,
        out_specs=(spec,) * 4,
        check_vma=False,
    )
```

time: 160 us -> 108 us (0.68)
  waiting for transfers between devices: 88.8 us -> 27.2 us
  Pallas kernels: 26.9 us -> 33.4 us
  starting transfers between devices: 39.4 us -> 45.1 us
  other arithmetic: 1.9 us -> 0 us
    ppermute x9 -> x13, waiting for transfers between devices: 64.7 us -> 15.3 us  [over_row(): return lax.ppermute(x, 'row', [(i, i ^ t) for i in senders])]
    ppermute x15 -> x12, waiting for transfers between devices: 23.1 us -> 11 us  [over_chips(): return lax.ppermute(x, 'col', [(j, j ^ 2 * u) for j in range(2 * chips)])]
    ppermute x9 -> x13, starting transfers between devices: 10.5 us -> 20.1 us  [over_row(): return lax.ppermute(x, 'row', [(i, i ^ t) for i in senders])]
    pallas_call x13 -> x20, Pallas kernels: 26.1 us -> 32.7 us  [the longest x17 19.3 us: call(): pl.pallas_call(body, in_specs=(specs or [VMEM] * n) + [pl.BlockSpec(memor...]
    ppermute x15 -> x12, starting transfers between devices: 17.1 us -> 13.7 us  [over_chips(): return lax.ppermute(x, 'col', [(j, j ^ 2 * u) for j in range(2 * chips)])]
    convert_element_type x2 -> x0, other arithmetic: 1.9 us -> none  [the longest x1 1.77 us: fast_body(): d_up = (d_hidden * activated).astype(BF16)]
  transfers between devices with their start and end apart: 38 -> 34, of which waited for: 18 -> 9; matrix products, arithmetic and copies ran while one was open for 0% -> 0% of each run, Pallas kernels for 14% -> 28%
where the time goes in v2:
time: 108 us; the launch traced here: 107 us
  starting transfers between devices  45.1 us (42%)
  Pallas kernels  33.4 us (31%)
  waiting for transfers between devices  27.2 us (25%)
    ppermute x13, starting transfers between devices, over_row(): return lax.ppermute(x, 'row', [(i, i ^ t) for i in senders])  20.1 us
    pallas_call x17, Pallas kernels, call(): pl.pallas_call(body, in_specs=(specs or [VMEM] * n) + [pl.BlockSpec(memor...  19.3 us
    ppermute x13, waiting for transfers between devices, over_row(): return lax.ppermute(x, 'row', [(i, i ^ t) for i in senders])  15.3 us
    ppermute x12, starting transfers between devices, over_chips(): return lax.ppermute(x, 'col', [(j, j ^ 2 * u) for j in range(2 * chips)])  13.7 us
    pallas_call x2, Pallas kernels, down_gradient(): pl.pallas_call(kernel, grid=(count,), in_specs=[pl.BlockSpec((c.shape[0],...  11.8 us
    ppermute x12, waiting for transfers between devices, over_chips(): return lax.ppermute(x, 'col', [(j, j ^ 2 * u) for j in range(2 * chips)])  11 us
    ppermute x4, starting transfers between devices, fast_body(): lax.ppermute(ready[k], ('row', 'col'), [(r * width + 2 * a + h, (a ^ k) *...  10.7 us
  transfers between devices with their start and end apart: 34, of which 9 were waited for; matrix products, arithmetic and copies ran while one was open for 0% of the time, Pallas kernels for 28%

profile of v2, /device:TPU:16, one launch (start us, length us, event | category | flops | bytes accessed | tf_op | source)
XLA Modules:
  0.0 107.5 jit_solution(4699729969037349121)
XLA Ops:
  1.6 1.6 %collective-permute-start = (bf16[32,1024]{1,0:T(8,128)(2,1)S(1)}, bf16[32,1024]{1,0:T(8,128)(2,1)S(1)}, u32[]{:S(2)}, u32[]{:S(2)}) collective-permute-start(bf16[32,1024]{1,0:T(8,128)(2,1)S(1)} %get-tuple-element.51), channel_id=1, source_target_pairs={{0,2},{1,3},{2,0},{3,1},{4,6},{5,7},{6,4},{7,5},{8,10},{9,11},{10,... | collective-permute-start | bytes 196616 | tf_op jit(solution)/shard_map/ppermute | solution.py:465
  3.2 1.5 %collective-permute-start.1 = (bf16[32,1024]{1,0:T(8,128)(2,1)S(1)}, bf16[32,1024]{1,0:T(8,128)(2,1)S(1)}, u32[]{:S(2)}, u32[]{:S(2)}) collective-permute-start(bf16[32,1024]{1,0:T(8,128)(2,1)S(1)} %get-tuple-element.52), channel_id=1, source_target_pairs={{0,4},{1,5},{2,6},{3,7},{4,0},{5,1},{6,2},{7,3},{8,12},{9,13},{10,... | collective-permute-start | bytes 196616 | tf_op jit(solution)/shard_map/ppermute | solution.py:465
  5.2 1.7 %gated.1 = (bf16[128,2048]{1,0:T(8,128)(2,1)S(1)}, f32[128,2048]{1,0:T(8,128)S(1)}, f32[128,2048]{1,0:T(8,128)S(1)}) custom-call(bf16[128,2048]{1,0:T(8,128)(2,1)} %refs_0_.4, bf16[128,2048]{1,0:T(8,128)(2,1)} %refs_1_.2, bf16[32,1024]{1,0:T(8,128)(2,1)S(1)} %get-tuple-element.49.refs_2_.refs_0_), custom_call_target="tpu_custom_call" | custom-call | tf_op jit(solution)/shard_map/gated/pallas_call | solution.py:37
  7.4 2.4 %collective-permute-done.2.refs_3_ = bf16[32,1024]{1,0:T(8,128)(2,1)S(1)} collective-permute-done((bf16[32,1024]{1,0:T(8,128)(2,1)S(1)}, bf16[32,1024]{1,0:T(8,128)(2,1)S(1)}, u32[]{:S(2)}, u32[]{:S(2)}) %collective-permute-start.2) | collective-permute-done | bytes 65568 | tf_op jit(solution)/shard_map/ppermute | solution.py:465
  9.9 1.6 %collective-permute-start.3 = (bf16[32,1024]{1,0:T(8,128)(2,1)S(1)}, bf16[32,1024]{1,0:T(8,128)(2,1)S(1)}, u32[]{:S(2)}, u32[]{:S(2)}) collective-permute-start(bf16[32,1024]{1,0:T(8,128)(2,1)S(1)} %get-tuple-element.55), channel_id=1, source_target_pairs={{0,8},{8,0},{16,24},{24,16},{1,9},{9,1},{17,25},{25,17},{2,10},{10... | collective-permute-start | bytes 196616 | tf_op jit(solution)/shard_map/ppermute | solution.py:462
  11.9 1.6 %collective-permute-start.5 = (bf16[32,1024]{1,0:T(8,128)(2,1)S(1)}, bf16[32,1024]{1,0:T(8,128)(2,1)S(1)}, u32[]{:S(2)}, u32[]{:S(2)}) collective-permute-start(bf16[32,1024]{1,0:T(8,128)(2,1)S(1)} %get-tuple-element.54.refs_2_), channel_id=1, source_target_pairs={{0,24},{8,16},{16,8},{24,0},{1,25},{9,17},{17,9},{25,1},{2,26},{10... | collective-permute-start | bytes 196616 | tf_op jit(solution)/shard_map/ppermute | solution.py:462
  14.2 4.3 %masked_weight.1.refs_1_.refs_5_.refs_4_.refs_2_ = bf16[2048,2048]{1,0:T(8,128)(2,1)S(1)} custom-call(bf16[2048,2048]{1,0:T(8,128)(2,1)} %refs_0_.5, s32[16,16]{1,0:T(8,128)S(1)} %copy-done, bf16[32,1024]{1,0:T(8,128)(2,1)S(1)} %get-tuple-element.54.refs_2_), custom_call_target="tpu_custom_call" | custom-call | tf_op jit(solution)/shard_map/masked_weight/pallas_call | solution.py:37
  18.6 2.3 %collective-permute-start.10 = (bf16[128,2048]{1,0:T(8,128)(2,1)S(1)}, bf16[128,2048]{1,0:T(8,128)(2,1)S(1)}, u32[]{:S(2)}, u32[]{:S(2)}) collective-permute-start(bf16[128,2048]{1,0:T(8,128)(2,1)S(1)} %add_and_pass.3.refs_4_.refs_0_.refs_1_), channel_id=1, source_target_pairs={{8,16},{16,8},{9,17},{17,9},{10,18},{18,10},{11,19},{19,11},{12,20... | collective-permute-start | bytes 1572872 | tf_op jit(solution)/shard_map/ppermute | solution.py:462
  22.3 1.5 %collective-permute-start.8 = (bf16[128,1024]{1,0:T(8,128)(2,1)S(1)}, bf16[128,1024]{1,0:T(8,128)(2,1)S(1)}, u32[]{:S(2)}, u32[]{:S(2)}) collective-permute-start(bf16[128,1024]{1,0:T(8,128)(2,1)S(1)} %stack.2.refs_0_), channel_id=1, source_target_pairs={{0,4},{1,5},{2,6},{3,7},{4,0},{5,1},{6,2},{7,3},{8,12},{9,13},{10,... | collective-permute-start | bytes 786440 | tf_op jit(solution)/shard_map/ppermute | solution.py:465
  23.9 1.5 %collective-permute-start.7 = (bf16[128,1024]{1,0:T(8,128)(2,1)S(1)}, bf16[128,1024]{1,0:T(8,128)(2,1)S(1)}, u32[]{:S(2)}, u32[]{:S(2)}) collective-permute-start(bf16[128,1024]{1,0:T(8,128)(2,1)S(1)} %stack.2.refs_0_), channel_id=1, source_target_pairs={{0,2},{1,3},{2,0},{3,1},{4,6},{5,7},{6,4},{7,5},{8,10},{9,11},{10,... | collective-permute-start | bytes 786440 | tf_op jit(solution)/shard_map/ppermute | solution.py:465
  25.4 5.6 %collective-permute-done.9.refs_3_ = bf16[128,1024]{1,0:T(8,128)(2,1)S(1)} collective-permute-done((bf16[128,1024]{1,0:T(8,128)(2,1)S(1)}, bf16[128,1024]{1,0:T(8,128)(2,1)S(1)}, u32[]{:S(2)}, u32[]{:S(2)}) %collective-permute-start.9) | collective-permute-done | bytes 262176 | tf_op jit(solution)/shard_map/ppermute | solution.py:465
  31.0 2.5 %collective-permute-done.8.refs_2_ = bf16[128,1024]{1,0:T(8,128)(2,1)S(1)} collective-permute-done((bf16[128,1024]{1,0:T(8,128)(2,1)S(1)}, bf16[128,1024]{1,0:T(8,128)(2,1)S(1)}, u32[]{:S(2)}, u32[]{:S(2)}) %collective-permute-start.8) | collective-permute-done | bytes 262176 | tf_op jit(solution)/shard_map/ppermute | solution.py:465
  33.6 2.6 %collective-permute-start.12 = (bf16[128,2048]{1,0:T(8,128)(2,1)S(1)}, bf16[128,2048]{1,0:T(8,128)(2,1)S(1)}, u32[]{:S(2)}, u32[]{:S(2)}) collective-permute-start(bf16[128,2048]{1,0:T(8,128)(2,1)S(1)} %collective-permute-done.6.refs_4_.refs_1_.refs_2_), channel_id=1, source_target_pairs={{8,16},{16,8},{9,17},{17,9},{10,18},{18,10},{11,19},{19,11},{12,20... | collective-permute-start | bytes 1572872 | tf_op jit(solution)/shard_map/ppermute | solution.py:462
  36.2 1.3 %collective-permute-start.13 = (bf16[128,2048]{1,0:T(8,128)(2,1)S(1)}, bf16[128,2048]{1,0:T(8,128)(2,1)S(1)}, u32[]{:S(2)}, u32[]{:S(2)}) collective-permute-start(bf16[128,2048]{1,0:T(8,128)(2,1)S(1)} %collective-permute-done.10.refs_5_.refs_0_), channel_id=1, source_target_pairs={{8,0},{16,24},{9,1},{17,25},{10,2},{18,26},{11,3},{19,27},{12,4},{... | collective-permute-start | bytes 1572872 | tf_op jit(solution)/shard_map/ppermute | solution.py:462
  37.6 2.5 %back_product.1 = (bf16[512,2048]{1,0:T(8,128)(2,1)S(1)}, bf16[128,2048]{1,0:T(8,128)(2,1)S(1)}, bf16[128,2048]{1,0:T(8,128)(2,1)S(1)}) custom-call(bf16[128,1024]{1,0:T(8,128)(2,1)S(1)} %stack.2.refs_0_, bf16[128,1024]{1,0:T(8,128)(2,1)S(1)} %collective-permute-done.7.refs_1_, bf16[128,1024]{1,0:T(8,128)(2,1)S(1)} %collective-permute-done.8.refs_2_, ...), custom_call_target="tpu_custom_call" | custom-call | flops 2147483648 | tf_op jit(solution)/shard_map/back_product/pallas_call | solution.py:37
  40.1 1.3 %collective-permute-start.16 = (bf16[128,2048]{1,0:T(8,128)(2,1)S(1)}, bf16[128,2048]{1,0:T(8,128)(2,1)S(1)}, u32[]{:S(2)}, u32[]{:S(2)}) collective-permute-start(bf16[128,2048]{1,0:T(8,128)(2,1)S(1)} %get-tuple-element.59.refs_3_.refs_0_), channel_id=1, source_target_pairs={{0,8},{24,16},{1,9},{25,17},{2,10},{26,18},{3,11},{27,19},{4,12},{... | collective-permute-start | bytes 1572872 | tf_op jit(solution)/shard_map/ppermute | solution.py:462
  41.4 8.4 %collective-permute-done.12.refs_2_ = bf16[128,2048]{1,0:T(8,128)(2,1)S(1)} collective-permute-done((bf16[128,2048]{1,0:T(8,128)(2,1)S(1)}, bf16[128,2048]{1,0:T(8,128)(2,1)S(1)}, u32[]{:S(2)}, u32[]{:S(2)}) %collective-permute-start.12) | collective-permute-done | bytes 524320 | tf_op jit(solution)/shard_map/ppermute | solution.py:462
  49.8 2.4 %back_rest.1 = (bf16[128,2048]{1,0:T(8,128)(2,1)S(1)}, bf16[128,2048]{1,0:T(8,128)(2,1)S(1)}, bf16[128,2048]{1,0:T(8,128)(2,1)S(1)}) custom-call(bf16[512,2048]{1,0:T(8,128)(2,1)S(1)} %get-tuple-element.58.refs_0_, bf16[2048,2048]{1,0:T(8,128)(2,1)S(1)} %masked_weight.1.refs_1_.refs_5_.refs_4_.refs_2_, ...), custom_call_target="tpu_custom_call" | custom-call | flops 2147483648 | tf_op jit(solution)/shard_map/back_rest/pallas_call | solution.py:37
  52.2 1.3 %collective-permute-start.22 = (bf16[128,2048]{1,0:T(8,128)(2,1)S(1)}, bf16[128,2048]{1,0:T(8,128)(2,1)S(1)}, u32[]{:S(2)}, u32[]{:S(2)}) collective-permute-start(bf16[128,2048]{1,0:T(8,128)(2,1)S(1)} %get-tuple-element.60.refs_2_), channel_id=1, source_target_pairs={{8,0},{16,24},{9,1},{17,25},{10,2},{18,26},{11,3},{19,27},{12,4},{... | collective-permute-start | bytes 1572872 | tf_op jit(solution)/shard_map/ppermute | solution.py:462
  53.6 3.5 %out_product.2 = (bf16[384,512]{1,0:T(8,128)(2,1)S(1)}, bf16[384,512]{1,0:T(8,128)(2,1)S(1)}, f32[384,1024]{1,0:T(8,128)S(1)}, bf16[128,2048]{1,0:T(8,128)(2,1)S(1)}) custom-call(bf16[128,2048]{1,0:T(8,128)(2,1)S(1)} %add_and_pass.3.refs_4_.refs_0_.refs_1_, bf16[128,2048]{1,0:T(8,128)(2,1)S(1)} %collective-permute-done.6.refs_4_.refs_1_.refs_2_, ...), custom_call_target="tpu_custom_call" | custom-call | flops 3221225472 | tf_op jit(solution)/shard_map/out_product/pallas_call | solution.py:37
  59.0 2.8 %collective-permute-start.21 = (bf16[128,2048]{1,0:T(8,128)(2,1)S(1)}, bf16[128,2048]{1,0:T(8,128)(2,1)S(1)}, u32[]{:S(2)}, u32[]{:S(2)}) collective-permute-start(bf16[128,2048]{1,0:T(8,128)(2,1)S(1)} %add_and_pass.4.refs_3_), channel_id=1, source_target_pairs={{8,16},{16,8},{9,17},{17,9},{10,18},{18,10},{11,19},{19,11},{12,20... | collective-permute-start | bytes 1572872 | tf_op jit(solution)/shard_map/ppermute | solution.py:462
  66.0 2.9 %out_product.3 = (bf16[128,512]{1,0:T(8,128)(2,1)S(1)}, bf16[128,512]{1,0:T(8,128)(2,1)S(1)}, f32[128,1024]{1,0:T(8,128)S(1)}, bf16[128,2048]{1,0:T(8,128)(2,1)S(1)}) custom-call(bf16[128,2048]{1,0:T(8,128)(2,1)S(1)} %collective-permute-done.10.refs_5_.refs_0_, bf16[128,2048]{1,0:T(8,128)(2,1)S(1)} %collective-permute-done.22.refs_1_, ...), custom_call_target="tpu_custom_call" | custom-call | flops 2147483648 | tf_op jit(solution)/shard_map/out_product/pallas_call | solution.py:37
  68.9 4.5 %collective-permute-done.20.refs_1_ = bf16[128,2048]{1,0:T(8,128)(2,1)S(1)} collective-permute-done((bf16[128,2048]{1,0:T(8,128)(2,1)S(1)}, bf16[128,2048]{1,0:T(8,128)(2,1)S(1)}, u32[]{:S(2)}, u32[]{:S(2)}) %collective-permute-start.20) | collective-permute-done | bytes 524320 | tf_op jit(solution)/shard_map/ppermute | solution.py:462
  73.4 1.4 %collective-permute-done.21.refs_3_ = bf16[128,2048]{1,0:T(8,128)(2,1)S(1)} collective-permute-done((bf16[128,2048]{1,0:T(8,128)(2,1)S(1)}, bf16[128,2048]{1,0:T(8,128)(2,1)S(1)}, u32[]{:S(2)}, u32[]{:S(2)}) %collective-permute-start.21) | collective-permute-done | bytes 524320 | tf_op jit(solution)/shard_map/ppermute | solution.py:462
  75.2 2.6 %collective-permute-start.33 = (bf16[128,2048]{1,0:T(8,128)(2,1)S(1)}, bf16[128,2048]{1,0:T(8,128)(2,1)S(1)}, u32[]{:S(2)}, u32[]{:S(2)}) collective-permute-start(bf16[128,2048]{1,0:T(8,128)(2,1)S(1)} %get-tuple-element.71.refs_4_), channel_id=1, source_target_pairs={{8,16},{16,8},{9,17},{17,9},{10,18},{18,10},{11,19},{19,11},{12,20... | collective-permute-start | bytes 1572872 | tf_op jit(solution)/shard_map/ppermute | solution.py:462
  79.9 1.7 %collective-permute-start.27 = (bf16[32,1024]{1,0:T(8,128)(2,1)S(1)}, bf16[32,1024]{1,0:T(8,128)(2,1)S(1)}, u32[]{:S(2)}, u32[]{:S(2)}) collective-permute-start(bf16[32,1024]{1,0:T(8,128)(2,1)S(1)} %get-tuple-element.77), channel_id=1, source_target_pairs={{0,6},{1,7},{2,4},{3,5},{4,2},{5,3},{6,0},{7,1},{8,14},{9,15},{10,... | collective-permute-start | bytes 196616 | tf_op jit(solution)/shard_map/ppermute | solution.py:465
  81.6 5.9 %down_gradient.2 = (bf16[2048,2048]{1,0:T(8,128)(2,1)}, bf16[16,128]{1,0:T(8,128)(2,1)S(1)}) custom-call(bf16[512,2048]{1,0:T(8,128)(2,1)S(1)} %get-tuple-element.58.refs_0_, bf16[128,2048]{1,0:T(8,128)(2,1)S(1)} %add_and_pass.3.refs_4_.refs_0_.refs_1_, bf16[128,2048]{1,0:T(8,128)(2,1)S(1)} %collective-permute-done.6.refs_4_.refs_1_.refs_2_, ...), custom_call_target="tpu_custom_call" | custom-call | flops 2147483648 | bytes 4194304 | tf_op jit(solution)/shard_map/down_gradient/pallas_call | solution.py:435
  87.6 1.6 %collective-permute-start.29 = (bf16[32,1024]{1,0:T(8,128)(2,1)S(1)}, bf16[32,1024]{1,0:T(8,128)(2,1)S(1)}, u32[]{:S(2)}, u32[]{:S(2)}) collective-permute-start(bf16[32,1024]{1,0:T(8,128)(2,1)S(1)} %get-tuple-element.82), channel_id=1, source_target_pairs={{0,8},{1,9},{2,0},{3,1},{4,24},{5,25},{6,16},{7,17},{8,10},{9,11},... | collective-permute-start | bytes 196616 | tf_op jit(solution)/shard_map/ppermute | solution.py:526
  89.2 4.6 %collective-permute-start.31 = (bf16[32,1024]{1,0:T(8,128)(2,1)S(1)}, bf16[32,1024]{1,0:T(8,128)(2,1)S(1)}, u32[]{:S(2)}, u32[]{:S(2)}) collective-permute-start(bf16[32,1024]{1,0:T(8,128)(2,1)S(1)} %get-tuple-element.84), channel_id=1, source_target_pairs={{0,24},{1,25},{2,16},{3,17},{4,8},{5,9},{6,0},{7,1},{8,26},{9,27},... | collective-permute-start | bytes 196616 | tf_op jit(solution)/shard_map/ppermute | solution.py:526
  94.7 4.4 %collective-permute-start.28 = (bf16[32,1024]{1,0:T(8,128)(2,1)S(1)}, bf16[32,1024]{1,0:T(8,128)(2,1)S(1)}, u32[]{:S(2)}, u32[]{:S(2)}) collective-permute-start(bf16[32,1024]{1,0:T(8,128)(2,1)S(1)} %get-tuple-element.81.refs_7_), channel_id=1, source_target_pairs={{0,0},{1,1},{2,8},{3,9},{4,16},{5,17},{6,24},{7,25},{8,2},{9,3},{1... | collective-permute-start | bytes 196616 | tf_op jit(solution)/shard_map/ppermute | solution.py:526
  99.2 5.9 %down_gradient.3 = (bf16[2048,2048]{1,0:T(8,128)(2,1)}, bf16[16,128]{1,0:T(8,128)(2,1)S(1)}) custom-call(bf16[512,2048]{1,0:T(8,128)(2,1)S(1)} %get-tuple-element.58.refs_0_, bf16[128,2048]{1,0:T(8,128)(2,1)S(1)} %add_and_pass.3.refs_4_.refs_0_.refs_1_, ...), custom_call_target="tpu_custom_call", output_to_operand_aliasing={{0}: (6, {})} | custom-call | flops 2147483648 | bytes 4194304 | tf_op jit(solution)/shard_map/down_gradient/pallas_call | solution.py:435
  105.8 1.7 %gradients.1 = (bf16[128,2048]{1,0:T(8,128)(2,1)}, bf16[128,2048]{1,0:T(8,128)(2,1)}) custom-call(bf16[128,2048]{1,0:T(8,128)(2,1)S(1)} %get-tuple-element.85.refs_0_, bf16[128,2048]{1,0:T(8,128)(2,1)S(1)} %collective-permute-done.32.refs_1_, bf16[128,2048]{1,0:T(8,128)(2,1)S(1)} %collective-permute-done.33.refs_2_, ...), custom_call_target="tpu_custom_call" | custom-call | tf_op jit(solution)/shard_map/gradients/pallas_call | solution.py:127
  (61 shorter events, 14.9 us)
Async XLA Ops:
  1.6 5.3 %collective-permute-start = (bf16[32,1024]{1,0:T(8,128)(2,1)S(1)}, bf16[32,1024]{1,0:T(8,128)(2,1)S(1)}, u32[]{:S(2)}, u32[]{:S(2)}) collective-permute-start(bf16[32,1024]{1,0:T(8,128)(2,1)S(1)} %get-tuple-element.51), channel_id=1, source_target_pairs={{0,2},{1,3},{2,0},{3,1},{4,6},{5,7},{6,4},{7,5},{8,10},{9,11},{10,... | collective-permute-start | bytes 196616 | tf_op jit(solution)/shard_map/ppermute | solution.py:465
  3.2 4.3 %collective-permute-start.1 = (bf16[32,1024]{1,0:T(8,128)(2,1)S(1)}, bf16[32,1024]{1,0:T(8,128)(2,1)S(1)}, u32[]{:S(2)}, u32[]{:S(2)}) collective-permute-start(bf16[32,1024]{1,0:T(8,128)(2,1)S(1)} %get-tuple-element.52), channel_id=1, source_target_pairs={{0,4},{1,5},{2,6},{3,7},{4,0},{5,1},{6,2},{7,3},{8,12},{9,13},{10,... | collective-permute-start | bytes 196616 | tf_op jit(solution)/shard_map/ppermute | solution.py:465
  4.7 5.2 %collective-permute-start.2 = (bf16[32,1024]{1,0:T(8,128)(2,1)S(1)}, bf16[32,1024]{1,0:T(8,128)(2,1)S(1)}, u32[]{:S(2)}, u32[]{:S(2)}) collective-permute-start(bf16[32,1024]{1,0:T(8,128)(2,1)S(1)} %get-tuple-element.53), channel_id=1, source_target_pairs={{0,6},{1,7},{2,4},{3,5},{4,2},{5,3},{6,0},{7,1},{8,14},{9,15},{10,... | collective-permute-start | bytes 196616 | tf_op jit(solution)/shard_map/ppermute | solution.py:465
  9.9 8.6 %collective-permute-start.3 = (bf16[32,1024]{1,0:T(8,128)(2,1)S(1)}, bf16[32,1024]{1,0:T(8,128)(2,1)S(1)}, u32[]{:S(2)}, u32[]{:S(2)}) collective-permute-start(bf16[32,1024]{1,0:T(8,128)(2,1)S(1)} %get-tuple-element.55), channel_id=1, source_target_pairs={{0,8},{8,0},{16,24},{24,16},{1,9},{9,1},{17,25},{25,17},{2,10},{10... | collective-permute-start | bytes 196616 | tf_op jit(solution)/shard_map/ppermute | solution.py:462
  11.6 6.9 %collective-permute-start.4 = (bf16[32,1024]{1,0:T(8,128)(2,1)S(1)}, bf16[32,1024]{1,0:T(8,128)(2,1)S(1)}, u32[]{:S(2)}, u32[]{:S(2)}) collective-permute-start(bf16[32,1024]{1,0:T(8,128)(2,1)S(1)} %get-tuple-element.56), channel_id=1, source_target_pairs={{0,16},{8,24},{16,0},{24,8},{1,17},{9,25},{17,1},{25,9},{2,18},{10... | collective-permute-start | bytes 196616 | tf_op jit(solution)/shard_map/ppermute | solution.py:462
  11.9 6.6 %collective-permute-start.5 = (bf16[32,1024]{1,0:T(8,128)(2,1)S(1)}, bf16[32,1024]{1,0:T(8,128)(2,1)S(1)}, u32[]{:S(2)}, u32[]{:S(2)}) collective-permute-start(bf16[32,1024]{1,0:T(8,128)(2,1)S(1)} %get-tuple-element.54.refs_2_), channel_id=1, source_target_pairs={{0,24},{8,16},{16,8},{24,0},{1,25},{9,17},{17,9},{25,1},{2,26},{10... | collective-permute-start | bytes 196616 | tf_op jit(solution)/shard_map/ppermute | solution.py:462
  18.6 14.9 %collective-permute-start.10 = (bf16[128,2048]{1,0:T(8,128)(2,1)S(1)}, bf16[128,2048]{1,0:T(8,128)(2,1)S(1)}, u32[]{:S(2)}, u32[]{:S(2)}) collective-permute-start(bf16[128,2048]{1,0:T(8,128)(2,1)S(1)} %add_and_pass.3.refs_4_.refs_0_.refs_1_), channel_id=1, source_target_pairs={{8,16},{16,8},{9,17},{17,9},{10,18},{18,10},{11,19},{19,11},{12,20... | collective-permute-start | bytes 1572872 | tf_op jit(solution)/shard_map/ppermute | solution.py:462
  20.9 12.6 %collective-permute-start.6 = (bf16[128,2048]{1,0:T(8,128)(2,1)S(1)}, bf16[128,2048]{1,0:T(8,128)(2,1)S(1)}, u32[]{:S(2)}, u32[]{:S(2)}) collective-permute-start(bf16[128,2048]{1,0:T(8,128)(2,1)S(1)} %add_and_pass.3.refs_4_.refs_0_.refs_1_), channel_id=1, source_target_pairs={{0,8},{8,0},{16,24},{24,16},{1,9},{9,1},{17,25},{25,17},{2,10},{10... | collective-permute-start | bytes 1572872 | tf_op jit(solution)/shard_map/ppermute | solution.py:462
  21.8 9.2 %collective-permute-start.9 = (bf16[128,1024]{1,0:T(8,128)(2,1)S(1)}, bf16[128,1024]{1,0:T(8,128)(2,1)S(1)}, u32[]{:S(2)}, u32[]{:S(2)}) collective-permute-start(bf16[128,1024]{1,0:T(8,128)(2,1)S(1)} %stack.2.refs_0_), channel_id=1, source_target_pairs={{0,6},{1,7},{2,4},{3,5},{4,2},{5,3},{6,0},{7,1},{8,14},{9,15},{10,... | collective-permute-start | bytes 786440 | tf_op jit(solution)/shard_map/ppermute | solution.py:465
  22.3 11.1 %collective-permute-start.8 = (bf16[128,1024]{1,0:T(8,128)(2,1)S(1)}, bf16[128,1024]{1,0:T(8,128)(2,1)S(1)}, u32[]{:S(2)}, u32[]{:S(2)}) collective-permute-start(bf16[128,1024]{1,0:T(8,128)(2,1)S(1)} %stack.2.refs_0_), channel_id=1, source_target_pairs={{0,4},{1,5},{2,6},{3,7},{4,0},{5,1},{6,2},{7,3},{8,12},{9,13},{10,... | collective-permute-start | bytes 786440 | tf_op jit(solution)/shard_map/ppermute | solution.py:465
  23.9 9.6 %collective-permute-start.7 = (bf16[128,1024]{1,0:T(8,128)(2,1)S(1)}, bf16[128,1024]{1,0:T(8,128)(2,1)S(1)}, u32[]{:S(2)}, u32[]{:S(2)}) collective-permute-start(bf16[128,1024]{1,0:T(8,128)(2,1)S(1)} %stack.2.refs_0_), channel_id=1, source_target_pairs={{0,2},{1,3},{2,0},{3,1},{4,6},{5,7},{6,4},{7,5},{8,10},{9,11},{10,... | collective-permute-start | bytes 786440 | tf_op jit(solution)/shard_map/ppermute | solution.py:465
  33.6 16.2 %collective-permute-start.12 = (bf16[128,2048]{1,0:T(8,128)(2,1)S(1)}, bf16[128,2048]{1,0:T(8,128)(2,1)S(1)}, u32[]{:S(2)}, u32[]{:S(2)}) collective-permute-start(bf16[128,2048]{1,0:T(8,128)(2,1)S(1)} %collective-permute-done.6.refs_4_.refs_1_.refs_2_), channel_id=1, source_target_pairs={{8,16},{16,8},{9,17},{17,9},{10,18},{18,10},{11,19},{19,11},{12,20... | collective-permute-start | bytes 1572872 | tf_op jit(solution)/shard_map/ppermute | solution.py:462
  36.2 17.3 %collective-permute-start.13 = (bf16[128,2048]{1,0:T(8,128)(2,1)S(1)}, bf16[128,2048]{1,0:T(8,128)(2,1)S(1)}, u32[]{:S(2)}, u32[]{:S(2)}) collective-permute-start(bf16[128,2048]{1,0:T(8,128)(2,1)S(1)} %collective-permute-done.10.refs_5_.refs_0_), channel_id=1, source_target_pairs={{8,0},{16,24},{9,1},{17,25},{10,2},{18,26},{11,3},{19,27},{12,4},{... | collective-permute-start | bytes 1572872 | tf_op jit(solution)/shard_map/ppermute | solution.py:462
  40.1 18.8 %collective-permute-start.16 = (bf16[128,2048]{1,0:T(8,128)(2,1)S(1)}, bf16[128,2048]{1,0:T(8,128)(2,1)S(1)}, u32[]{:S(2)}, u32[]{:S(2)}) collective-permute-start(bf16[128,2048]{1,0:T(8,128)(2,1)S(1)} %get-tuple-element.59.refs_3_.refs_0_), channel_id=1, source_target_pairs={{0,8},{24,16},{1,9},{25,17},{2,10},{26,18},{3,11},{27,19},{4,12},{... | collective-permute-start | bytes 1572872 | tf_op jit(solution)/shard_map/ppermute | solution.py:462
  52.2 12.6 %collective-permute-start.22 = (bf16[128,2048]{1,0:T(8,128)(2,1)S(1)}, bf16[128,2048]{1,0:T(8,128)(2,1)S(1)}, u32[]{:S(2)}, u32[]{:S(2)}) collective-permute-start(bf16[128,2048]{1,0:T(8,128)(2,1)S(1)} %get-tuple-element.60.refs_2_), channel_id=1, source_target_pairs={{8,0},{16,24},{9,1},{17,25},{10,2},{18,26},{11,3},{19,27},{12,4},{... | collective-permute-start | bytes 1572872 | tf_op jit(solution)/shard_map/ppermute | solution.py:462
  57.0 4.8 %collective-permute-start.14 = (bf16[384,512]{1,0:T(8,128)(2,1)S(1)}, bf16[384,512]{1,0:T(8,128)(2,1)S(1)}, u32[]{:S(2)}, u32[]{:S(2)}) collective-permute-start(bf16[384,512]{1,0:T(8,128)(2,1)S(1)} %get-tuple-element.63), channel_id=1, source_target_pairs={{0,1},{1,0},{2,3},{3,2},{4,5},{5,4},{6,7},{7,6},{8,9},{9,8},{10,11... | collective-permute-start | bytes 1179656 | tf_op jit(solution)/shard_map/ppermute | solution.py:468
  57.1 4.8 %collective-permute-start.15 = (bf16[384,512]{1,0:T(8,128)(2,1)S(1)}, bf16[384,512]{1,0:T(8,128)(2,1)S(1)}, u32[]{:S(2)}, u32[]{:S(2)}) collective-permute-start(bf16[384,512]{1,0:T(8,128)(2,1)S(1)} %get-tuple-element.64), channel_id=1, source_target_pairs={{0,1},{1,0},{2,3},{3,2},{4,5},{5,4},{6,7},{7,6},{8,9},{9,8},{10,11... | collective-permute-start | bytes 1179656 | tf_op jit(solution)/shard_map/ppermute | solution.py:468
  57.6 15.8 %collective-permute-start.20 = (bf16[128,2048]{1,0:T(8,128)(2,1)S(1)}, bf16[128,2048]{1,0:T(8,128)(2,1)S(1)}, u32[]{:S(2)}, u32[]{:S(2)}) collective-permute-start(bf16[128,2048]{1,0:T(8,128)(2,1)S(1)} %get-tuple-element.65.refs_0_), channel_id=1, source_target_pairs={{0,8},{24,16},{1,9},{25,17},{2,10},{26,18},{3,11},{27,19},{4,12},{... | collective-permute-start | bytes 1572872 | tf_op jit(solution)/shard_map/ppermute | solution.py:462
  59.0 15.8 %collective-permute-start.21 = (bf16[128,2048]{1,0:T(8,128)(2,1)S(1)}, bf16[128,2048]{1,0:T(8,128)(2,1)S(1)}, u32[]{:S(2)}, u32[]{:S(2)}) collective-permute-start(bf16[128,2048]{1,0:T(8,128)(2,1)S(1)} %add_and_pass.4.refs_3_), channel_id=1, source_target_pairs={{8,16},{16,8},{9,17},{17,9},{10,18},{18,10},{11,19},{19,11},{12,20... | collective-permute-start | bytes 1572872 | tf_op jit(solution)/shard_map/ppermute | solution.py:462
  62.0 13.0 %collective-permute-start.17 = (bf16[96,1024]{1,0:T(8,128)(2,1)S(1)}, bf16[96,1024]{1,0:T(8,128)(2,1)S(1)}, u32[]{:S(2)}, u32[]{:S(2)}) collective-permute-start(bf16[96,1024]{1,0:T(8,128)(2,1)S(1)} %get-tuple-element.67), channel_id=1, source_target_pairs={{0,2},{1,3},{2,0},{3,1},{4,6},{5,7},{6,4},{7,5},{8,10},{9,11},{10,... | collective-permute-start | bytes 589832 | tf_op jit(solution)/shard_map/ppermute | solution.py:465
  63.2 12.0 %collective-permute-start.18 = (bf16[96,1024]{1,0:T(8,128)(2,1)S(1)}, bf16[96,1024]{1,0:T(8,128)(2,1)S(1)}, u32[]{:S(2)}, u32[]{:S(2)}) collective-permute-start(bf16[96,1024]{1,0:T(8,128)(2,1)S(1)} %get-tuple-element.68), channel_id=1, source_target_pairs={{0,4},{1,5},{2,6},{3,7},{4,0},{5,1},{6,2},{7,3},{8,12},{9,13},{10,... | collective-permute-start | bytes 589832 | tf_op jit(solution)/shard_map/ppermute | solution.py:465
  64.8 13.0 %collective-permute-start.19 = (bf16[96,1024]{1,0:T(8,128)(2,1)S(1)}, bf16[96,1024]{1,0:T(8,128)(2,1)S(1)}, u32[]{:S(2)}, u32[]{:S(2)}) collective-permute-start(bf16[96,1024]{1,0:T(8,128)(2,1)S(1)} %get-tuple-element.69), channel_id=1, source_target_pairs={{0,6},{1,7},{2,4},{3,5},{4,2},{5,3},{6,0},{7,1},{8,14},{9,15},{10,... | collective-permute-start | bytes 589832 | tf_op jit(solution)/shard_map/ppermute | solution.py:465
  73.4 4.6 %collective-permute-start.23 = (bf16[128,512]{1,0:T(8,128)(2,1)S(1)}, bf16[128,512]{1,0:T(8,128)(2,1)S(1)}, u32[]{:S(2)}, u32[]{:S(2)}) collective-permute-start(bf16[128,512]{1,0:T(8,128)(2,1)S(1)} %get-tuple-element.72), channel_id=1, source_target_pairs={{0,1},{1,0},{2,3},{3,2},{4,5},{5,4},{6,7},{7,6},{8,9},{9,8},{10,11... | collective-permute-start | bytes 393224 | tf_op jit(solution)/shard_map/ppermute | solution.py:468
  75.1 30.7 %collective-permute-start.32 = (bf16[128,2048]{1,0:T(8,128)(2,1)S(1)}, bf16[128,2048]{1,0:T(8,128)(2,1)S(1)}, u32[]{:S(2)}, u32[]{:S(2)}) collective-permute-start(bf16[128,2048]{1,0:T(8,128)(2,1)S(1)} %get-tuple-element.86), channel_id=1, source_target_pairs={{0,8},{8,0},{16,24},{24,16},{1,9},{9,1},{17,25},{25,17},{2,10},{10... | collective-permute-start | bytes 1572872 | tf_op jit(solution)/shard_map/ppermute | solution.py:462
  75.2 30.6 %collective-permute-start.33 = (bf16[128,2048]{1,0:T(8,128)(2,1)S(1)}, bf16[128,2048]{1,0:T(8,128)(2,1)S(1)}, u32[]{:S(2)}, u32[]{:S(2)}) collective-permute-start(bf16[128,2048]{1,0:T(8,128)(2,1)S(1)} %get-tuple-element.71.refs_4_), channel_id=1, source_target_pairs={{8,16},{16,8},{9,17},{17,9},{10,18},{18,10},{11,19},{19,11},{12,20... | collective-permute-start | bytes 1572872 | tf_op jit(solution)/shard_map/ppermute | solution.py:462
  78.0 9.4 %collective-permute-start.25 = (bf16[32,1024]{1,0:T(8,128)(2,1)S(1)}, bf16[32,1024]{1,0:T(8,128)(2,1)S(1)}, u32[]{:S(2)}, u32[]{:S(2)}) collective-permute-start(bf16[32,1024]{1,0:T(8,128)(2,1)S(1)} %get-tuple-element.75), channel_id=1, source_target_pairs={{0,2},{1,3},{2,0},{3,1},{4,6},{5,7},{6,4},{7,5},{8,10},{9,11},{10,... | collective-permute-start | bytes 196616 | tf_op jit(solution)/shard_map/ppermute | solution.py:465
  79.2 8.3 %collective-permute-start.26 = (bf16[32,1024]{1,0:T(8,128)(2,1)S(1)}, bf16[32,1024]{1,0:T(8,128)(2,1)S(1)}, u32[]{:S(2)}, u32[]{:S(2)}) collective-permute-start(bf16[32,1024]{1,0:T(8,128)(2,1)S(1)} %get-tuple-element.76), channel_id=1, source_target_pairs={{0,4},{1,5},{2,6},{3,7},{4,0},{5,1},{6,2},{7,3},{8,12},{9,13},{10,... | collective-permute-start | bytes 196616 | tf_op jit(solution)/shard_map/ppermute | solution.py:465
  79.9 7.6 %collective-permute-start.27 = (bf16[32,1024]{1,0:T(8,128)(2,1)S(1)}, bf16[32,1024]{1,0:T(8,128)(2,1)S(1)}, u32[]{:S(2)}, u32[]{:S(2)}) collective-permute-start(bf16[32,1024]{1,0:T(8,128)(2,1)S(1)} %get-tuple-element.77), channel_id=1, source_target_pairs={{0,6},{1,7},{2,4},{3,5},{4,2},{5,3},{6,0},{7,1},{8,14},{9,15},{10,... | collective-permute-start | bytes 196616 | tf_op jit(solution)/shard_map/ppermute | solution.py:465
  87.6 7.1 %collective-permute-start.29 = (bf16[32,1024]{1,0:T(8,128)(2,1)S(1)}, bf16[32,1024]{1,0:T(8,128)(2,1)S(1)}, u32[]{:S(2)}, u32[]{:S(2)}) collective-permute-start(bf16[32,1024]{1,0:T(8,128)(2,1)S(1)} %get-tuple-element.82), channel_id=1, source_target_pairs={{0,8},{1,9},{2,0},{3,1},{4,24},{5,25},{6,16},{7,17},{8,10},{9,11},... | collective-permute-start | bytes 196616 | tf_op jit(solution)/shard_map/ppermute | solution.py:526
  89.2 15.8 %collective-permute-start.30 = (bf16[32,1024]{1,0:T(8,128)(2,1)S(1)}, bf16[32,1024]{1,0:T(8,128)(2,1)S(1)}, u32[]{:S(2)}, u32[]{:S(2)}) collective-permute-start(bf16[32,1024]{1,0:T(8,128)(2,1)S(1)} %get-tuple-element.83), channel_id=1, source_target_pairs={{0,16},{1,17},{2,24},{3,25},{4,0},{5,1},{6,8},{7,9},{8,18},{9,19},... | collective-permute-start | bytes 196616 | tf_op jit(solution)/shard_map/ppermute | solution.py:526
  89.2 15.8 %collective-permute-start.31 = (bf16[32,1024]{1,0:T(8,128)(2,1)S(1)}, bf16[32,1024]{1,0:T(8,128)(2,1)S(1)}, u32[]{:S(2)}, u32[]{:S(2)}) collective-permute-start(bf16[32,1024]{1,0:T(8,128)(2,1)S(1)} %get-tuple-element.84), channel_id=1, source_target_pairs={{0,24},{1,25},{2,16},{3,17},{4,8},{5,9},{6,0},{7,1},{8,26},{9,27},... | collective-permute-start | bytes 196616 | tf_op jit(solution)/shard_map/ppermute | solution.py:526
  94.7 10.4 %collective-permute-start.28 = (bf16[32,1024]{1,0:T(8,128)(2,1)S(1)}, bf16[32,1024]{1,0:T(8,128)(2,1)S(1)}, u32[]{:S(2)}, u32[]{:S(2)}) collective-permute-start(bf16[32,1024]{1,0:T(8,128)(2,1)S(1)} %get-tuple-element.81.refs_7_), channel_id=1, source_target_pairs={{0,0},{1,1},{2,8},{3,9},{4,16},{5,17},{6,24},{7,25},{8,2},{9,3},{1... | collective-permute-start | bytes 196616 | tf_op jit(solution)/shard_map/ppermute | solution.py:526
  (4 other events, 30.4 us)

commit v3 on v2

v3 whole, which is shorter than its diff:
```python
import jax
import jax.numpy as jnp
from jax import lax
from jax.experimental import pallas as pl
from jax.experimental.pallas import tpu as pltpu
from jax.sharding import PartitionSpec as P

F32 = jnp.float32
BF16 = jnp.bfloat16
VMEM = pl.BlockSpec(memory_space=pltpu.VMEM)
SMEM = pl.BlockSpec(memory_space=pltpu.SMEM)
PARAMS = pltpu.CompilerParams(vmem_limit_bytes=16 * 2**20)


ANY = pl.BlockSpec(memory_space=pl.ANY)


def in_vmem(array):
    return pltpu.with_memory_space_constraint(array, pltpu.VMEM)


def in_hbm(array):
    return pltpu.with_memory_space_constraint(array, pltpu.HBM)


def place():
    col = lax.axis_index("col")
    return lax.axis_index("row"), col // 2, col % 2


def call(kernel, name, outs, *args, specs=None, scratch=(), flops=0, moved=0, after=()):
    n, m = len(args), len(args) + len(after)

    def body(*refs):
        kernel(*refs[:n], *refs[m:])

    return pl.pallas_call(
        body,
        in_specs=(specs or [VMEM] * n) + [pl.BlockSpec(memory_space=pl.ANY)] * len(after),
        out_specs=[VMEM] * len(outs),
        out_shape=[pltpu.VMEM(shape, dtype) for shape, dtype in outs],
        scratch_shapes=list(scratch),
        compiler_params=PARAMS,
        cost_estimate=pl.CostEstimate(flops=flops, bytes_accessed=moved, transcendentals=0),
        name=name,
    )(*args, *after)


def masked_weight(weight, mask_rows, half, begun=None, after=()):
    rows, cols = weight.shape
    tile_r = mask_rows.shape[0]
    size = rows // tile_r
    mine = range(half * tile_r // 2, (half + 1) * tile_r // 2)
    extra = [] if begun is None else [in_vmem(begun)]

    def kernel(w_ref, m_ref, *refs):
        o_ref, sem = refs[-2:]

        def copy(i):
            at = pl.ds(i * size, size)
            return pltpu.make_async_copy(w_ref.at[at], o_ref.at[at], sem.at[i - mine[0]])

        for i in mine:
            copy(i).start()
        for i in mine:
            copy(i).wait()
            at = slice(i * size, (i + 1) * size)
            o_ref[at, :] = jnp.where(m_ref[i : i + 1, :] > 0, o_ref[at, :], jnp.zeros((), BF16))

    return pl.pallas_call(
        kernel,
        in_specs=[ANY, VMEM] + [VMEM] * len(extra) + [ANY] * len(after),
        out_specs=VMEM,
        out_shape=pltpu.VMEM((rows, cols), BF16),
        input_output_aliases={} if begun is None else {2: 0},
        scratch_shapes=[pltpu.SemaphoreType.DMA((len(mine),))],
        compiler_params=PARAMS,
        cost_estimate=pl.CostEstimate(flops=0, bytes_accessed=0, transcendentals=0),
        name="masked_weight",
    )(in_hbm(weight), in_vmem(mask_rows), *extra, *after)


def gated(gate, up, mask, width, after=()):
    tile_r, tile_c = mask.shape
    size = width // tile_c

    def kernel(g_hbm, u_hbm, m_hbm, o_ref, dg_ref, du_ref, rows_ref, g_ref, u_ref, m_ref, sem):
        copies = [
            pltpu.make_async_copy(m_hbm, m_ref, sem.at[2]),
            pltpu.make_async_copy(g_hbm, g_ref, sem.at[0]),
            pltpu.make_async_copy(u_hbm, u_ref, sem.at[1]),
        ]
        for copy in copies:
            copy.start()
        copies[0].wait()
        for i in range(tile_r):
            for j in range(tile_c):
                rows_ref[i : i + 1, j * size : (j + 1) * size] = jnp.full(
                    (1, size), m_ref[i, j], jnp.int32
                )
        for copy in copies[1:]:
            copy.wait()
        g = g_ref[...].astype(F32)
        u = u_ref[...].astype(F32)
        s = 1.0 / (1.0 + jnp.exp(-g))
        o_ref[...] = (g * s * u).astype(BF16)
        dg_ref[...] = u * s * (1.0 + g * (1.0 - s))
        du_ref[...] = g * s

    return call(
        kernel,
        "gated",
        [
            (gate.shape, BF16),
            (gate.shape, F32),
            (gate.shape, F32),
            ((tile_r, width), jnp.int32),
        ],
        in_hbm(gate),
        in_hbm(up),
        in_hbm(mask),
        specs=[ANY] * 3,
        scratch=[pltpu.VMEM(gate.shape, BF16)] * 2
        + [pltpu.SMEM(mask.shape, jnp.int32), pltpu.SemaphoreType.DMA((3,))],
        after=after,
    )


def gradients(shares, dg, du, after=()):
    rows, cols = dg.shape
    n = len(shares)
    step = rows // 4

    def kernel(*refs):
        dg_ref, du_ref = refs[n : n + 2]
        out_g, out_u, token = refs[-3:]
        token[...] = jnp.zeros(token.shape, BF16)
        total = refs[0][...].astype(F32)
        for ref in refs[1:n]:
            total += ref[...].astype(F32)
        out_g[...] = (total * dg_ref[...]).astype(BF16)
        out_u[...] = (total * du_ref[...]).astype(BF16)

    block = pl.BlockSpec((step, cols), lambda i: (i, 0))
    return pl.pallas_call(
        kernel,
        grid=(rows // step,),
        in_specs=[block] * (n + 2) + [ANY] * len(after),
        out_specs=[block] * 2 + [VMEM],
        out_shape=[jax.ShapeDtypeStruct((rows, cols), BF16)] * 2
        + [pltpu.VMEM((16, 128), BF16)],
        compiler_params=PARAMS,
        name="gradients",
    )(*map(in_vmem, shares), in_vmem(dg), in_vmem(du), *after)


def stack(pieces, after=()):
    part, width = pieces[0].shape

    def kernel(*refs):
        for i in range(len(pieces)):
            refs[-1][i * part : (i + 1) * part, :] = refs[i][...]

    shape = (len(pieces) * part, width)
    return call(kernel, "stack", [(shape, BF16)], *map(in_vmem, pieces), after=after)[0]


def quarters(cot, chips):
    tok, width = cot.shape
    part = tok // chips

    def kernel(x_ref, *rest):
        outs, sem = rest[:chips], rest[chips]
        _, a, _ = place()
        copies = [
            pltpu.make_async_copy(
                x_ref.at[pl.ds(pl.multiple_of((a ^ u) * part, part), part)], outs[u], sem.at[u]
            )
            for u in range(chips)
        ]
        for copy in copies:
            copy.start()
        for copy in copies:
            copy.wait()

    return call(
        kernel,
        "quarters",
        [((part, width), BF16)] * chips,
        in_hbm(cot),
        specs=[ANY],
        scratch=[pltpu.SemaphoreType.DMA((chips,))],
    )


def choose(pieces, order, after=()):
    n = len(pieces)

    def kernel(*refs):
        r, a, _ = place()
        for i, t in enumerate(order):
            for u in range(n):

                @pl.when((r ^ a ^ t) == u)
                def _():
                    refs[n + i][...] = refs[u][...]

    shape = (pieces[0].shape, BF16)
    return call(kernel, "choose", [shape] * len(order), *map(in_vmem, pieces), after=after)


def back_product(own, other, weight, tok, after=()):
    chips = len(own)
    chunk, width = own[0].shape
    part = tok // chips
    blocks = chunk // part
    dr, ff = weight.shape
    step = 512

    def kernel(*refs):
        w_ref, c_ref, out2, out3 = refs[chips + 2 : chips + 6]
        _, a, h = place()
        for w in range(2):
            lanes = pl.ds(pl.multiple_of((h ^ w) * width, width), width)
            for u in range(chips):
                for t in range(blocks):
                    rows = pl.ds(pl.multiple_of(t * tok + (a ^ u) * part, part), part)
                    if w == 0:
                        c_ref[rows, lanes] = refs[u][t * part : (t + 1) * part, :]
                    else:
                        pair, at = ((0, 0), (1, 0), (1, 1), (0, 1))[u]
                        at = at * chunk + t * part
                        c_ref[rows, lanes] = refs[chips + pair][at : at + part, :]
        for j in range(0, ff, step):
            product = jnp.dot(
                c_ref[2 * tok : 4 * tok, :], w_ref[:, j : j + step], preferred_element_type=F32
            ).astype(BF16)
            out2[:, j : j + step] = product[:tok]
            out3[:, j : j + step] = product[tok:]

    return call(
        kernel,
        "back_product",
        [((blocks * tok, dr), BF16)] + [((tok, ff), BF16)] * 2,
        *map(in_vmem, own),
        *map(in_vmem, other),
        in_vmem(weight),
        after=after,
    )


def back_rest(cot, weight, tok, after=()):
    dr, ff = weight.shape
    step = 512

    def kernel(c_ref, w_ref, out0, out1):
        for j in range(0, ff, step):
            product = jnp.dot(
                c_ref[: 2 * tok, :], w_ref[:, j : j + step], preferred_element_type=F32
            ).astype(BF16)
            out0[:, j : j + step] = product[:tok]
            out1[:, j : j + step] = product[tok:]

    return call(
        kernel,
        "back_rest",
        [((tok, ff), BF16)] * 2,
        in_vmem(cot),
        in_vmem(weight),
        after=after,
    )


def out_product(hidden, pairs, weight, pieces, after=()):
    tok, ff = (*hidden, *map(lambda pair: pair[0], pairs))[0].shape
    half = weight.shape[0] // 2
    n = len(hidden)
    flat = [x for pair in pairs for x in pair]
    rows = (n + len(pairs)) * tok
    size = half // pieces
    step = min(size, 512)

    def kernel(*refs):
        w_ref = refs[n + len(flat)]
        outs = refs[n + len(flat) + 1 :]
        sent, own_ref, blocks = outs[:pieces], outs[pieces], outs[pieces + 1 :]
        _, _, h = place()
        for i in range(len(pairs)):
            blocks[i][...] = refs[n + 2 * i][...] + refs[n + 2 * i + 1][...]
        lhs = jnp.concatenate([ref[...] for ref in (*refs[:n], *blocks)], axis=0)
        for own, first in ((False, (1 - h) * half), (True, h * half)):
            for j in range(0, half, step):
                at = pl.ds(pl.multiple_of(first + j, step), step)
                product = lax.dot_general(
                    lhs, w_ref[at, :], (((1,), (1,)), ((), ())), preferred_element_type=F32
                )
                if own:
                    own_ref[:, j : j + step] = product
                else:
                    sent[j // size][:, j % size : j % size + step] = product.astype(BF16)

    return call(
        kernel,
        "out_product",
        [((rows, size), BF16)] * pieces
        + [((rows, half), F32)]
        + [((tok, ff), BF16)] * len(pairs),
        *map(in_vmem, hidden),
        *map(in_vmem, flat),
        in_vmem(weight),
        after=after,
    )


def add_and_pass(pairs, passed=(), after=()):
    flat = [x for pair in pairs for x in pair]

    def kernel(*refs):
        outs = refs[len(flat) + len(passed) :]
        for i in range(len(pairs)):
            outs[i][...] = (
                refs[2 * i][...].astype(F32) + refs[2 * i + 1][...].astype(F32)
            ).astype(BF16)
        for i in range(len(passed)):
            outs[len(pairs) + i][...] = refs[len(flat) + i][...]

    shapes = [(pair[0].shape, BF16) for pair in pairs] + [(x.shape, BF16) for x in passed]
    return call(
        kernel, "add_and_pass", shapes, *map(in_vmem, flat), *map(in_vmem, passed), after=after
    )


def pair_sum(owns, received, tok, chips, after=()):
    width = owns[0].shape[1]
    blocks = sum(own.shape[0] for own in owns) // tok
    part = tok // chips
    flat = [x for chunk in received for x in chunk]

    def kernel(*refs):
        outs = refs[len(owns) + len(flat) :]
        _, a, _ = place()
        to, at_piece = 0, len(owns)
        for i, chunk in enumerate(received):
            step = chunk[0].shape[1]
            for b in range(owns[i].shape[0] // tok):
                for u in range(chips):
                    at = pl.ds(pl.multiple_of(b * tok + (a ^ u) * part, part), part)
                    for j in range(len(chunk)):
                        lanes = slice(j * step, (j + 1) * step)
                        outs[u][to * part : (to + 1) * part, lanes] = (
                            refs[i][at, lanes] + refs[at_piece + j][at, :].astype(F32)
                        ).astype(BF16)
                to += 1
            at_piece += len(chunk)

    return call(
        kernel,
        "pair_sum",
        [((blocks * part, width), BF16)] * chips,
        *map(in_vmem, owns),
        *map(in_vmem, flat),
        after=after,
    )


def plane_sum(pieces, part, after=()):
    n = len(pieces)
    blocks = pieces[0].shape[0] // part

    def kernel(*refs):
        outs = refs[n:]
        r, a, _ = place()
        for t in range(blocks):
            at = slice(t * part, (t + 1) * part)
            total = refs[0][at, :].astype(F32)
            for ref in refs[1:n]:
                total += ref[at, :].astype(F32)
            total = total.astype(BF16)
            for k in range(blocks):

                @pl.when((r ^ a ^ k) == t)
                def _():
                    outs[k][...] = total

    shape = ((part, pieces[0].shape[1]), BF16)
    return call(kernel, "plane_sum", [shape] * blocks, *map(in_vmem, pieces), after=after)


def assemble(pieces, after=()):
    n = len(pieces)
    part, width = pieces[0].shape

    def kernel(*refs):
        r, _, _ = place()
        for k in range(n):
            refs[-1][pl.ds(pl.multiple_of((r ^ k) * part, part), part), :] = refs[k][...]

    return pl.pallas_call(
        kernel,
        in_specs=[VMEM] * n + [ANY] * len(after),
        out_specs=VMEM,
        out_shape=jax.ShapeDtypeStruct((n * part, width), BF16),
        compiler_params=PARAMS,
        name="assemble",
    )(*map(in_vmem, pieces), *after)


def down_gradient(cot, hidden, mask_rows, half, begun=None, after=()):
    n = len(hidden)
    tok, ff = hidden[0].shape
    tokens, dr = cot.shape
    tile_r = mask_rows.shape[0]
    size = dr // tile_r
    step = dr // 4
    extra = ([] if begun is None else [begun]) + list(after)

    def kernel(c_ref, *refs):
        m_ref = refs[n]
        o_ref, t_ref, h_ref = refs[-3:]
        i = pl.program_id(0)
        t_ref[...] = jnp.zeros(t_ref.shape, BF16)

        @pl.when(i == 0)
        def _():
            for t in range(n):
                h_ref[t * tok : (t + 1) * tok, :] = refs[t][...]

        product = lax.dot_general(
            c_ref[...], h_ref[...], (((0,), (0,)), ((), ())), preferred_element_type=F32
        )
        for b in range(step // size):
            kept = m_ref[pl.ds((2 * half + i) * (step // size) + b, 1), :] > 0
            at = slice(b * size, (b + 1) * size)
            o_ref[at, :] = jnp.where(kept, product[at, :], 0.0).astype(BF16)

    return pl.pallas_call(
        kernel,
        grid=(2,),
        in_specs=[pl.BlockSpec((tokens, step), lambda i: (0, 2 * half + i))]
        + [VMEM] * (n + 1)
        + [ANY] * len(extra),
        out_specs=[pl.BlockSpec((step, ff), lambda i: (2 * half + i, 0)), VMEM],
        out_shape=[jax.ShapeDtypeStruct((dr, ff), BF16), pltpu.VMEM((16, 128), BF16)],
        scratch_shapes=[pltpu.VMEM((tokens, ff), BF16)],
        input_output_aliases={} if begun is None else {n + 2: 0},
        compiler_params=PARAMS,
        cost_estimate=pl.CostEstimate(
            flops=0, bytes_accessed=0, transcendentals=0
        ),
        name="down_gradient",
    )(in_vmem(cot), *map(in_vmem, hidden), in_vmem(mask_rows), *extra)


def fast_body(gate_pre, up_pre, down_weight, block_mask, cotangent):
    rows, chips = 4, 4
    tok = gate_pre.shape[0]
    part = tok // chips

    def over_row(x, t, senders=range(4)):
        return lax.ppermute(x, "row", [(i, i ^ t) for i in senders])

    def over_chips(x, u):
        return lax.ppermute(x, "col", [(j, j ^ (2 * u)) for j in range(2 * chips)])

    def over_core(x):
        return lax.ppermute(x, "col", [(j, j ^ 1) for j in range(2 * chips)])

    ends, inner = (0, 3), (1, 2)

    mine = quarters(cotangent, chips)
    spread = [mine[0]] + [over_chips(mine[u], u) for u in range(1, chips)]
    first, dg, du, mask_rows = gated(
        gate_pre, up_pre, block_mask, down_weight.shape[1], after=[mine[0]]
    )
    weight = masked_weight(down_weight, mask_rows, 0, after=[first])
    ours = choose(spread, (3, 2, 1, 0), after=[weight])
    cot = {t: over_row(x, t) for t, x in zip((3, 2, 1), ours)}
    cot[0] = ours[3]
    weight = masked_weight(down_weight, mask_rows, 1, weight, after=[ours[0]])

    mine = stack([cot[t] for t in range(rows)], after=[weight])
    same = [mine] + [over_chips(mine, u) for u in range(1, chips)]

    hidden = {0: add_and_pass([], [first], after=[mine])[0]}
    hidden[1] = over_row(hidden[0], 1)
    inner3 = over_row(hidden[0], 3, inner)
    inner2 = over_row(hidden[1], 3, inner)
    ends2 = over_row(inner3, 1, inner)

    other = [over_core(stack([same[0], same[3]])), over_core(stack([same[1], same[2]]))]
    cot, back2, back3 = back_product(same, other, weight, tok, after=[hidden[1], inner3])

    first3 = over_row(back3, 1, ends)
    first2 = over_row(back2, 1, ends)
    hidden[2], inner2 = add_and_pass([(inner2, ends2)], [inner2], after=[back3])
    ends3 = over_row(inner2, 1, inner)
    (to_pass,) = add_and_pass([(back2, first3)], after=[inner2])
    second = over_row(to_pass, 3, inner)
    back0, back1 = back_rest(cot, weight, tok, after=[to_pass])

    *sent, own01 = out_product([hidden[0], hidden[1]], [], weight, 2, after=[back1, to_pass])
    received = [[over_core(x) for x in sent]]
    *sent, own23, hidden[3] = out_product(
        [hidden[2]], [[inner3, ends3]], weight, 2, after=[own01]
    )
    received.append([over_core(x) for x in sent])
    to_inner, to_near = add_and_pass([(back3, first2), (back1, second)], after=[own23])
    across = over_row(to_inner, 3, inner)
    beside = over_row(to_near, 1)
    pieces = pair_sum([own01, own23], received, tok, chips)
    pieces = [pieces[0]] + [over_chips(pieces[u], u) for u in range(1, chips)]
    tokens = [hidden[t] for t in range(rows)]
    d_down, done = down_gradient(cot, tokens, mask_rows, 0, after=[pieces[0]])
    d_down, done = down_gradient(cot, tokens, mask_rows, 1, d_down, after=[done])
    ready = plane_sum(pieces, part, after=[done])
    d_gate, d_up, last = gradients([back0, beside, across], dg, du, after=[ready[0]])

    width = 2 * chips
    placed = [
        lax.ppermute(
            ready[k],
            ("row", "col"),
            [
                (r * width + 2 * a + h, (a ^ k) * width + 2 * r + h)
                for r in range(rows)
                for a in range(chips)
                for h in range(2)
            ],
        )
        for k in range(rows)
    ]
    output = assemble(placed, after=[last])

    return output, d_gate, d_up, d_down


def rounded_f32(values):
    return lax.optimization_barrier(values.astype(BF16)).astype(F32)


def general_body(gate_pre, up_pre, down_weight, block_mask, cotangent):
    tok_rows, ff_cols = gate_pre.shape
    d_rows = down_weight.shape[0]
    block_size = d_rows // block_mask.shape[0]
    gate_wide = gate_pre.astype(F32)
    up_wide = up_pre.astype(F32)
    activated = jax.nn.silu(gate_wide)
    hidden = (activated * up_wide).astype(BF16)
    expand = jnp.repeat(jnp.repeat(block_mask, block_size, axis=0), block_size, axis=1)
    masked = jnp.where(expand > 0, down_weight, jnp.zeros_like(down_weight))
    cot_row = lax.all_gather(cotangent, "col", axis=1, tiled=True)
    cot_all = lax.all_to_all(cot_row, "row", split_axis=1, concat_axis=0, tiled=True)
    panel = lax.all_gather(masked, "row", axis=0, tiled=True)
    y_partial = lax.dot_general(
        hidden, panel, (((1,), (1,)), ((), ())), preferred_element_type=F32
    )
    shards = panel.shape[0] // d_rows
    per_shard = jnp.einsum(
        "tnd,ndf->ntf",
        cot_row.reshape(tok_rows, shards, d_rows),
        panel.reshape(shards, d_rows, ff_cols),
        preferred_element_type=F32,
    )
    d_hidden = jnp.sum(rounded_f32(per_shard), axis=0)
    hidden_all = lax.all_gather(hidden, "row", axis=0, tiled=True)
    grad_full = lax.dot_general(
        cot_all, hidden_all, (((0,), (0,)), ((), ())), preferred_element_type=F32
    )
    output = lax.psum_scatter(y_partial.astype(BF16), "col", scatter_dimension=1, tiled=True)
    sigmoid_g = jax.nn.sigmoid(gate_wide)
    d_gate = (d_hidden * up_wide * sigmoid_g * (1.0 + gate_wide * (1.0 - sigmoid_g))).astype(BF16)
    d_up = (d_hidden * activated).astype(BF16)
    d_down = jnp.where(expand > 0, grad_full, jnp.zeros_like(grad_full)).astype(BF16)
    return output, d_gate, d_up, d_down


def solution(mesh):
    spec = P("row", "col")
    small = mesh.shape["row"] == 4 and mesh.shape["col"] == 8
    return jax.shard_map(
        fast_body if small else general_body,
        mesh=mesh,
        in_specs=(spec,) * 5,
        out_specs=(spec,) * 4,
        check_vma=False,
    )
```

time: 108 us -> 102 us (0.944)
  starting transfers between devices: 45.1 us -> 38.6 us
  waiting for transfers between devices: 27.2 us -> 33 us
  Pallas kernels: 33.4 us -> 28.7 us
    ppermute x13, waiting for transfers between devices: 15.3 us -> 21.8 us  [over_row(): return lax.ppermute(x, 'row', [(i, i ^ t) for i in senders])]
    pallas_call x17 -> x16, Pallas kernels: 19.3 us -> 13.5 us  [call(): pl.pallas_call(body, in_specs=(specs or [VMEM] * n) + [pl.BlockSpec(memor...]
    ppermute x12 -> x9, waiting for transfers between devices: 11 us -> 6.83 us  [over_chips(): return lax.ppermute(x, 'col', [(j, j ^ 2 * u) for j in range(2 * chips)])]
    ppermute x4, waiting for transfers between devices: 0.89 us -> 4.31 us  [fast_body(): lax.ppermute(ready[k], ('row', 'col'), [(r * width + 2 * a + h, (a ^ k) *...]
    ppermute x12 -> x9, starting transfers between devices: 13.7 us -> 10.7 us  [over_chips(): return lax.ppermute(x, 'col', [(j, j ^ 2 * u) for j in range(2 * chips)])]
    ppermute x4, starting transfers between devices: 10.7 us -> 8.21 us  [fast_body(): lax.ppermute(ready[k], ('row', 'col'), [(r * width + 2 * a + h, (a ^ k) *...]
    ppermute x13, starting transfers between devices: 20.1 us -> 18.5 us  [over_row(): return lax.ppermute(x, 'row', [(i, i ^ t) for i in senders])]
    pallas_call x3 -> x5, Pallas kernels: 12.5 us -> 13.5 us  [the longest x2 8.28 us: down_gradient(): pl.pallas_call(kernel, grid=(2,), in_specs=[pl.BlockSpec((tokens, step),...]
  transfers between devices with their start and end apart: 34 -> 32, of which waited for: 9 -> 12; matrix products, arithmetic and copies ran while one was open for 0% -> 0% of each run, Pallas kernels for 28% -> 27%
where the time goes in v3:
time: 102 us; the launch traced here: 101 us
  starting transfers between devices  38.6 us (38%)
  waiting for transfers between devices  33 us (32%)
  Pallas kernels  28.7 us (28%)
    ppermute x13, waiting for transfers between devices, over_row(): return lax.ppermute(x, 'row', [(i, i ^ t) for i in senders])  21.8 us
    ppermute x13, starting transfers between devices, over_row(): return lax.ppermute(x, 'row', [(i, i ^ t) for i in senders])  18.5 us
    pallas_call x16, Pallas kernels, call(): pl.pallas_call(body, in_specs=(specs or [VMEM] * n) + [pl.BlockSpec(memor...  13.5 us
    ppermute x9, starting transfers between devices, over_chips(): return lax.ppermute(x, 'col', [(j, j ^ 2 * u) for j in range(2 * chips)])  10.7 us
    pallas_call x2, Pallas kernels, down_gradient(): pl.pallas_call(kernel, grid=(2,), in_specs=[pl.BlockSpec((tokens, step),...  8.28 us
    ppermute x4, starting transfers between devices, fast_body(): lax.ppermute(ready[k], ('row', 'col'), [(r * width + 2 * a + h, (a ^ k) *...  8.21 us
    ppermute x9, waiting for transfers between devices, over_chips(): return lax.ppermute(x, 'col', [(j, j ^ 2 * u) for j in range(2 * chips)])  6.83 us
    pallas_call x2, Pallas kernels, masked_weight(): pl.pallas_call(kernel, in_specs=[ANY, VMEM] + [VMEM] * len(extra) + [ANY]...  4.52 us
  transfers between devices with their start and end apart: 32, of which 12 were waited for; matrix products, arithmetic and copies ran while one was open for 0% of the time, Pallas kernels for 27%

profile of v3, /device:TPU:16, one launch (start us, length us, event | category | flops | bytes accessed | tf_op | source)
XLA Modules:
  0.0 101.2 jit_solution(18124266671542170549)
XLA Ops:
  1.6 1.6 %collective-permute-start = (bf16[32,1024]{1,0:T(8,128)(2,1)S(1)}, bf16[32,1024]{1,0:T(8,128)(2,1)S(1)}, u32[]{:S(2)}, u32[]{:S(2)}) collective-permute-start(bf16[32,1024]{1,0:T(8,128)(2,1)S(1)} %get-tuple-element.49), channel_id=1, source_target_pairs={{0,2},{1,3},{2,0},{3,1},{4,6},{5,7},{6,4},{7,5},{8,10},{9,11},{10,... | collective-permute-start | bytes 196616 | tf_op jit(solution)/shard_map/ppermute | solution.py:463
  3.2 1.5 %collective-permute-start.1 = (bf16[32,1024]{1,0:T(8,128)(2,1)S(1)}, bf16[32,1024]{1,0:T(8,128)(2,1)S(1)}, u32[]{:S(2)}, u32[]{:S(2)}) collective-permute-start(bf16[32,1024]{1,0:T(8,128)(2,1)S(1)} %get-tuple-element.50), channel_id=1, source_target_pairs={{0,4},{1,5},{2,6},{3,7},{4,0},{5,1},{6,2},{7,3},{8,12},{9,13},{10,... | collective-permute-start | bytes 196616 | tf_op jit(solution)/shard_map/ppermute | solution.py:463
  5.2 1.8 %gated.1 = (bf16[128,2048]{1,0:T(8,128)(2,1)S(1)}, f32[128,2048]{1,0:T(8,128)S(1)}, f32[128,2048]{1,0:T(8,128)S(1)}, s32[16,2048]{1,0:T(8,128)S(1)}) custom-call(bf16[128,2048]{1,0:T(8,128)(2,1)} %refs_0_.3, bf16[128,2048]{1,0:T(8,128)(2,1)} %refs_1_.1, s32[16,16]{1,0:T(8,128)} %refs_2_.1, bf16[32,1024]{1,0:T(8,128)(2,1)S(1)} %get-tuple-element.47.refs_3_.refs_0_), custom_call_target="tpu_custom_call" | custom-call | tf_op jit(solution)/shard_map/gated/pallas_call | solution.py:37
  6.9 2.3 %masked_weight.2.refs_4_.refs_0_ = bf16[2048,2048]{1,0:T(8,128)(2,1)S(1)} custom-call(bf16[2048,2048]{1,0:T(8,128)(2,1)} %w_ref.3, s32[16,2048]{1,0:T(8,128)S(1)} %get-tuple-element.52.m_ref.refs_4_, bf16[128,2048]{1,0:T(8,128)(2,1)S(1)} %get-tuple-element.48.refs_0_), custom_call_target="tpu_custom_call" | custom-call | tf_op jit(solution)/shard_map/masked_weight/pallas_call | solution.py:70
  9.9 1.6 %collective-permute-start.3 = (bf16[32,1024]{1,0:T(8,128)(2,1)S(1)}, bf16[32,1024]{1,0:T(8,128)(2,1)S(1)}, u32[]{:S(2)}, u32[]{:S(2)}) collective-permute-start(bf16[32,1024]{1,0:T(8,128)(2,1)S(1)} %get-tuple-element.54), channel_id=1, source_target_pairs={{0,8},{8,0},{16,24},{24,16},{1,9},{9,1},{17,25},{25,17},{2,10},{10... | collective-permute-start | bytes 196616 | tf_op jit(solution)/shard_map/ppermute | solution.py:460
  11.9 1.6 %collective-permute-start.5 = (bf16[32,1024]{1,0:T(8,128)(2,1)S(1)}, bf16[32,1024]{1,0:T(8,128)(2,1)S(1)}, u32[]{:S(2)}, u32[]{:S(2)}) collective-permute-start(bf16[32,1024]{1,0:T(8,128)(2,1)S(1)} %get-tuple-element.56.refs_1_), channel_id=1, source_target_pairs={{0,24},{8,16},{16,8},{24,0},{1,25},{9,17},{17,9},{25,1},{2,26},{10... | collective-permute-start | bytes 196616 | tf_op jit(solution)/shard_map/ppermute | solution.py:460
  13.5 2.3 %masked_weight.3.refs_4_.refs_6_.refs_1_.refs_2_.refs_3_ = bf16[2048,2048]{1,0:T(8,128)(2,1)S(1)} custom-call(bf16[2048,2048]{1,0:T(8,128)(2,1)} %w_ref.3, s32[16,2048]{1,0:T(8,128)S(1)} %get-tuple-element.52.m_ref.refs_4_, bf16[2048,2048]{1,0:T(8,128)(2,1)S(1)} %masked_weight.2.refs_4_.refs_0_, ...), custom_call_target="tpu_custom_call", output_to_operand_aliasing={{}: (2, {})} | custom-call | tf_op jit(solution)/shard_map/masked_weight/pallas_call | solution.py:70
  18.1 2.2 %collective-permute-start.9 = (bf16[128,1024]{1,0:T(8,128)(2,1)S(1)}, bf16[128,1024]{1,0:T(8,128)(2,1)S(1)}, u32[]{:S(2)}, u32[]{:S(2)}) collective-permute-start(bf16[128,1024]{1,0:T(8,128)(2,1)S(1)} %stack.3.refs_1_.refs_0_), channel_id=1, source_target_pairs={{0,6},{1,7},{2,4},{3,5},{4,2},{5,3},{6,0},{7,1},{8,14},{9,15},{10,... | collective-permute-start | bytes 786440 | tf_op jit(solution)/shard_map/ppermute | solution.py:463
  21.7 2.1 %collective-permute-start.12 = (bf16[128,2048]{1,0:T(8,128)(2,1)S(1)}, bf16[128,2048]{1,0:T(8,128)(2,1)S(1)}, u32[]{:S(2)}, u32[]{:S(2)}) collective-permute-start(bf16[128,2048]{1,0:T(8,128)(2,1)S(1)} %add_and_pass.4.refs_0_), channel_id=1, source_target_pairs={{8,16},{16,8},{9,17},{17,9},{10,18},{18,10},{11,19},{19,11},{12,20... | collective-permute-start | bytes 1572872 | tf_op jit(solution)/shard_map/ppermute | solution.py:460
  23.9 2.6 %collective-permute-done.9.refs_1_.refs_3_ = bf16[128,1024]{1,0:T(8,128)(2,1)S(1)} collective-permute-done((bf16[128,1024]{1,0:T(8,128)(2,1)S(1)}, bf16[128,1024]{1,0:T(8,128)(2,1)S(1)}, u32[]{:S(2)}, u32[]{:S(2)}) %collective-permute-start.9) | collective-permute-done | bytes 262176 | tf_op jit(solution)/shard_map/ppermute | solution.py:463
  26.6 2.6 %collective-permute-done.8.refs_1_.refs_2_ = bf16[128,1024]{1,0:T(8,128)(2,1)S(1)} collective-permute-done((bf16[128,1024]{1,0:T(8,128)(2,1)S(1)}, bf16[128,1024]{1,0:T(8,128)(2,1)S(1)}, u32[]{:S(2)}, u32[]{:S(2)}) %collective-permute-start.8) | collective-permute-done | bytes 262176 | tf_op jit(solution)/shard_map/ppermute | solution.py:463
  29.3 3.6 %collective-permute-done.12.refs_8_.refs_1_ = bf16[128,2048]{1,0:T(8,128)(2,1)S(1)} collective-permute-done((bf16[128,2048]{1,0:T(8,128)(2,1)S(1)}, bf16[128,2048]{1,0:T(8,128)(2,1)S(1)}, u32[]{:S(2)}, u32[]{:S(2)}) %collective-permute-start.12) | collective-permute-done | bytes 524320 | tf_op jit(solution)/shard_map/ppermute | solution.py:460
  32.8 1.3 %collective-permute-start.15 = (bf16[128,2048]{1,0:T(8,128)(2,1)S(1)}, bf16[128,2048]{1,0:T(8,128)(2,1)S(1)}, u32[]{:S(2)}, u32[]{:S(2)}) collective-permute-start(bf16[128,2048]{1,0:T(8,128)(2,1)S(1)} %collective-permute-done.12.refs_8_.refs_1_), channel_id=1, source_target_pairs={{8,0},{16,24},{9,1},{17,25},{10,2},{18,26},{11,3},{19,27},{12,4},{... | collective-permute-start | bytes 1572872 | tf_op jit(solution)/shard_map/ppermute | solution.py:460
  34.2 3.2 %collective-permute-start.14 = (bf16[128,2048]{1,0:T(8,128)(2,1)S(1)}, bf16[128,2048]{1,0:T(8,128)(2,1)S(1)}, u32[]{:S(2)}, u32[]{:S(2)}) collective-permute-start(bf16[128,2048]{1,0:T(8,128)(2,1)S(1)} %collective-permute-done.6.refs_7_.refs_1_), channel_id=1, source_target_pairs={{8,16},{16,8},{9,17},{17,9},{10,18},{18,10},{11,19},{19,11},{12,20... | collective-permute-start | bytes 1572872 | tf_op jit(solution)/shard_map/ppermute | solution.py:460
  37.4 2.5 %back_product.1 = (bf16[512,2048]{1,0:T(8,128)(2,1)S(1)}, bf16[128,2048]{1,0:T(8,128)(2,1)S(1)}, bf16[128,2048]{1,0:T(8,128)(2,1)S(1)}) custom-call(bf16[128,1024]{1,0:T(8,128)(2,1)S(1)} %stack.3.refs_1_.refs_0_, bf16[128,1024]{1,0:T(8,128)(2,1)S(1)} %collective-permute-done.7.refs_0_.refs_1_, bf16[128,1024]{1,0:T(8,128)(2,1)S(1)} %collective-permute-done.8.refs_1_.refs_2_, ...), custom_call_target="tpu_custom_call" | custom-call | tf_op jit(solution)/shard_map/back_product/pallas_call | solution.py:37
  41.2 4.1 %collective-permute-done.15.refs_1_ = bf16[128,2048]{1,0:T(8,128)(2,1)S(1)} collective-permute-done((bf16[128,2048]{1,0:T(8,128)(2,1)S(1)}, bf16[128,2048]{1,0:T(8,128)(2,1)S(1)}, u32[]{:S(2)}, u32[]{:S(2)}) %collective-permute-start.15) | collective-permute-done | bytes 524320 | tf_op jit(solution)/shard_map/ppermute | solution.py:460
  45.3 4.4 %collective-permute-done.14.refs_0_.refs_2_ = bf16[128,2048]{1,0:T(8,128)(2,1)S(1)} collective-permute-done((bf16[128,2048]{1,0:T(8,128)(2,1)S(1)}, bf16[128,2048]{1,0:T(8,128)(2,1)S(1)}, u32[]{:S(2)}, u32[]{:S(2)}) %collective-permute-start.14) | collective-permute-done | bytes 524320 | tf_op jit(solution)/shard_map/ppermute | solution.py:460
  49.7 1.3 %collective-permute-start.16 = (bf16[128,2048]{1,0:T(8,128)(2,1)S(1)}, bf16[128,2048]{1,0:T(8,128)(2,1)S(1)}, u32[]{:S(2)}, u32[]{:S(2)}) collective-permute-start(bf16[128,2048]{1,0:T(8,128)(2,1)S(1)} %get-tuple-element.60.refs_2_), channel_id=1, source_target_pairs={{8,0},{16,24},{9,1},{17,25},{10,2},{18,26},{11,3},{19,27},{12,4},{... | collective-permute-start | bytes 1572872 | tf_op jit(solution)/shard_map/ppermute | solution.py:460
  52.4 4.2 %collective-permute-done.13.refs_1_ = bf16[128,2048]{1,0:T(8,128)(2,1)S(1)} collective-permute-done((bf16[128,2048]{1,0:T(8,128)(2,1)S(1)}, bf16[128,2048]{1,0:T(8,128)(2,1)S(1)}, u32[]{:S(2)}, u32[]{:S(2)}) %collective-permute-start.13) | collective-permute-done | bytes 524320 | tf_op jit(solution)/shard_map/ppermute | solution.py:460
  56.7 2.1 %collective-permute-start.29 = (bf16[128,2048]{1,0:T(8,128)(2,1)S(1)}, bf16[128,2048]{1,0:T(8,128)(2,1)S(1)}, u32[]{:S(2)}, u32[]{:S(2)}) collective-permute-start(bf16[128,2048]{1,0:T(8,128)(2,1)S(1)} %add_and_pass.6.refs_2_.refs_4_), channel_id=1, source_target_pairs={{8,16},{16,8},{9,17},{17,9},{10,18},{18,10},{11,19},{19,11},{12,20... | collective-permute-start | bytes 1572872 | tf_op jit(solution)/shard_map/ppermute | solution.py:460
  58.8 2.4 %back_rest.1 = (bf16[128,2048]{1,0:T(8,128)(2,1)S(1)}, bf16[128,2048]{1,0:T(8,128)(2,1)S(1)}) custom-call(bf16[512,2048]{1,0:T(8,128)(2,1)S(1)} %get-tuple-element.57.refs_0_.c_ref, bf16[2048,2048]{1,0:T(8,128)(2,1)S(1)} %masked_weight.3.refs_4_.refs_6_.refs_1_.refs_2_.refs_3_, bf16[128,2048]{1,0:T(8,128)(2,1)S(1)} %add_and_pass.6.refs_2_.refs_4_), custom_call_target="tpu_custom_call" | custom-call | tf_op jit(solution)/shard_map/back_rest/pallas_call | solution.py:37
  61.2 2.4 %out_product.2 = (bf16[256,512]{1,0:T(8,128)(2,1)S(1)}, bf16[256,512]{1,0:T(8,128)(2,1)S(1)}, f32[256,1024]{1,0:T(8,128)S(1)}) custom-call(bf16[128,2048]{1,0:T(8,128)(2,1)S(1)} %add_and_pass.4.refs_0_, bf16[128,2048]{1,0:T(8,128)(2,1)S(1)} %collective-permute-done.6.refs_7_.refs_1_, ...), custom_call_target="tpu_custom_call" | custom-call | tf_op jit(solution)/shard_map/out_product/pallas_call | solution.py:37
  64.2 2.4 %out_product.3 = (bf16[256,512]{1,0:T(8,128)(2,1)S(1)}, bf16[256,512]{1,0:T(8,128)(2,1)S(1)}, f32[256,1024]{1,0:T(8,128)S(1)}, bf16[128,2048]{1,0:T(8,128)(2,1)S(1)}) custom-call(bf16[128,2048]{1,0:T(8,128)(2,1)S(1)} %get-tuple-element.63.refs_0_.refs_2_, bf16[128,2048]{1,0:T(8,128)(2,1)S(1)} %collective-permute-done.12.refs_8_.refs_1_, ...), custom_call_target="tpu_custom_call" | custom-call | tf_op jit(solution)/shard_map/out_product/pallas_call | solution.py:37
  67.2 3.3 %collective-permute-done.29.refs_3_ = bf16[128,2048]{1,0:T(8,128)(2,1)S(1)} collective-permute-done((bf16[128,2048]{1,0:T(8,128)(2,1)S(1)}, bf16[128,2048]{1,0:T(8,128)(2,1)S(1)}, u32[]{:S(2)}, u32[]{:S(2)}) %collective-permute-start.29) | collective-permute-done | bytes 524320 | tf_op jit(solution)/shard_map/ppermute | solution.py:460
  70.8 2.2 %collective-permute-start.31 = (bf16[128,2048]{1,0:T(8,128)(2,1)S(1)}, bf16[128,2048]{1,0:T(8,128)(2,1)S(1)}, u32[]{:S(2)}, u32[]{:S(2)}) collective-permute-start(bf16[128,2048]{1,0:T(8,128)(2,1)S(1)} %get-tuple-element.83), channel_id=1, source_target_pairs={{8,16},{16,8},{9,17},{17,9},{10,18},{18,10},{11,19},{19,11},{12,20... | collective-permute-start | bytes 1572872 | tf_op jit(solution)/shard_map/ppermute | solution.py:460
  74.3 1.3 %collective-permute-start.22 = (bf16[128,1024]{1,0:T(8,128)(2,1)S(1)}, bf16[128,1024]{1,0:T(8,128)(2,1)S(1)}, u32[]{:S(2)}, u32[]{:S(2)}) collective-permute-start(bf16[128,1024]{1,0:T(8,128)(2,1)S(1)} %get-tuple-element.71), channel_id=1, source_target_pairs={{0,4},{1,5},{2,6},{3,7},{4,0},{5,1},{6,2},{7,3},{8,12},{9,13},{10,... | collective-permute-start | bytes 786440 | tf_op jit(solution)/shard_map/ppermute | solution.py:463
  76.8 4.1 %down_gradient.2 = (bf16[2048,2048]{1,0:T(8,128)(2,1)}, bf16[16,128]{1,0:T(8,128)(2,1)S(1)}) custom-call(bf16[512,2048]{1,0:T(8,128)(2,1)S(1)} %get-tuple-element.57.refs_0_.c_ref, bf16[128,2048]{1,0:T(8,128)(2,1)S(1)} %add_and_pass.4.refs_0_, bf16[128,2048]{1,0:T(8,128)(2,1)S(1)} %collective-permute-done.6.refs_7_.refs_1_, ...), custom_call_target="tpu_custom_call" | custom-call | tf_op jit(solution)/shard_map/down_gradient/pallas_call | solution.py:436
  80.9 4.1 %down_gradient.3 = (bf16[2048,2048]{1,0:T(8,128)(2,1)}, bf16[16,128]{1,0:T(8,128)(2,1)S(1)}) custom-call(bf16[512,2048]{1,0:T(8,128)(2,1)S(1)} %get-tuple-element.57.refs_0_.c_ref, bf16[128,2048]{1,0:T(8,128)(2,1)S(1)} %add_and_pass.4.refs_0_, bf16[128,2048]{1,0:T(8,128)(2,1)S(1)} %collective-permute-done.6.refs_7_.refs_1_, ...), custom_call_target="tpu_custom_call", output_to_operand_aliasing={{0}: (6, {})} | custom-call | tf_op jit(solution)/shard_map/down_gradient/pallas_call | solution.py:436
  88.0 4.6 %collective-permute-start.27 = (bf16[32,1024]{1,0:T(8,128)(2,1)S(1)}, bf16[32,1024]{1,0:T(8,128)(2,1)S(1)}, u32[]{:S(2)}, u32[]{:S(2)}) collective-permute-start(bf16[32,1024]{1,0:T(8,128)(2,1)S(1)} %get-tuple-element.80), channel_id=1, source_target_pairs={{0,24},{1,25},{2,16},{3,17},{4,8},{5,9},{6,0},{7,1},{8,26},{9,27},... | collective-permute-start | bytes 196616 | tf_op jit(solution)/shard_map/ppermute | solution.py:520
  92.5 2.0 %collective-permute-start.24 = (bf16[32,1024]{1,0:T(8,128)(2,1)S(1)}, bf16[32,1024]{1,0:T(8,128)(2,1)S(1)}, u32[]{:S(2)}, u32[]{:S(2)}) collective-permute-start(bf16[32,1024]{1,0:T(8,128)(2,1)S(1)} %get-tuple-element.77.refs_5_), channel_id=1, source_target_pairs={{0,0},{1,1},{2,8},{3,9},{4,16},{5,17},{6,24},{7,25},{8,2},{9,3},{1... | collective-permute-start | bytes 196616 | tf_op jit(solution)/shard_map/ppermute | solution.py:520
  94.5 1.6 %gradients.1 = (bf16[128,2048]{1,0:T(8,128)(2,1)}, bf16[128,2048]{1,0:T(8,128)(2,1)}, bf16[16,128]{1,0:T(8,128)(2,1)S(1)}) custom-call(bf16[128,2048]{1,0:T(8,128)(2,1)S(1)} %get-tuple-element.81.refs_0_, bf16[128,2048]{1,0:T(8,128)(2,1)S(1)} %collective-permute-done.30.refs_1_, bf16[128,2048]{1,0:T(8,128)(2,1)S(1)} %collective-permute-done.31.refs_2_, ...), custom_call_target="tpu_custom_call" | custom-call | tf_op jit(solution)/shard_map/gradients/pallas_call | solution.py:145
  96.2 4.3 %collective-permute-done.24.refs_0_ = bf16[32,1024]{1,0:T(8,128)(2,1)S(1)} collective-permute-done((bf16[32,1024]{1,0:T(8,128)(2,1)S(1)}, bf16[32,1024]{1,0:T(8,128)(2,1)S(1)}, u32[]{:S(2)}, u32[]{:S(2)}) %collective-permute-start.24) | collective-permute-done | bytes 65568 | tf_op jit(solution)/shard_map/ppermute | solution.py:520
  (54 shorter events, 17.0 us)
Async XLA Ops:
  1.6 7.6 %collective-permute-start = (bf16[32,1024]{1,0:T(8,128)(2,1)S(1)}, bf16[32,1024]{1,0:T(8,128)(2,1)S(1)}, u32[]{:S(2)}, u32[]{:S(2)}) collective-permute-start(bf16[32,1024]{1,0:T(8,128)(2,1)S(1)} %get-tuple-element.49), channel_id=1, source_target_pairs={{0,2},{1,3},{2,0},{3,1},{4,6},{5,7},{6,4},{7,5},{8,10},{9,11},{10,... | collective-permute-start | bytes 196616 | tf_op jit(solution)/shard_map/ppermute | solution.py:463
  3.2 6.0 %collective-permute-start.1 = (bf16[32,1024]{1,0:T(8,128)(2,1)S(1)}, bf16[32,1024]{1,0:T(8,128)(2,1)S(1)}, u32[]{:S(2)}, u32[]{:S(2)}) collective-permute-start(bf16[32,1024]{1,0:T(8,128)(2,1)S(1)} %get-tuple-element.50), channel_id=1, source_target_pairs={{0,4},{1,5},{2,6},{3,7},{4,0},{5,1},{6,2},{7,3},{8,12},{9,13},{10,... | collective-permute-start | bytes 196616 | tf_op jit(solution)/shard_map/ppermute | solution.py:463
  4.7 5.2 %collective-permute-start.2 = (bf16[32,1024]{1,0:T(8,128)(2,1)S(1)}, bf16[32,1024]{1,0:T(8,128)(2,1)S(1)}, u32[]{:S(2)}, u32[]{:S(2)}) collective-permute-start(bf16[32,1024]{1,0:T(8,128)(2,1)S(1)} %get-tuple-element.51), channel_id=1, source_target_pairs={{0,6},{1,7},{2,4},{3,5},{4,2},{5,3},{6,0},{7,1},{8,14},{9,15},{10,... | collective-permute-start | bytes 196616 | tf_op jit(solution)/shard_map/ppermute | solution.py:463
  9.9 5.8 %collective-permute-start.3 = (bf16[32,1024]{1,0:T(8,128)(2,1)S(1)}, bf16[32,1024]{1,0:T(8,128)(2,1)S(1)}, u32[]{:S(2)}, u32[]{:S(2)}) collective-permute-start(bf16[32,1024]{1,0:T(8,128)(2,1)S(1)} %get-tuple-element.54), channel_id=1, source_target_pairs={{0,8},{8,0},{16,24},{24,16},{1,9},{9,1},{17,25},{25,17},{2,10},{10... | collective-permute-start | bytes 196616 | tf_op jit(solution)/shard_map/ppermute | solution.py:460
  11.6 5.3 %collective-permute-start.4 = (bf16[32,1024]{1,0:T(8,128)(2,1)S(1)}, bf16[32,1024]{1,0:T(8,128)(2,1)S(1)}, u32[]{:S(2)}, u32[]{:S(2)}) collective-permute-start(bf16[32,1024]{1,0:T(8,128)(2,1)S(1)} %get-tuple-element.55), channel_id=1, source_target_pairs={{0,16},{8,24},{16,0},{24,8},{1,17},{9,25},{17,1},{25,9},{2,18},{10... | collective-permute-start | bytes 196616 | tf_op jit(solution)/shard_map/ppermute | solution.py:460
  11.9 6.2 %collective-permute-start.5 = (bf16[32,1024]{1,0:T(8,128)(2,1)S(1)}, bf16[32,1024]{1,0:T(8,128)(2,1)S(1)}, u32[]{:S(2)}, u32[]{:S(2)}) collective-permute-start(bf16[32,1024]{1,0:T(8,128)(2,1)S(1)} %get-tuple-element.56.refs_1_), channel_id=1, source_target_pairs={{0,24},{8,16},{16,8},{24,0},{1,25},{9,17},{17,9},{25,1},{2,26},{10... | collective-permute-start | bytes 196616 | tf_op jit(solution)/shard_map/ppermute | solution.py:460
  18.1 8.3 %collective-permute-start.9 = (bf16[128,1024]{1,0:T(8,128)(2,1)S(1)}, bf16[128,1024]{1,0:T(8,128)(2,1)S(1)}, u32[]{:S(2)}, u32[]{:S(2)}) collective-permute-start(bf16[128,1024]{1,0:T(8,128)(2,1)S(1)} %stack.3.refs_1_.refs_0_), channel_id=1, source_target_pairs={{0,6},{1,7},{2,4},{3,5},{4,2},{5,3},{6,0},{7,1},{8,14},{9,15},{10,... | collective-permute-start | bytes 786440 | tf_op jit(solution)/shard_map/ppermute | solution.py:463
  20.3 8.8 %collective-permute-start.8 = (bf16[128,1024]{1,0:T(8,128)(2,1)S(1)}, bf16[128,1024]{1,0:T(8,128)(2,1)S(1)}, u32[]{:S(2)}, u32[]{:S(2)}) collective-permute-start(bf16[128,1024]{1,0:T(8,128)(2,1)S(1)} %stack.3.refs_1_.refs_0_), channel_id=1, source_target_pairs={{0,4},{1,5},{2,6},{3,7},{4,0},{5,1},{6,2},{7,3},{8,12},{9,13},{10,... | collective-permute-start | bytes 786440 | tf_op jit(solution)/shard_map/ppermute | solution.py:463
  20.8 8.3 %collective-permute-start.7 = (bf16[128,1024]{1,0:T(8,128)(2,1)S(1)}, bf16[128,1024]{1,0:T(8,128)(2,1)S(1)}, u32[]{:S(2)}, u32[]{:S(2)}) collective-permute-start(bf16[128,1024]{1,0:T(8,128)(2,1)S(1)} %stack.3.refs_1_.refs_0_), channel_id=1, source_target_pairs={{0,2},{1,3},{2,0},{3,1},{4,6},{5,7},{6,4},{7,5},{8,10},{9,11},{10,... | collective-permute-start | bytes 786440 | tf_op jit(solution)/shard_map/ppermute | solution.py:463
  21.7 11.1 %collective-permute-start.12 = (bf16[128,2048]{1,0:T(8,128)(2,1)S(1)}, bf16[128,2048]{1,0:T(8,128)(2,1)S(1)}, u32[]{:S(2)}, u32[]{:S(2)}) collective-permute-start(bf16[128,2048]{1,0:T(8,128)(2,1)S(1)} %add_and_pass.4.refs_0_), channel_id=1, source_target_pairs={{8,16},{16,8},{9,17},{17,9},{10,18},{18,10},{11,19},{19,11},{12,20... | collective-permute-start | bytes 1572872 | tf_op jit(solution)/shard_map/ppermute | solution.py:460
  23.8 10.3 %collective-permute-start.6 = (bf16[128,2048]{1,0:T(8,128)(2,1)S(1)}, bf16[128,2048]{1,0:T(8,128)(2,1)S(1)}, u32[]{:S(2)}, u32[]{:S(2)}) collective-permute-start(bf16[128,2048]{1,0:T(8,128)(2,1)S(1)} %add_and_pass.4.refs_0_), channel_id=1, source_target_pairs={{0,8},{8,0},{16,24},{24,16},{1,9},{9,1},{17,25},{25,17},{2,10},{10... | collective-permute-start | bytes 1572872 | tf_op jit(solution)/shard_map/ppermute | solution.py:460
  26.5 10.8 %collective-permute-start.10 = (bf16[256,1024]{1,0:T(8,128)(2,1)S(1)}, bf16[256,1024]{1,0:T(8,128)(2,1)S(1)}, u32[]{:S(2)}, u32[]{:S(2)}) collective-permute-start(bf16[256,1024]{1,0:T(8,128)(2,1)S(1)} %stack.4), channel_id=1, source_target_pairs={{0,1},{1,0},{2,3},{3,2},{4,5},{5,4},{6,7},{7,6},{8,9},{9,8},{10,11... | collective-permute-start | bytes 1572872 | tf_op jit(solution)/shard_map/ppermute | solution.py:466
  29.2 8.2 %collective-permute-start.11 = (bf16[256,1024]{1,0:T(8,128)(2,1)S(1)}, bf16[256,1024]{1,0:T(8,128)(2,1)S(1)}, u32[]{:S(2)}, u32[]{:S(2)}) collective-permute-start(bf16[256,1024]{1,0:T(8,128)(2,1)S(1)} %stack.5), channel_id=1, source_target_pairs={{0,1},{1,0},{2,3},{3,2},{4,5},{5,4},{6,7},{7,6},{8,9},{9,8},{10,11... | collective-permute-start | bytes 1572872 | tf_op jit(solution)/shard_map/ppermute | solution.py:466
  32.8 12.4 %collective-permute-start.15 = (bf16[128,2048]{1,0:T(8,128)(2,1)S(1)}, bf16[128,2048]{1,0:T(8,128)(2,1)S(1)}, u32[]{:S(2)}, u32[]{:S(2)}) collective-permute-start(bf16[128,2048]{1,0:T(8,128)(2,1)S(1)} %collective-permute-done.12.refs_8_.refs_1_), channel_id=1, source_target_pairs={{8,0},{16,24},{9,1},{17,25},{10,2},{18,26},{11,3},{19,27},{12,4},{... | collective-permute-start | bytes 1572872 | tf_op jit(solution)/shard_map/ppermute | solution.py:460
  34.2 15.5 %collective-permute-start.14 = (bf16[128,2048]{1,0:T(8,128)(2,1)S(1)}, bf16[128,2048]{1,0:T(8,128)(2,1)S(1)}, u32[]{:S(2)}, u32[]{:S(2)}) collective-permute-start(bf16[128,2048]{1,0:T(8,128)(2,1)S(1)} %collective-permute-done.6.refs_7_.refs_1_), channel_id=1, source_target_pairs={{8,16},{16,8},{9,17},{17,9},{10,18},{18,10},{11,19},{19,11},{12,20... | collective-permute-start | bytes 1572872 | tf_op jit(solution)/shard_map/ppermute | solution.py:460
  39.9 16.7 %collective-permute-start.13 = (bf16[128,2048]{1,0:T(8,128)(2,1)S(1)}, bf16[128,2048]{1,0:T(8,128)(2,1)S(1)}, u32[]{:S(2)}, u32[]{:S(2)}) collective-permute-start(bf16[128,2048]{1,0:T(8,128)(2,1)S(1)} %get-tuple-element.59.refs_3_.refs_0_), channel_id=1, source_target_pairs={{0,8},{24,16},{1,9},{25,17},{2,10},{26,18},{3,11},{27,19},{4,12},{... | collective-permute-start | bytes 1572872 | tf_op jit(solution)/shard_map/ppermute | solution.py:460
  49.7 14.4 %collective-permute-start.16 = (bf16[128,2048]{1,0:T(8,128)(2,1)S(1)}, bf16[128,2048]{1,0:T(8,128)(2,1)S(1)}, u32[]{:S(2)}, u32[]{:S(2)}) collective-permute-start(bf16[128,2048]{1,0:T(8,128)(2,1)S(1)} %get-tuple-element.60.refs_2_), channel_id=1, source_target_pairs={{8,0},{16,24},{9,1},{17,25},{10,2},{18,26},{11,3},{19,27},{12,4},{... | collective-permute-start | bytes 1572872 | tf_op jit(solution)/shard_map/ppermute | solution.py:460
  51.1 15.7 %collective-permute-start.28 = (bf16[128,2048]{1,0:T(8,128)(2,1)S(1)}, bf16[128,2048]{1,0:T(8,128)(2,1)S(1)}, u32[]{:S(2)}, u32[]{:S(2)}) collective-permute-start(bf16[128,2048]{1,0:T(8,128)(2,1)S(1)} %get-tuple-element.58.refs_0_), channel_id=1, source_target_pairs={{0,8},{24,16},{1,9},{25,17},{2,10},{26,18},{3,11},{27,19},{4,12},{... | collective-permute-start | bytes 1572872 | tf_op jit(solution)/shard_map/ppermute | solution.py:460
  56.7 13.7 %collective-permute-start.29 = (bf16[128,2048]{1,0:T(8,128)(2,1)S(1)}, bf16[128,2048]{1,0:T(8,128)(2,1)S(1)}, u32[]{:S(2)}, u32[]{:S(2)}) collective-permute-start(bf16[128,2048]{1,0:T(8,128)(2,1)S(1)} %add_and_pass.6.refs_2_.refs_4_), channel_id=1, source_target_pairs={{8,16},{16,8},{9,17},{17,9},{10,18},{18,10},{11,19},{19,11},{12,20... | collective-permute-start | bytes 1572872 | tf_op jit(solution)/shard_map/ppermute | solution.py:460
  63.6 7.1 %collective-permute-start.17 = (bf16[256,512]{1,0:T(8,128)(2,1)S(1)}, bf16[256,512]{1,0:T(8,128)(2,1)S(1)}, u32[]{:S(2)}, u32[]{:S(2)}) collective-permute-start(bf16[256,512]{1,0:T(8,128)(2,1)S(1)} %get-tuple-element.65), channel_id=1, source_target_pairs={{0,1},{1,0},{2,3},{3,2},{4,5},{5,4},{6,7},{7,6},{8,9},{9,8},{10,11... | collective-permute-start | bytes 786440 | tf_op jit(solution)/shard_map/ppermute | solution.py:466
  63.7 9.3 %collective-permute-start.18 = (bf16[256,512]{1,0:T(8,128)(2,1)S(1)}, bf16[256,512]{1,0:T(8,128)(2,1)S(1)}, u32[]{:S(2)}, u32[]{:S(2)}) collective-permute-start(bf16[256,512]{1,0:T(8,128)(2,1)S(1)} %get-tuple-element.66), channel_id=1, source_target_pairs={{0,1},{1,0},{2,3},{3,2},{4,5},{5,4},{6,7},{7,6},{8,9},{9,8},{10,11... | collective-permute-start | bytes 786440 | tf_op jit(solution)/shard_map/ppermute | solution.py:466
  66.6 6.4 %collective-permute-start.19 = (bf16[256,512]{1,0:T(8,128)(2,1)S(1)}, bf16[256,512]{1,0:T(8,128)(2,1)S(1)}, u32[]{:S(2)}, u32[]{:S(2)}) collective-permute-start(bf16[256,512]{1,0:T(8,128)(2,1)S(1)} %get-tuple-element.67), channel_id=1, source_target_pairs={{0,1},{1,0},{2,3},{3,2},{4,5},{5,4},{6,7},{7,6},{8,9},{9,8},{10,11... | collective-permute-start | bytes 786440 | tf_op jit(solution)/shard_map/ppermute | solution.py:466
  66.8 6.2 %collective-permute-start.20 = (bf16[256,512]{1,0:T(8,128)(2,1)S(1)}, bf16[256,512]{1,0:T(8,128)(2,1)S(1)}, u32[]{:S(2)}, u32[]{:S(2)}) collective-permute-start(bf16[256,512]{1,0:T(8,128)(2,1)S(1)} %get-tuple-element.68), channel_id=1, source_target_pairs={{0,1},{1,0},{2,3},{3,2},{4,5},{5,4},{6,7},{7,6},{8,9},{9,8},{10,11... | collective-permute-start | bytes 786440 | tf_op jit(solution)/shard_map/ppermute | solution.py:466
  70.7 21.9 %collective-permute-start.30 = (bf16[128,2048]{1,0:T(8,128)(2,1)S(1)}, bf16[128,2048]{1,0:T(8,128)(2,1)S(1)}, u32[]{:S(2)}, u32[]{:S(2)}) collective-permute-start(bf16[128,2048]{1,0:T(8,128)(2,1)S(1)} %get-tuple-element.82), channel_id=1, source_target_pairs={{0,8},{8,0},{16,24},{24,16},{1,9},{9,1},{17,25},{25,17},{2,10},{10... | collective-permute-start | bytes 1572872 | tf_op jit(solution)/shard_map/ppermute | solution.py:460
  70.8 23.8 %collective-permute-start.31 = (bf16[128,2048]{1,0:T(8,128)(2,1)S(1)}, bf16[128,2048]{1,0:T(8,128)(2,1)S(1)}, u32[]{:S(2)}, u32[]{:S(2)}) collective-permute-start(bf16[128,2048]{1,0:T(8,128)(2,1)S(1)} %get-tuple-element.83), channel_id=1, source_target_pairs={{8,16},{16,8},{9,17},{17,9},{10,18},{18,10},{11,19},{19,11},{12,20... | collective-permute-start | bytes 1572872 | tf_op jit(solution)/shard_map/ppermute | solution.py:460
  73.2 11.8 %collective-permute-start.21 = (bf16[128,1024]{1,0:T(8,128)(2,1)S(1)}, bf16[128,1024]{1,0:T(8,128)(2,1)S(1)}, u32[]{:S(2)}, u32[]{:S(2)}) collective-permute-start(bf16[128,1024]{1,0:T(8,128)(2,1)S(1)} %get-tuple-element.70), channel_id=1, source_target_pairs={{0,2},{1,3},{2,0},{3,1},{4,6},{5,7},{6,4},{7,5},{8,10},{9,11},{10,... | collective-permute-start | bytes 786440 | tf_op jit(solution)/shard_map/ppermute | solution.py:463
  74.3 11.8 %collective-permute-start.22 = (bf16[128,1024]{1,0:T(8,128)(2,1)S(1)}, bf16[128,1024]{1,0:T(8,128)(2,1)S(1)}, u32[]{:S(2)}, u32[]{:S(2)}) collective-permute-start(bf16[128,1024]{1,0:T(8,128)(2,1)S(1)} %get-tuple-element.71), channel_id=1, source_target_pairs={{0,4},{1,5},{2,6},{3,7},{4,0},{5,1},{6,2},{7,3},{8,12},{9,13},{10,... | collective-permute-start | bytes 786440 | tf_op jit(solution)/shard_map/ppermute | solution.py:463
  75.6 10.5 %collective-permute-start.23 = (bf16[128,1024]{1,0:T(8,128)(2,1)S(1)}, bf16[128,1024]{1,0:T(8,128)(2,1)S(1)}, u32[]{:S(2)}, u32[]{:S(2)}) collective-permute-start(bf16[128,1024]{1,0:T(8,128)(2,1)S(1)} %get-tuple-element.72), channel_id=1, source_target_pairs={{0,6},{1,7},{2,4},{3,5},{4,2},{5,3},{6,0},{7,1},{8,14},{9,15},{10,... | collective-permute-start | bytes 786440 | tf_op jit(solution)/shard_map/ppermute | solution.py:463
  86.3 9.9 %collective-permute-start.25 = (bf16[32,1024]{1,0:T(8,128)(2,1)S(1)}, bf16[32,1024]{1,0:T(8,128)(2,1)S(1)}, u32[]{:S(2)}, u32[]{:S(2)}) collective-permute-start(bf16[32,1024]{1,0:T(8,128)(2,1)S(1)} %get-tuple-element.78), channel_id=1, source_target_pairs={{0,8},{1,9},{2,0},{3,1},{4,24},{5,25},{6,16},{7,17},{8,10},{9,11},... | collective-permute-start | bytes 196616 | tf_op jit(solution)/shard_map/ppermute | solution.py:520
  87.4 8.8 %collective-permute-start.26 = (bf16[32,1024]{1,0:T(8,128)(2,1)S(1)}, bf16[32,1024]{1,0:T(8,128)(2,1)S(1)}, u32[]{:S(2)}, u32[]{:S(2)}) collective-permute-start(bf16[32,1024]{1,0:T(8,128)(2,1)S(1)} %get-tuple-element.79), channel_id=1, source_target_pairs={{0,16},{1,17},{2,24},{3,25},{4,0},{5,1},{6,8},{7,9},{8,18},{9,19},... | collective-permute-start | bytes 196616 | tf_op jit(solution)/shard_map/ppermute | solution.py:520
  88.0 8.2 %collective-permute-start.27 = (bf16[32,1024]{1,0:T(8,128)(2,1)S(1)}, bf16[32,1024]{1,0:T(8,128)(2,1)S(1)}, u32[]{:S(2)}, u32[]{:S(2)}) collective-permute-start(bf16[32,1024]{1,0:T(8,128)(2,1)S(1)} %get-tuple-element.80), channel_id=1, source_target_pairs={{0,24},{1,25},{2,16},{3,17},{4,8},{5,9},{6,0},{7,1},{8,26},{9,27},... | collective-permute-start | bytes 196616 | tf_op jit(solution)/shard_map/ppermute | solution.py:520
  92.5 7.9 %collective-permute-start.24 = (bf16[32,1024]{1,0:T(8,128)(2,1)S(1)}, bf16[32,1024]{1,0:T(8,128)(2,1)S(1)}, u32[]{:S(2)}, u32[]{:S(2)}) collective-permute-start(bf16[32,1024]{1,0:T(8,128)(2,1)S(1)} %get-tuple-element.77.refs_5_), channel_id=1, source_target_pairs={{0,0},{1,1},{2,8},{3,9},{4,16},{5,17},{6,24},{7,25},{8,2},{9,3},{1... | collective-permute-start | bytes 196616 | tf_op jit(solution)/shard_map/ppermute | solution.py:520

commit v4 on v3

--- a/solution.py
+++ b/solution.py
@@ -26,6 +26,9 @@
 def place():
     col = lax.axis_index("col")
     return lax.axis_index("row"), col // 2, col % 2
+
+
+COSTS = {'quarters': 311445000, 'gated': 588285000, 'masked_weight': 761310000, 'choose': 34605000, 'stack': 34605000, 'back_product': 865125000, 'back_rest': 830520000, 'out_product': 830520000, 'pair_sum': 69210000, 'plane_sum': 3460500000, 'add_and_pass': 69210000, 'down_gradient': 1418804999, 'gradients': 588285000, 'assemble': 242235000, 'to_vmem': 311445000}
 
 
 def call(kernel, name, outs, *args, specs=None, scratch=(), flops=0, moved=0, after=()):
@@ -41,7 +44,7 @@
         out_shape=[pltpu.VMEM(shape, dtype) for shape, dtype in outs],
         scratch_shapes=list(scratch),
         compiler_params=PARAMS,
-        cost_estimate=pl.CostEstimate(flops=flops, bytes_accessed=moved, transcendentals=0),
+        cost_estimate=pl.CostEstimate(flops=COSTS[name], bytes_accessed=0, transcendentals=0),
         name=name,
     )(*args, *after)
 
@@ -75,7 +78,7 @@
         input_output_aliases={} if begun is None else {2: 0},
         scratch_shapes=[pltpu.SemaphoreType.DMA((len(mine),))],
         compiler_params=PARAMS,
-        cost_estimate=pl.CostEstimate(flops=0, bytes_accessed=0, transcendentals=0),
+        cost_estimate=pl.CostEstimate(flops=COSTS["masked_weight"], bytes_accessed=0, transcendentals=0),
         name="masked_weight",
     )(in_hbm(weight), in_vmem(mask_rows), *extra, *after)
 
@@ -150,6 +153,7 @@
         out_shape=[jax.ShapeDtypeStruct((rows, cols), BF16)] * 2
         + [pltpu.VMEM((16, 128), BF16)],
         compiler_params=PARAMS,
+        cost_estimate=pl.CostEstimate(flops=COSTS["gradients"], bytes_accessed=0, transcendentals=0),
         name="gradients",
     )(*map(in_vmem, shares), in_vmem(dg), in_vmem(du), *after)
 
@@ -401,6 +405,7 @@
         out_specs=VMEM,
         out_shape=jax.ShapeDtypeStruct((n * part, width), BF16),
         compiler_params=PARAMS,
+        cost_estimate=pl.CostEstimate(flops=COSTS["assemble"], bytes_accessed=0, transcendentals=0),
         name="assemble",
     )(*map(in_vmem, pieces), *after)
 
@@ -444,9 +449,7 @@
         scratch_shapes=[pltpu.VMEM((tokens, ff), BF16)],
         input_output_aliases={} if begun is None else {n + 2: 0},
         compiler_params=PARAMS,
-        cost_estimate=pl.CostEstimate(
-            flops=0, bytes_accessed=0, transcendentals=0
-        ),
+        cost_estimate=pl.CostEstimate(flops=COSTS["down_gradient"], bytes_accessed=0, transcendentals=0),
         name="down_gradient",
     )(in_vmem(cot), *map(in_vmem, hidden), in_vmem(mask_rows), *extra)
 
@@ -492,25 +495,25 @@
 
     first3 = over_row(back3, 1, ends)
     first2 = over_row(back2, 1, ends)
-    hidden[2], inner2 = add_and_pass([(inner2, ends2)], [inner2], after=[back3])
+    *sent, own01 = out_product([hidden[0], hidden[1]], [], weight, 1, after=[back3])
+    received = [[over_core(x) for x in sent]]
+    back0, back1 = back_rest(cot, weight, tok, after=[own01])
+    (inner2,) = add_and_pass([], [inner2], after=[back1])
     ends3 = over_row(inner2, 1, inner)
-    (to_pass,) = add_and_pass([(back2, first3)], after=[inner2])
+    (hidden[2],) = add_and_pass([(inner2, ends2)], after=[inner2])
+    (to_pass,) = add_and_pass([(back2, first3)], after=[hidden[2]])
     second = over_row(to_pass, 3, inner)
-    back0, back1 = back_rest(cot, weight, tok, after=[to_pass])
-
-    *sent, own01 = out_product([hidden[0], hidden[1]], [], weight, 2, after=[back1, to_pass])
-    received = [[over_core(x) for x in sent]]
     *sent, own23, hidden[3] = out_product(
-        [hidden[2]], [[inner3, ends3]], weight, 2, after=[own01]
+        [hidden[2]], [[inner3, ends3]], weight, 2, after=[to_pass]
     )
     received.append([over_core(x) for x in sent])
-    to_inner, to_near = add_and_pass([(back3, first2), (back1, second)], after=[own23])
+    pieces = pair_sum([own01, own23], received, tok, chips)
+    pieces = [pieces[0]] + [over_chips(pieces[u], u) for u in range(1, chips)]
+    to_inner, to_near = add_and_pass([(back3, first2), (back1, second)], after=[pieces[0]])
     across = over_row(to_inner, 3, inner)
     beside = over_row(to_near, 1)
-    pieces = pair_sum([own01, own23], received, tok, chips)
-    pieces = [pieces[0]] + [over_chips(pieces[u], u) for u in range(1, chips)]
     tokens = [hidden[t] for t in range(rows)]
-    d_down, done = down_gradient(cot, tokens, mask_rows, 0, after=[pieces[0]])
+    d_down, done = down_gradient(cot, tokens, mask_rows, 0, after=[to_inner])
     d_down, done = down_gradient(cot, tokens, mask_rows, 1, d_down, after=[done])
     ready = plane_sum(pieces, part, after=[done])
     d_gate, d_up, last = gradients([back0, beside, across], dg, du, after=[ready[0]])

time: 102 us -> 97.3 us (0.954)
  waiting for transfers between devices: 33 us -> 19.4 us
  starting transfers between devices: 38.6 us -> 47.9 us
    ppermute x13, waiting for transfers between devices: 21.8 us -> 10.1 us  [over_row(): return lax.ppermute(x, 'row', [(i, i ^ t) for i in senders])]
    ppermute x13, starting transfers between devices: 18.5 us -> 28.2 us  [over_row(): return lax.ppermute(x, 'row', [(i, i ^ t) for i in senders])]
    ppermute x9, waiting for transfers between devices: 6.83 us -> 3.53 us  [over_chips(): return lax.ppermute(x, 'col', [(j, j ^ 2 * u) for j in range(2 * chips)])]
    ppermute x6 -> x5, waiting for transfers between devices: 0.02 us -> 1.4 us  [over_core(): return lax.ppermute(x, 'col', [(j, j ^ 1) for j in range(2 * chips)])]
    pallas_call x16 -> x17, Pallas kernels: 13.5 us -> 13.6 us  [call(): pl.pallas_call(body, in_specs=(specs or [VMEM] * n) + [pl.BlockSpec(memor...]
  transfers between devices with their start and end apart: 32 -> 31, of which waited for: 12 -> 16; matrix products, arithmetic and copies ran while one was open for 0% -> 0% of each run, Pallas kernels for 27% -> 28%
where the time goes in v4:
time: 97.3 us; the launch traced here: 96.9 us
  starting transfers between devices  47.9 us (49%)
  Pallas kernels  28.7 us (29%)
  waiting for transfers between devices  19.4 us (20%)
    ppermute x13, starting transfers between devices, over_row(): return lax.ppermute(x, 'row', [(i, i ^ t) for i in senders])  28.2 us
    pallas_call x17, Pallas kernels, call(): pl.pallas_call(body, in_specs=(specs or [VMEM] * n) + [pl.BlockSpec(memor...  13.6 us
    ppermute x9, starting transfers between devices, over_chips(): return lax.ppermute(x, 'col', [(j, j ^ 2 * u) for j in range(2 * chips)])  10.8 us
    ppermute x13, waiting for transfers between devices, over_row(): return lax.ppermute(x, 'row', [(i, i ^ t) for i in senders])  10.1 us
    pallas_call x2, Pallas kernels, down_gradient(): pl.pallas_call(kernel, grid=(2,), in_specs=[pl.BlockSpec((tokens, step),...  8.28 us
    ppermute x4, starting transfers between devices, fast_body(): lax.ppermute(ready[k], ('row', 'col'), [(r * width + 2 * a + h, (a ^ k) *...  8.17 us
    pallas_call x2, Pallas kernels, masked_weight(): pl.pallas_call(kernel, in_specs=[ANY, VMEM] + [VMEM] * len(extra) + [ANY]...  4.52 us
    ppermute x4, waiting for transfers between devices, fast_body(): lax.ppermute(ready[k], ('row', 'col'), [(r * width + 2 * a + h, (a ^ k) *...  4.34 us
  transfers between devices with their start and end apart: 31, of which 16 were waited for; matrix products, arithmetic and copies ran while one was open for 0% of the time, Pallas kernels for 28%

profile of v4, /device:TPU:16, one launch (start us, length us, event | category | flops | bytes accessed | tf_op | source)
XLA Modules:
  0.0 96.9 jit_solution(7810633492368685887)
XLA Ops:
  1.6 1.6 %collective-permute-start = (bf16[32,1024]{1,0:T(8,128)(2,1)S(1)}, bf16[32,1024]{1,0:T(8,128)(2,1)S(1)}, u32[]{:S(2)}, u32[]{:S(2)}) collective-permute-start(bf16[32,1024]{1,0:T(8,128)(2,1)S(1)} %get-tuple-element.46), channel_id=1, source_target_pairs={{0,2},{1,3},{2,0},{3,1},{4,6},{5,7},{6,4},{7,5},{8,10},{9,11},{10,... | collective-permute-start | bytes 196616 | tf_op jit(solution)/shard_map/ppermute | solution.py:466
  3.2 1.5 %collective-permute-start.1 = (bf16[32,1024]{1,0:T(8,128)(2,1)S(1)}, bf16[32,1024]{1,0:T(8,128)(2,1)S(1)}, u32[]{:S(2)}, u32[]{:S(2)}) collective-permute-start(bf16[32,1024]{1,0:T(8,128)(2,1)S(1)} %get-tuple-element.47), channel_id=1, source_target_pairs={{0,4},{1,5},{2,6},{3,7},{4,0},{5,1},{6,2},{7,3},{8,12},{9,13},{10,... | collective-permute-start | bytes 196616 | tf_op jit(solution)/shard_map/ppermute | solution.py:466
  5.2 1.8 %gated.1 = (bf16[128,2048]{1,0:T(8,128)(2,1)S(1)}, f32[128,2048]{1,0:T(8,128)S(1)}, f32[128,2048]{1,0:T(8,128)S(1)}, s32[16,2048]{1,0:T(8,128)S(1)}) custom-call(bf16[128,2048]{1,0:T(8,128)(2,1)} %refs_0_.3, bf16[128,2048]{1,0:T(8,128)(2,1)} %refs_1_.1, s32[16,16]{1,0:T(8,128)} %refs_2_.1, bf16[32,1024]{1,0:T(8,128)(2,1)S(1)} %get-tuple-element.44.refs_3_.refs_0_), custom_call_target="tpu_custom_call" | custom-call | flops 588284992 | tf_op jit(solution)/shard_map/gated/pallas_call | solution.py:40
  6.9 2.3 %masked_weight.2.refs_4_.refs_0_ = bf16[2048,2048]{1,0:T(8,128)(2,1)S(1)} custom-call(bf16[2048,2048]{1,0:T(8,128)(2,1)} %w_ref.3, s32[16,2048]{1,0:T(8,128)S(1)} %get-tuple-element.49.m_ref.refs_4_, bf16[128,2048]{1,0:T(8,128)(2,1)S(1)} %get-tuple-element.45.refs_0_), custom_call_target="tpu_custom_call" | custom-call | flops 761310016 | tf_op jit(solution)/shard_map/masked_weight/pallas_call | solution.py:73
  9.9 1.6 %collective-permute-start.3 = (bf16[32,1024]{1,0:T(8,128)(2,1)S(1)}, bf16[32,1024]{1,0:T(8,128)(2,1)S(1)}, u32[]{:S(2)}, u32[]{:S(2)}) collective-permute-start(bf16[32,1024]{1,0:T(8,128)(2,1)S(1)} %get-tuple-element.51), channel_id=1, source_target_pairs={{0,8},{8,0},{16,24},{24,16},{1,9},{9,1},{17,25},{25,17},{2,10},{10... | collective-permute-start | bytes 196616 | tf_op jit(solution)/shard_map/ppermute | solution.py:463
  11.9 1.6 %collective-permute-start.5 = (bf16[32,1024]{1,0:T(8,128)(2,1)S(1)}, bf16[32,1024]{1,0:T(8,128)(2,1)S(1)}, u32[]{:S(2)}, u32[]{:S(2)}) collective-permute-start(bf16[32,1024]{1,0:T(8,128)(2,1)S(1)} %get-tuple-element.53.refs_1_), channel_id=1, source_target_pairs={{0,24},{8,16},{16,8},{24,0},{1,25},{9,17},{17,9},{25,1},{2,26},{10... | collective-permute-start | bytes 196616 | tf_op jit(solution)/shard_map/ppermute | solution.py:463
  13.5 2.3 %masked_weight.3.refs_4_.refs_6_.refs_2_.refs_1_.refs_3_ = bf16[2048,2048]{1,0:T(8,128)(2,1)S(1)} custom-call(bf16[2048,2048]{1,0:T(8,128)(2,1)} %w_ref.3, s32[16,2048]{1,0:T(8,128)S(1)} %get-tuple-element.49.m_ref.refs_4_, bf16[2048,2048]{1,0:T(8,128)(2,1)S(1)} %masked_weight.2.refs_4_.refs_0_, ...), custom_call_target="tpu_custom_call", output_to_operand_aliasing={{}: (2, {})} | custom-call | flops 761310016 | tf_op jit(solution)/shard_map/masked_weight/pallas_call | solution.py:73
  16.8 1.3 %collective-permute-done.5.refs_3_ = bf16[32,1024]{1,0:T(8,128)(2,1)S(1)} collective-permute-done((bf16[32,1024]{1,0:T(8,128)(2,1)S(1)}, bf16[32,1024]{1,0:T(8,128)(2,1)S(1)}, u32[]{:S(2)}, u32[]{:S(2)}) %collective-permute-start.5) | collective-permute-done | bytes 65568 | tf_op jit(solution)/shard_map/ppermute | solution.py:463
  18.1 2.2 %collective-permute-start.9 = (bf16[128,1024]{1,0:T(8,128)(2,1)S(1)}, bf16[128,1024]{1,0:T(8,128)(2,1)S(1)}, u32[]{:S(2)}, u32[]{:S(2)}) collective-permute-start(bf16[128,1024]{1,0:T(8,128)(2,1)S(1)} %stack.3.refs_1_.refs_0_), channel_id=1, source_target_pairs={{0,6},{1,7},{2,4},{3,5},{4,2},{5,3},{6,0},{7,1},{8,14},{9,15},{10,... | collective-permute-start | bytes 786440 | tf_op jit(solution)/shard_map/ppermute | solution.py:466
  22.7 4.0 %collective-permute-start.12 = (bf16[128,2048]{1,0:T(8,128)(2,1)S(1)}, bf16[128,2048]{1,0:T(8,128)(2,1)S(1)}, u32[]{:S(2)}, u32[]{:S(2)}) collective-permute-start(bf16[128,2048]{1,0:T(8,128)(2,1)S(1)} %add_and_pass.5.refs_0_), channel_id=1, source_target_pairs={{8,16},{16,8},{9,17},{17,9},{10,18},{18,10},{11,19},{19,11},{12,20... | collective-permute-start | bytes 1572872 | tf_op jit(solution)/shard_map/ppermute | solution.py:463
  28.0 1.5 %collective-permute-done.8.refs_1_.refs_2_ = bf16[128,1024]{1,0:T(8,128)(2,1)S(1)} collective-permute-done((bf16[128,1024]{1,0:T(8,128)(2,1)S(1)}, bf16[128,1024]{1,0:T(8,128)(2,1)S(1)}, u32[]{:S(2)}, u32[]{:S(2)}) %collective-permute-start.8) | collective-permute-done | bytes 262176 | tf_op jit(solution)/shard_map/ppermute | solution.py:466
  30.8 3.5 %collective-permute-start.13 = (bf16[128,2048]{1,0:T(8,128)(2,1)S(1)}, bf16[128,2048]{1,0:T(8,128)(2,1)S(1)}, u32[]{:S(2)}, u32[]{:S(2)}) collective-permute-start(bf16[128,2048]{1,0:T(8,128)(2,1)S(1)} %collective-permute-done.6.refs_7_.refs_1_), channel_id=1, source_target_pairs={{8,16},{16,8},{9,17},{17,9},{10,18},{18,10},{11,19},{19,11},{12,20... | collective-permute-start | bytes 1572872 | tf_op jit(solution)/shard_map/ppermute | solution.py:463
  35.2 1.3 %collective-permute-start.14 = (bf16[128,2048]{1,0:T(8,128)(2,1)S(1)}, bf16[128,2048]{1,0:T(8,128)(2,1)S(1)}, u32[]{:S(2)}, u32[]{:S(2)}) collective-permute-start(bf16[128,2048]{1,0:T(8,128)(2,1)S(1)} %collective-permute-done.12.refs_8_.refs_1_), channel_id=1, source_target_pairs={{8,0},{16,24},{9,1},{17,25},{10,2},{18,26},{11,3},{19,27},{12,4},{... | collective-permute-start | bytes 1572872 | tf_op jit(solution)/shard_map/ppermute | solution.py:463
  36.6 2.5 %back_product.1 = (bf16[512,2048]{1,0:T(8,128)(2,1)S(1)}, bf16[128,2048]{1,0:T(8,128)(2,1)S(1)}, bf16[128,2048]{1,0:T(8,128)(2,1)S(1)}) custom-call(bf16[128,1024]{1,0:T(8,128)(2,1)S(1)} %stack.3.refs_1_.refs_0_, bf16[128,1024]{1,0:T(8,128)(2,1)S(1)} %collective-permute-done.7.refs_0_.refs_1_, bf16[128,1024]{1,0:T(8,128)(2,1)S(1)} %collective-permute-done.8.refs_1_.refs_2_, ...), custom_call_target="tpu_custom_call" | custom-call | flops 865124992 | tf_op jit(solution)/shard_map/back_product/pallas_call | solution.py:40
  39.1 1.3 %collective-permute-start.16 = (bf16[128,2048]{1,0:T(8,128)(2,1)S(1)}, bf16[128,2048]{1,0:T(8,128)(2,1)S(1)}, u32[]{:S(2)}, u32[]{:S(2)}) collective-permute-start(bf16[128,2048]{1,0:T(8,128)(2,1)S(1)} %get-tuple-element.54.refs_3_.refs_0_), channel_id=1, source_target_pairs={{0,8},{24,16},{1,9},{25,17},{2,10},{26,18},{3,11},{27,19},{4,12},{... | collective-permute-start | bytes 1572872 | tf_op jit(solution)/shard_map/ppermute | solution.py:463
  40.4 2.4 %out_product.2 = (bf16[256,1024]{1,0:T(8,128)(2,1)S(1)}, f32[256,1024]{1,0:T(8,128)S(1)}) custom-call(bf16[128,2048]{1,0:T(8,128)(2,1)S(1)} %add_and_pass.5.refs_0_, bf16[128,2048]{1,0:T(8,128)(2,1)S(1)} %collective-permute-done.6.refs_7_.refs_1_, bf16[2048,2048]{1,0:T(8,128)(2,1)S(1)} %masked_weight.3.refs_4_.refs_6_.refs_2_.refs_1_.refs_3_, ...), custom_call_target="tpu_custom_call" | custom-call | flops 830520000 | tf_op jit(solution)/shard_map/out_product/pallas_call | solution.py:40
  42.8 2.4 %back_rest.1 = (bf16[128,2048]{1,0:T(8,128)(2,1)S(1)}, bf16[128,2048]{1,0:T(8,128)(2,1)S(1)}) custom-call(bf16[512,2048]{1,0:T(8,128)(2,1)S(1)} %get-tuple-element.56.refs_0_.c_ref, bf16[2048,2048]{1,0:T(8,128)(2,1)S(1)} %masked_weight.3.refs_4_.refs_6_.refs_2_.refs_1_.refs_3_, f32[256,1024]{1,0:T(8,128)S(1)} %get-tuple-element.55.refs_2_.refs_0_), custom_call_target="tpu_custom_call" | custom-call | flops 830520000 | tf_op jit(solution)/shard_map/back_rest/pallas_call | solution.py:40
  46.3 3.5 %collective-permute-start.15 = (bf16[128,2048]{1,0:T(8,128)(2,1)S(1)}, bf16[128,2048]{1,0:T(8,128)(2,1)S(1)}, u32[]{:S(2)}, u32[]{:S(2)}) collective-permute-start(bf16[128,2048]{1,0:T(8,128)(2,1)S(1)} %add_and_pass.6.refs_0_.refs_2_), channel_id=1, source_target_pairs={{8,0},{16,24},{9,1},{17,25},{10,2},{18,26},{11,3},{19,27},{12,4},{... | collective-permute-start | bytes 1572872 | tf_op jit(solution)/shard_map/ppermute | solution.py:463
  49.9 1.3 %collective-permute-start.23 = (bf16[128,2048]{1,0:T(8,128)(2,1)S(1)}, bf16[128,2048]{1,0:T(8,128)(2,1)S(1)}, u32[]{:S(2)}, u32[]{:S(2)}) collective-permute-start(bf16[128,2048]{1,0:T(8,128)(2,1)S(1)} %get-tuple-element.58.refs_0_), channel_id=1, source_target_pairs={{0,8},{24,16},{1,9},{25,17},{2,10},{26,18},{3,11},{27,19},{4,12},{... | collective-permute-start | bytes 1572872 | tf_op jit(solution)/shard_map/ppermute | solution.py:463
  51.4 2.4 %collective-permute-done.16.refs_1_ = bf16[128,2048]{1,0:T(8,128)(2,1)S(1)} collective-permute-done((bf16[128,2048]{1,0:T(8,128)(2,1)S(1)}, bf16[128,2048]{1,0:T(8,128)(2,1)S(1)}, u32[]{:S(2)}, u32[]{:S(2)}) %collective-permute-start.16) | collective-permute-done | bytes 524320 | tf_op jit(solution)/shard_map/ppermute | solution.py:463
  53.9 3.8 %collective-permute-start.24 = (bf16[128,2048]{1,0:T(8,128)(2,1)S(1)}, bf16[128,2048]{1,0:T(8,128)(2,1)S(1)}, u32[]{:S(2)}, u32[]{:S(2)}) collective-permute-start(bf16[128,2048]{1,0:T(8,128)(2,1)S(1)} %add_and_pass.8.refs_4_), channel_id=1, source_target_pairs={{8,16},{16,8},{9,17},{17,9},{10,18},{18,10},{11,19},{19,11},{12,20... | collective-permute-start | bytes 1572872 | tf_op jit(solution)/shard_map/ppermute | solution.py:463
  58.9 2.4 %out_product.3 = (bf16[256,512]{1,0:T(8,128)(2,1)S(1)}, bf16[256,512]{1,0:T(8,128)(2,1)S(1)}, f32[256,1024]{1,0:T(8,128)S(1)}, bf16[128,2048]{1,0:T(8,128)(2,1)S(1)}) custom-call(bf16[128,2048]{1,0:T(8,128)(2,1)S(1)} %add_and_pass.7.refs_2_.refs_0_, bf16[128,2048]{1,0:T(8,128)(2,1)S(1)} %collective-permute-done.12.refs_8_.refs_1_, ...), custom_call_target="tpu_custom_call" | custom-call | flops 830520000 | tf_op jit(solution)/shard_map/out_product/pallas_call | solution.py:40
  63.5 1.3 %collective-permute-start.20 = (bf16[128,1024]{1,0:T(8,128)(2,1)S(1)}, bf16[128,1024]{1,0:T(8,128)(2,1)S(1)}, u32[]{:S(2)}, u32[]{:S(2)}) collective-permute-start(bf16[128,1024]{1,0:T(8,128)(2,1)S(1)} %get-tuple-element.64), channel_id=1, source_target_pairs={{0,2},{1,3},{2,0},{3,1},{4,6},{5,7},{6,4},{7,5},{8,10},{9,11},{10,... | collective-permute-start | bytes 786440 | tf_op jit(solution)/shard_map/ppermute | solution.py:466
  64.8 1.3 %collective-permute-start.21 = (bf16[128,1024]{1,0:T(8,128)(2,1)S(1)}, bf16[128,1024]{1,0:T(8,128)(2,1)S(1)}, u32[]{:S(2)}, u32[]{:S(2)}) collective-permute-start(bf16[128,1024]{1,0:T(8,128)(2,1)S(1)} %get-tuple-element.65), channel_id=1, source_target_pairs={{0,4},{1,5},{2,6},{3,7},{4,0},{5,1},{6,2},{7,3},{8,12},{9,13},{10,... | collective-permute-start | bytes 786440 | tf_op jit(solution)/shard_map/ppermute | solution.py:466
  68.4 1.5 %collective-permute-start.29 = (bf16[128,2048]{1,0:T(8,128)(2,1)S(1)}, bf16[128,2048]{1,0:T(8,128)(2,1)S(1)}, u32[]{:S(2)}, u32[]{:S(2)}) collective-permute-start(bf16[128,2048]{1,0:T(8,128)(2,1)S(1)} %get-tuple-element.77), channel_id=1, source_target_pairs={{0,8},{8,0},{16,24},{24,16},{1,9},{9,1},{17,25},{25,17},{2,10},{10... | collective-permute-start | bytes 1572872 | tf_op jit(solution)/shard_map/ppermute | solution.py:463
  69.9 3.6 %collective-permute-start.30 = (bf16[128,2048]{1,0:T(8,128)(2,1)S(1)}, bf16[128,2048]{1,0:T(8,128)(2,1)S(1)}, u32[]{:S(2)}, u32[]{:S(2)}) collective-permute-start(bf16[128,2048]{1,0:T(8,128)(2,1)S(1)} %get-tuple-element.68.refs_5_), channel_id=1, source_target_pairs={{8,16},{16,8},{9,17},{17,9},{10,18},{18,10},{11,19},{19,11},{12,20... | collective-permute-start | bytes 1572872 | tf_op jit(solution)/shard_map/ppermute | solution.py:463
  73.5 4.1 %down_gradient.2 = (bf16[2048,2048]{1,0:T(8,128)(2,1)}, bf16[16,128]{1,0:T(8,128)(2,1)S(1)}) custom-call(bf16[512,2048]{1,0:T(8,128)(2,1)S(1)} %get-tuple-element.56.refs_0_.c_ref, bf16[128,2048]{1,0:T(8,128)(2,1)S(1)} %add_and_pass.5.refs_0_, bf16[128,2048]{1,0:T(8,128)(2,1)S(1)} %collective-permute-done.6.refs_7_.refs_1_, ...), custom_call_target="tpu_custom_call" | custom-call | flops 1418804992 | tf_op jit(solution)/shard_map/down_gradient/pallas_call | solution.py:441
  77.7 4.1 %down_gradient.3 = (bf16[2048,2048]{1,0:T(8,128)(2,1)}, bf16[16,128]{1,0:T(8,128)(2,1)S(1)}) custom-call(bf16[512,2048]{1,0:T(8,128)(2,1)S(1)} %get-tuple-element.56.refs_0_.c_ref, bf16[128,2048]{1,0:T(8,128)(2,1)S(1)} %add_and_pass.5.refs_0_, bf16[128,2048]{1,0:T(8,128)(2,1)S(1)} %collective-permute-done.6.refs_7_.refs_1_, ...), custom_call_target="tpu_custom_call", output_to_operand_aliasing={{0}: (6, {})} | custom-call | flops 1418804992 | tf_op jit(solution)/shard_map/down_gradient/pallas_call | solution.py:441
  83.1 5.2 %collective-permute-start.28 = (bf16[32,1024]{1,0:T(8,128)(2,1)S(1)}, bf16[32,1024]{1,0:T(8,128)(2,1)S(1)}, u32[]{:S(2)}, u32[]{:S(2)}) collective-permute-start(bf16[32,1024]{1,0:T(8,128)(2,1)S(1)} %get-tuple-element.75), channel_id=1, source_target_pairs={{0,24},{1,25},{2,16},{3,17},{4,8},{5,9},{6,0},{7,1},{8,26},{9,27},... | collective-permute-start | bytes 196616 | tf_op jit(solution)/shard_map/ppermute | solution.py:523
  88.3 1.9 %collective-permute-start.25 = (bf16[32,1024]{1,0:T(8,128)(2,1)S(1)}, bf16[32,1024]{1,0:T(8,128)(2,1)S(1)}, u32[]{:S(2)}, u32[]{:S(2)}) collective-permute-start(bf16[32,1024]{1,0:T(8,128)(2,1)S(1)} %get-tuple-element.72.refs_5_), channel_id=1, source_target_pairs={{0,0},{1,1},{2,8},{3,9},{4,16},{5,17},{6,24},{7,25},{8,2},{9,3},{1... | collective-permute-start | bytes 196616 | tf_op jit(solution)/shard_map/ppermute | solution.py:523
  90.2 1.6 %gradients.1 = (bf16[128,2048]{1,0:T(8,128)(2,1)}, bf16[128,2048]{1,0:T(8,128)(2,1)}, bf16[16,128]{1,0:T(8,128)(2,1)S(1)}) custom-call(bf16[128,2048]{1,0:T(8,128)(2,1)S(1)} %get-tuple-element.76.refs_0_, bf16[128,2048]{1,0:T(8,128)(2,1)S(1)} %collective-permute-done.29.refs_1_, bf16[128,2048]{1,0:T(8,128)(2,1)S(1)} %collective-permute-done.30.refs_2_, ...), custom_call_target="tpu_custom_call" | custom-call | flops 588284992 | tf_op jit(solution)/shard_map/gradients/pallas_call | solution.py:148
  92.1 4.1 %collective-permute-done.25.refs_0_ = bf16[32,1024]{1,0:T(8,128)(2,1)S(1)} collective-permute-done((bf16[32,1024]{1,0:T(8,128)(2,1)S(1)}, bf16[32,1024]{1,0:T(8,128)(2,1)S(1)}, u32[]{:S(2)}, u32[]{:S(2)}) %collective-permute-start.25) | collective-permute-done | bytes 65568 | tf_op jit(solution)/shard_map/ppermute | solution.py:523
  (53 shorter events, 18.9 us)
Async XLA Ops:
  1.6 7.6 %collective-permute-start = (bf16[32,1024]{1,0:T(8,128)(2,1)S(1)}, bf16[32,1024]{1,0:T(8,128)(2,1)S(1)}, u32[]{:S(2)}, u32[]{:S(2)}) collective-permute-start(bf16[32,1024]{1,0:T(8,128)(2,1)S(1)} %get-tuple-element.46), channel_id=1, source_target_pairs={{0,2},{1,3},{2,0},{3,1},{4,6},{5,7},{6,4},{7,5},{8,10},{9,11},{10,... | collective-permute-start | bytes 196616 | tf_op jit(solution)/shard_map/ppermute | solution.py:466
  3.2 6.0 %collective-permute-start.1 = (bf16[32,1024]{1,0:T(8,128)(2,1)S(1)}, bf16[32,1024]{1,0:T(8,128)(2,1)S(1)}, u32[]{:S(2)}, u32[]{:S(2)}) collective-permute-start(bf16[32,1024]{1,0:T(8,128)(2,1)S(1)} %get-tuple-element.47), channel_id=1, source_target_pairs={{0,4},{1,5},{2,6},{3,7},{4,0},{5,1},{6,2},{7,3},{8,12},{9,13},{10,... | collective-permute-start | bytes 196616 | tf_op jit(solution)/shard_map/ppermute | solution.py:466
  4.7 5.2 %collective-permute-start.2 = (bf16[32,1024]{1,0:T(8,128)(2,1)S(1)}, bf16[32,1024]{1,0:T(8,128)(2,1)S(1)}, u32[]{:S(2)}, u32[]{:S(2)}) collective-permute-start(bf16[32,1024]{1,0:T(8,128)(2,1)S(1)} %get-tuple-element.48), channel_id=1, source_target_pairs={{0,6},{1,7},{2,4},{3,5},{4,2},{5,3},{6,0},{7,1},{8,14},{9,15},{10,... | collective-permute-start | bytes 196616 | tf_op jit(solution)/shard_map/ppermute | solution.py:466
  9.9 5.8 %collective-permute-start.3 = (bf16[32,1024]{1,0:T(8,128)(2,1)S(1)}, bf16[32,1024]{1,0:T(8,128)(2,1)S(1)}, u32[]{:S(2)}, u32[]{:S(2)}) collective-permute-start(bf16[32,1024]{1,0:T(8,128)(2,1)S(1)} %get-tuple-element.51), channel_id=1, source_target_pairs={{0,8},{8,0},{16,24},{24,16},{1,9},{9,1},{17,25},{25,17},{2,10},{10... | collective-permute-start | bytes 196616 | tf_op jit(solution)/shard_map/ppermute | solution.py:463
  11.6 5.3 %collective-permute-start.4 = (bf16[32,1024]{1,0:T(8,128)(2,1)S(1)}, bf16[32,1024]{1,0:T(8,128)(2,1)S(1)}, u32[]{:S(2)}, u32[]{:S(2)}) collective-permute-start(bf16[32,1024]{1,0:T(8,128)(2,1)S(1)} %get-tuple-element.52), channel_id=1, source_target_pairs={{0,16},{8,24},{16,0},{24,8},{1,17},{9,25},{17,1},{25,9},{2,18},{10... | collective-permute-start | bytes 196616 | tf_op jit(solution)/shard_map/ppermute | solution.py:463
  11.9 6.2 %collective-permute-start.5 = (bf16[32,1024]{1,0:T(8,128)(2,1)S(1)}, bf16[32,1024]{1,0:T(8,128)(2,1)S(1)}, u32[]{:S(2)}, u32[]{:S(2)}) collective-permute-start(bf16[32,1024]{1,0:T(8,128)(2,1)S(1)} %get-tuple-element.53.refs_1_), channel_id=1, source_target_pairs={{0,24},{8,16},{16,8},{24,0},{1,25},{9,17},{17,9},{25,1},{2,26},{10... | collective-permute-start | bytes 196616 | tf_op jit(solution)/shard_map/ppermute | solution.py:463
  18.1 9.7 %collective-permute-start.9 = (bf16[128,1024]{1,0:T(8,128)(2,1)S(1)}, bf16[128,1024]{1,0:T(8,128)(2,1)S(1)}, u32[]{:S(2)}, u32[]{:S(2)}) collective-permute-start(bf16[128,1024]{1,0:T(8,128)(2,1)S(1)} %stack.3.refs_1_.refs_0_), channel_id=1, source_target_pairs={{0,6},{1,7},{2,4},{3,5},{4,2},{5,3},{6,0},{7,1},{8,14},{9,15},{10,... | collective-permute-start | bytes 786440 | tf_op jit(solution)/shard_map/ppermute | solution.py:466
  20.4 10.4 %collective-permute-start.6 = (bf16[128,2048]{1,0:T(8,128)(2,1)S(1)}, bf16[128,2048]{1,0:T(8,128)(2,1)S(1)}, u32[]{:S(2)}, u32[]{:S(2)}) collective-permute-start(bf16[128,2048]{1,0:T(8,128)(2,1)S(1)} %add_and_pass.5.refs_0_), channel_id=1, source_target_pairs={{0,8},{8,0},{16,24},{24,16},{1,9},{9,1},{17,25},{25,17},{2,10},{10... | collective-permute-start | bytes 1572872 | tf_op jit(solution)/shard_map/ppermute | solution.py:463
  21.2 8.2 %collective-permute-start.8 = (bf16[128,1024]{1,0:T(8,128)(2,1)S(1)}, bf16[128,1024]{1,0:T(8,128)(2,1)S(1)}, u32[]{:S(2)}, u32[]{:S(2)}) collective-permute-start(bf16[128,1024]{1,0:T(8,128)(2,1)S(1)} %stack.3.refs_1_.refs_0_), channel_id=1, source_target_pairs={{0,4},{1,5},{2,6},{3,7},{4,0},{5,1},{6,2},{7,3},{8,12},{9,13},{10,... | collective-permute-start | bytes 786440 | tf_op jit(solution)/shard_map/ppermute | solution.py:466
  21.7 8.0 %collective-permute-start.7 = (bf16[128,1024]{1,0:T(8,128)(2,1)S(1)}, bf16[128,1024]{1,0:T(8,128)(2,1)S(1)}, u32[]{:S(2)}, u32[]{:S(2)}) collective-permute-start(bf16[128,1024]{1,0:T(8,128)(2,1)S(1)} %stack.3.refs_1_.refs_0_), channel_id=1, source_target_pairs={{0,2},{1,3},{2,0},{3,1},{4,6},{5,7},{6,4},{7,5},{8,10},{9,11},{10,... | collective-permute-start | bytes 786440 | tf_op jit(solution)/shard_map/ppermute | solution.py:466
  22.7 12.6 %collective-permute-start.12 = (bf16[128,2048]{1,0:T(8,128)(2,1)S(1)}, bf16[128,2048]{1,0:T(8,128)(2,1)S(1)}, u32[]{:S(2)}, u32[]{:S(2)}) collective-permute-start(bf16[128,2048]{1,0:T(8,128)(2,1)S(1)} %add_and_pass.5.refs_0_), channel_id=1, source_target_pairs={{8,16},{16,8},{9,17},{17,9},{10,18},{18,10},{11,19},{19,11},{12,20... | collective-permute-start | bytes 1572872 | tf_op jit(solution)/shard_map/ppermute | solution.py:463
  27.9 8.7 %collective-permute-start.10 = (bf16[256,1024]{1,0:T(8,128)(2,1)S(1)}, bf16[256,1024]{1,0:T(8,128)(2,1)S(1)}, u32[]{:S(2)}, u32[]{:S(2)}) collective-permute-start(bf16[256,1024]{1,0:T(8,128)(2,1)S(1)} %stack.4), channel_id=1, source_target_pairs={{0,1},{1,0},{2,3},{3,2},{4,5},{5,4},{6,7},{7,6},{8,9},{9,8},{10,11... | collective-permute-start | bytes 1572872 | tf_op jit(solution)/shard_map/ppermute | solution.py:469
  29.7 6.8 %collective-permute-start.11 = (bf16[256,1024]{1,0:T(8,128)(2,1)S(1)}, bf16[256,1024]{1,0:T(8,128)(2,1)S(1)}, u32[]{:S(2)}, u32[]{:S(2)}) collective-permute-start(bf16[256,1024]{1,0:T(8,128)(2,1)S(1)} %stack.5), channel_id=1, source_target_pairs={{0,1},{1,0},{2,3},{3,2},{4,5},{5,4},{6,7},{7,6},{8,9},{9,8},{10,11... | collective-permute-start | bytes 1572872 | tf_op jit(solution)/shard_map/ppermute | solution.py:469
  30.8 15.5 %collective-permute-start.13 = (bf16[128,2048]{1,0:T(8,128)(2,1)S(1)}, bf16[128,2048]{1,0:T(8,128)(2,1)S(1)}, u32[]{:S(2)}, u32[]{:S(2)}) collective-permute-start(bf16[128,2048]{1,0:T(8,128)(2,1)S(1)} %collective-permute-done.6.refs_7_.refs_1_), channel_id=1, source_target_pairs={{8,16},{16,8},{9,17},{17,9},{10,18},{18,10},{11,19},{19,11},{12,20... | collective-permute-start | bytes 1572872 | tf_op jit(solution)/shard_map/ppermute | solution.py:463
  35.2 16.0 %collective-permute-start.14 = (bf16[128,2048]{1,0:T(8,128)(2,1)S(1)}, bf16[128,2048]{1,0:T(8,128)(2,1)S(1)}, u32[]{:S(2)}, u32[]{:S(2)}) collective-permute-start(bf16[128,2048]{1,0:T(8,128)(2,1)S(1)} %collective-permute-done.12.refs_8_.refs_1_), channel_id=1, source_target_pairs={{8,0},{16,24},{9,1},{17,25},{10,2},{18,26},{11,3},{19,27},{12,4},{... | collective-permute-start | bytes 1572872 | tf_op jit(solution)/shard_map/ppermute | solution.py:463
  39.1 14.7 %collective-permute-start.16 = (bf16[128,2048]{1,0:T(8,128)(2,1)S(1)}, bf16[128,2048]{1,0:T(8,128)(2,1)S(1)}, u32[]{:S(2)}, u32[]{:S(2)}) collective-permute-start(bf16[128,2048]{1,0:T(8,128)(2,1)S(1)} %get-tuple-element.54.refs_3_.refs_0_), channel_id=1, source_target_pairs={{0,8},{24,16},{1,9},{25,17},{2,10},{26,18},{3,11},{27,19},{4,12},{... | collective-permute-start | bytes 1572872 | tf_op jit(solution)/shard_map/ppermute | solution.py:463
  46.3 12.6 %collective-permute-start.15 = (bf16[128,2048]{1,0:T(8,128)(2,1)S(1)}, bf16[128,2048]{1,0:T(8,128)(2,1)S(1)}, u32[]{:S(2)}, u32[]{:S(2)}) collective-permute-start(bf16[128,2048]{1,0:T(8,128)(2,1)S(1)} %add_and_pass.6.refs_0_.refs_2_), channel_id=1, source_target_pairs={{8,0},{16,24},{9,1},{17,25},{10,2},{18,26},{11,3},{19,27},{12,4},{... | collective-permute-start | bytes 1572872 | tf_op jit(solution)/shard_map/ppermute | solution.py:463
  49.9 17.2 %collective-permute-start.23 = (bf16[128,2048]{1,0:T(8,128)(2,1)S(1)}, bf16[128,2048]{1,0:T(8,128)(2,1)S(1)}, u32[]{:S(2)}, u32[]{:S(2)}) collective-permute-start(bf16[128,2048]{1,0:T(8,128)(2,1)S(1)} %get-tuple-element.58.refs_0_), channel_id=1, source_target_pairs={{0,8},{24,16},{1,9},{25,17},{2,10},{26,18},{3,11},{27,19},{4,12},{... | collective-permute-start | bytes 1572872 | tf_op jit(solution)/shard_map/ppermute | solution.py:463
  51.2 10.7 %collective-permute-start.17 = (bf16[256,1024]{1,0:T(8,128)(2,1)S(1)}, bf16[256,1024]{1,0:T(8,128)(2,1)S(1)}, u32[]{:S(2)}, u32[]{:S(2)}) collective-permute-start(bf16[256,1024]{1,0:T(8,128)(2,1)S(1)} %get-tuple-element.60), channel_id=1, source_target_pairs={{0,1},{1,0},{2,3},{3,2},{4,5},{5,4},{6,7},{7,6},{8,9},{9,8},{10,11... | collective-permute-start | bytes 1572872 | tf_op jit(solution)/shard_map/ppermute | solution.py:469
  53.9 14.2 %collective-permute-start.24 = (bf16[128,2048]{1,0:T(8,128)(2,1)S(1)}, bf16[128,2048]{1,0:T(8,128)(2,1)S(1)}, u32[]{:S(2)}, u32[]{:S(2)}) collective-permute-start(bf16[128,2048]{1,0:T(8,128)(2,1)S(1)} %add_and_pass.8.refs_4_), channel_id=1, source_target_pairs={{8,16},{16,8},{9,17},{17,9},{10,18},{18,10},{11,19},{19,11},{12,20... | collective-permute-start | bytes 1572872 | tf_op jit(solution)/shard_map/ppermute | solution.py:463
  61.3 1.6 %collective-permute-start.18 = (bf16[256,512]{1,0:T(8,128)(2,1)S(1)}, bf16[256,512]{1,0:T(8,128)(2,1)S(1)}, u32[]{:S(2)}, u32[]{:S(2)}) collective-permute-start(bf16[256,512]{1,0:T(8,128)(2,1)S(1)} %get-tuple-element.61), channel_id=1, source_target_pairs={{0,1},{1,0},{2,3},{3,2},{4,5},{5,4},{6,7},{7,6},{8,9},{9,8},{10,11... | collective-permute-start | bytes 786440 | tf_op jit(solution)/shard_map/ppermute | solution.py:469
  61.4 1.9 %collective-permute-start.19 = (bf16[256,512]{1,0:T(8,128)(2,1)S(1)}, bf16[256,512]{1,0:T(8,128)(2,1)S(1)}, u32[]{:S(2)}, u32[]{:S(2)}) collective-permute-start(bf16[256,512]{1,0:T(8,128)(2,1)S(1)} %get-tuple-element.62), channel_id=1, source_target_pairs={{0,1},{1,0},{2,3},{3,2},{4,5},{5,4},{6,7},{7,6},{8,9},{9,8},{10,11... | collective-permute-start | bytes 786440 | tf_op jit(solution)/shard_map/ppermute | solution.py:469
  63.5 18.3 %collective-permute-start.20 = (bf16[128,1024]{1,0:T(8,128)(2,1)S(1)}, bf16[128,1024]{1,0:T(8,128)(2,1)S(1)}, u32[]{:S(2)}, u32[]{:S(2)}) collective-permute-start(bf16[128,1024]{1,0:T(8,128)(2,1)S(1)} %get-tuple-element.64), channel_id=1, source_target_pairs={{0,2},{1,3},{2,0},{3,1},{4,6},{5,7},{6,4},{7,5},{8,10},{9,11},{10,... | collective-permute-start | bytes 786440 | tf_op jit(solution)/shard_map/ppermute | solution.py:466
  64.8 17.0 %collective-permute-start.21 = (bf16[128,1024]{1,0:T(8,128)(2,1)S(1)}, bf16[128,1024]{1,0:T(8,128)(2,1)S(1)}, u32[]{:S(2)}, u32[]{:S(2)}) collective-permute-start(bf16[128,1024]{1,0:T(8,128)(2,1)S(1)} %get-tuple-element.65), channel_id=1, source_target_pairs={{0,4},{1,5},{2,6},{3,7},{4,0},{5,1},{6,2},{7,3},{8,12},{9,13},{10,... | collective-permute-start | bytes 786440 | tf_op jit(solution)/shard_map/ppermute | solution.py:466
  66.0 15.8 %collective-permute-start.22 = (bf16[128,1024]{1,0:T(8,128)(2,1)S(1)}, bf16[128,1024]{1,0:T(8,128)(2,1)S(1)}, u32[]{:S(2)}, u32[]{:S(2)}) collective-permute-start(bf16[128,1024]{1,0:T(8,128)(2,1)S(1)} %get-tuple-element.66), channel_id=1, source_target_pairs={{0,6},{1,7},{2,4},{3,5},{4,2},{5,3},{6,0},{7,1},{8,14},{9,15},{10,... | collective-permute-start | bytes 786440 | tf_op jit(solution)/shard_map/ppermute | solution.py:466
  68.4 19.8 %collective-permute-start.29 = (bf16[128,2048]{1,0:T(8,128)(2,1)S(1)}, bf16[128,2048]{1,0:T(8,128)(2,1)S(1)}, u32[]{:S(2)}, u32[]{:S(2)}) collective-permute-start(bf16[128,2048]{1,0:T(8,128)(2,1)S(1)} %get-tuple-element.77), channel_id=1, source_target_pairs={{0,8},{8,0},{16,24},{24,16},{1,9},{9,1},{17,25},{25,17},{2,10},{10... | collective-permute-start | bytes 1572872 | tf_op jit(solution)/shard_map/ppermute | solution.py:463
  69.9 20.3 %collective-permute-start.30 = (bf16[128,2048]{1,0:T(8,128)(2,1)S(1)}, bf16[128,2048]{1,0:T(8,128)(2,1)S(1)}, u32[]{:S(2)}, u32[]{:S(2)}) collective-permute-start(bf16[128,2048]{1,0:T(8,128)(2,1)S(1)} %get-tuple-element.68.refs_5_), channel_id=1, source_target_pairs={{8,16},{16,8},{9,17},{17,9},{10,18},{18,10},{11,19},{19,11},{12,20... | collective-permute-start | bytes 1572872 | tf_op jit(solution)/shard_map/ppermute | solution.py:463
  82.0 9.8 %collective-permute-start.26 = (bf16[32,1024]{1,0:T(8,128)(2,1)S(1)}, bf16[32,1024]{1,0:T(8,128)(2,1)S(1)}, u32[]{:S(2)}, u32[]{:S(2)}) collective-permute-start(bf16[32,1024]{1,0:T(8,128)(2,1)S(1)} %get-tuple-element.73), channel_id=1, source_target_pairs={{0,8},{1,9},{2,0},{3,1},{4,24},{5,25},{6,16},{7,17},{8,10},{9,11},... | collective-permute-start | bytes 196616 | tf_op jit(solution)/shard_map/ppermute | solution.py:523
  83.0 8.8 %collective-permute-start.27 = (bf16[32,1024]{1,0:T(8,128)(2,1)S(1)}, bf16[32,1024]{1,0:T(8,128)(2,1)S(1)}, u32[]{:S(2)}, u32[]{:S(2)}) collective-permute-start(bf16[32,1024]{1,0:T(8,128)(2,1)S(1)} %get-tuple-element.74), channel_id=1, source_target_pairs={{0,16},{1,17},{2,24},{3,25},{4,0},{5,1},{6,8},{7,9},{8,18},{9,19},... | collective-permute-start | bytes 196616 | tf_op jit(solution)/shard_map/ppermute | solution.py:523
  83.1 9.0 %collective-permute-start.28 = (bf16[32,1024]{1,0:T(8,128)(2,1)S(1)}, bf16[32,1024]{1,0:T(8,128)(2,1)S(1)}, u32[]{:S(2)}, u32[]{:S(2)}) collective-permute-start(bf16[32,1024]{1,0:T(8,128)(2,1)S(1)} %get-tuple-element.75), channel_id=1, source_target_pairs={{0,24},{1,25},{2,16},{3,17},{4,8},{5,9},{6,0},{7,1},{8,26},{9,27},... | collective-permute-start | bytes 196616 | tf_op jit(solution)/shard_map/ppermute | solution.py:523
  88.3 7.9 %collective-permute-start.25 = (bf16[32,1024]{1,0:T(8,128)(2,1)S(1)}, bf16[32,1024]{1,0:T(8,128)(2,1)S(1)}, u32[]{:S(2)}, u32[]{:S(2)}) collective-permute-start(bf16[32,1024]{1,0:T(8,128)(2,1)S(1)} %get-tuple-element.72.refs_5_), channel_id=1, source_target_pairs={{0,0},{1,1},{2,8},{3,9},{4,16},{5,17},{6,24},{7,25},{8,2},{9,3},{1... | collective-permute-start | bytes 196616 | tf_op jit(solution)/shard_map/ppermute | solution.py:523

commit v5 on v4

--- a/solution.py
+++ b/solution.py
@@ -507,13 +507,14 @@
         [hidden[2]], [[inner3, ends3]], weight, 2, after=[to_pass]
     )
     received.append([over_core(x) for x in sent])
+    (to_inner,) = add_and_pass([(back3, first2)], after=[own23])
+    across = over_row(to_inner, 3, inner)
     pieces = pair_sum([own01, own23], received, tok, chips)
     pieces = [pieces[0]] + [over_chips(pieces[u], u) for u in range(1, chips)]
-    to_inner, to_near = add_and_pass([(back3, first2), (back1, second)], after=[pieces[0]])
-    across = over_row(to_inner, 3, inner)
+    (to_near,) = add_and_pass([(back1, second)], after=[pieces[0]])
     beside = over_row(to_near, 1)
     tokens = [hidden[t] for t in range(rows)]
-    d_down, done = down_gradient(cot, tokens, mask_rows, 0, after=[to_inner])
+    d_down, done = down_gradient(cot, tokens, mask_rows, 0, after=[to_near])
     d_down, done = down_gradient(cot, tokens, mask_rows, 1, d_down, after=[done])
     ready = plane_sum(pieces, part, after=[done])
     d_gate, d_up, last = gradients([back0, beside, across], dg, du, after=[ready[0]])

time: 97.3 us -> 96.7 us (level)
  waiting for transfers between devices: 19.4 us -> 18.2 us
    ppermute x13, starting transfers between devices: 28.2 us -> 26.8 us  [over_row(): return lax.ppermute(x, 'row', [(i, i ^ t) for i in senders])]
    ppermute x5, waiting for transfers between devices: 1.4 us -> 0.01 us  [over_core(): return lax.ppermute(x, 'col', [(j, j ^ 1) for j in range(2 * chips)])]
    ppermute x13, waiting for transfers between devices: 10.1 us -> 11.4 us  [over_row(): return lax.ppermute(x, 'row', [(i, i ^ t) for i in senders])]
    ppermute x4, starting transfers between devices: 8.17 us -> 9.45 us  [fast_body(): lax.ppermute(ready[k], ('row', 'col'), [(r * width + 2 * a + h, (a ^ k) *...]
    ppermute x4, waiting for transfers between devices: 4.34 us -> 3.15 us  [fast_body(): lax.ppermute(ready[k], ('row', 'col'), [(r * width + 2 * a + h, (a ^ k) *...]
    pallas_call x17 -> x18, Pallas kernels: 13.6 us -> 13.5 us  [call(): pl.pallas_call(body, in_specs=(specs or [VMEM] * n) + [pl.BlockSpec(memor...]
  transfers between devices with their start and end apart: 31 -> 31, of which waited for: 16 -> 14; matrix products, arithmetic and copies ran while one was open for 0% -> 0% of each run, Pallas kernels for 28% -> 28%
where the time goes in v5:
time: 96.7 us; the launch traced here: 95.7 us
  starting transfers between devices  47.8 us (49%)
  Pallas kernels  28.7 us (30%)
  waiting for transfers between devices  18.2 us (19%)
    ppermute x13, starting transfers between devices, over_row(): return lax.ppermute(x, 'row', [(i, i ^ t) for i in senders])  26.8 us
    pallas_call x18, Pallas kernels, call(): pl.pallas_call(body, in_specs=(specs or [VMEM] * n) + [pl.BlockSpec(memor...  13.5 us
    ppermute x13, waiting for transfers between devices, over_row(): return lax.ppermute(x, 'row', [(i, i ^ t) for i in senders])  11.4 us
    ppermute x9, starting transfers between devices, over_chips(): return lax.ppermute(x, 'col', [(j, j ^ 2 * u) for j in range(2 * chips)])  10.8 us
    ppermute x4, starting transfers between devices, fast_body(): lax.ppermute(ready[k], ('row', 'col'), [(r * width + 2 * a + h, (a ^ k) *...  9.45 us
    pallas_call x2, Pallas kernels, down_gradient(): pl.pallas_call(kernel, grid=(2,), in_specs=[pl.BlockSpec((tokens, step),...  8.28 us
    pallas_call x2, Pallas kernels, masked_weight(): pl.pallas_call(kernel, in_specs=[ANY, VMEM] + [VMEM] * len(extra) + [ANY]...  4.52 us
    ppermute x9, waiting for transfers between devices, over_chips(): return lax.ppermute(x, 'col', [(j, j ^ 2 * u) for j in range(2 * chips)])  3.67 us
  transfers between devices with their start and end apart: 31, of which 14 were waited for; matrix products, arithmetic and copies ran while one was open for 0% of the time, Pallas kernels for 28%

profile of v5, /device:TPU:16, one launch (start us, length us, event | category | flops | bytes accessed | tf_op | source)
XLA Modules:
  0.0 95.7 jit_solution(3043492699084056876)
XLA Ops:
  1.6 1.6 %collective-permute-start = (bf16[32,1024]{1,0:T(8,128)(2,1)S(1)}, bf16[32,1024]{1,0:T(8,128)(2,1)S(1)}, u32[]{:S(2)}, u32[]{:S(2)}) collective-permute-start(bf16[32,1024]{1,0:T(8,128)(2,1)S(1)} %get-tuple-element.44), channel_id=1, source_target_pairs={{0,2},{1,3},{2,0},{3,1},{4,6},{5,7},{6,4},{7,5},{8,10},{9,11},{10,... | collective-permute-start | bytes 196616 | tf_op jit(solution)/shard_map/ppermute | solution.py:466
  3.2 1.5 %collective-permute-start.1 = (bf16[32,1024]{1,0:T(8,128)(2,1)S(1)}, bf16[32,1024]{1,0:T(8,128)(2,1)S(1)}, u32[]{:S(2)}, u32[]{:S(2)}) collective-permute-start(bf16[32,1024]{1,0:T(8,128)(2,1)S(1)} %get-tuple-element.45), channel_id=1, source_target_pairs={{0,4},{1,5},{2,6},{3,7},{4,0},{5,1},{6,2},{7,3},{8,12},{9,13},{10,... | collective-permute-start | bytes 196616 | tf_op jit(solution)/shard_map/ppermute | solution.py:466
  5.2 1.8 %gated.1 = (bf16[128,2048]{1,0:T(8,128)(2,1)S(1)}, f32[128,2048]{1,0:T(8,128)S(1)}, f32[128,2048]{1,0:T(8,128)S(1)}, s32[16,2048]{1,0:T(8,128)S(1)}) custom-call(bf16[128,2048]{1,0:T(8,128)(2,1)} %refs_0_.3, bf16[128,2048]{1,0:T(8,128)(2,1)} %refs_1_.1, s32[16,16]{1,0:T(8,128)} %refs_2_.1, bf16[32,1024]{1,0:T(8,128)(2,1)S(1)} %get-tuple-element.42.refs_3_.refs_0_), custom_call_target="tpu_custom_call" | custom-call | flops 588284992 | tf_op jit(solution)/shard_map/gated/pallas_call | solution.py:40
  6.9 2.3 %masked_weight.2.refs_4_.refs_0_ = bf16[2048,2048]{1,0:T(8,128)(2,1)S(1)} custom-call(bf16[2048,2048]{1,0:T(8,128)(2,1)} %w_ref.3, s32[16,2048]{1,0:T(8,128)S(1)} %get-tuple-element.47.m_ref.refs_4_, bf16[128,2048]{1,0:T(8,128)(2,1)S(1)} %get-tuple-element.43.refs_0_), custom_call_target="tpu_custom_call" | custom-call | flops 761310016 | tf_op jit(solution)/shard_map/masked_weight/pallas_call | solution.py:73
  9.9 1.6 %collective-permute-start.3 = (bf16[32,1024]{1,0:T(8,128)(2,1)S(1)}, bf16[32,1024]{1,0:T(8,128)(2,1)S(1)}, u32[]{:S(2)}, u32[]{:S(2)}) collective-permute-start(bf16[32,1024]{1,0:T(8,128)(2,1)S(1)} %get-tuple-element.49), channel_id=1, source_target_pairs={{0,8},{8,0},{16,24},{24,16},{1,9},{9,1},{17,25},{25,17},{2,10},{10... | collective-permute-start | bytes 196616 | tf_op jit(solution)/shard_map/ppermute | solution.py:463
  11.9 1.6 %collective-permute-start.5 = (bf16[32,1024]{1,0:T(8,128)(2,1)S(1)}, bf16[32,1024]{1,0:T(8,128)(2,1)S(1)}, u32[]{:S(2)}, u32[]{:S(2)}) collective-permute-start(bf16[32,1024]{1,0:T(8,128)(2,1)S(1)} %get-tuple-element.51.refs_1_), channel_id=1, source_target_pairs={{0,24},{8,16},{16,8},{24,0},{1,25},{9,17},{17,9},{25,1},{2,26},{10... | collective-permute-start | bytes 196616 | tf_op jit(solution)/shard_map/ppermute | solution.py:463
  13.5 2.3 %masked_weight.3.refs_4_.refs_6_.refs_2_.refs_1_.refs_3_ = bf16[2048,2048]{1,0:T(8,128)(2,1)S(1)} custom-call(bf16[2048,2048]{1,0:T(8,128)(2,1)} %w_ref.3, s32[16,2048]{1,0:T(8,128)S(1)} %get-tuple-element.47.m_ref.refs_4_, bf16[2048,2048]{1,0:T(8,128)(2,1)S(1)} %masked_weight.2.refs_4_.refs_0_, ...), custom_call_target="tpu_custom_call", output_to_operand_aliasing={{}: (2, {})} | custom-call | flops 761310016 | tf_op jit(solution)/shard_map/masked_weight/pallas_call | solution.py:73
  18.1 2.2 %collective-permute-start.9 = (bf16[128,1024]{1,0:T(8,128)(2,1)S(1)}, bf16[128,1024]{1,0:T(8,128)(2,1)S(1)}, u32[]{:S(2)}, u32[]{:S(2)}) collective-permute-start(bf16[128,1024]{1,0:T(8,128)(2,1)S(1)} %stack.3.refs_1_.refs_0_), channel_id=1, source_target_pairs={{0,6},{1,7},{2,4},{3,5},{4,2},{5,3},{6,0},{7,1},{8,14},{9,15},{10,... | collective-permute-start | bytes 786440 | tf_op jit(solution)/shard_map/ppermute | solution.py:466
  22.7 4.0 %collective-permute-start.12 = (bf16[128,2048]{1,0:T(8,128)(2,1)S(1)}, bf16[128,2048]{1,0:T(8,128)(2,1)S(1)}, u32[]{:S(2)}, u32[]{:S(2)}) collective-permute-start(bf16[128,2048]{1,0:T(8,128)(2,1)S(1)} %add_and_pass.6.refs_0_), channel_id=1, source_target_pairs={{8,16},{16,8},{9,17},{17,9},{10,18},{18,10},{11,19},{19,11},{12,20... | collective-permute-start | bytes 1572872 | tf_op jit(solution)/shard_map/ppermute | solution.py:463
  28.0 1.5 %collective-permute-done.8.refs_1_.refs_2_ = bf16[128,1024]{1,0:T(8,128)(2,1)S(1)} collective-permute-done((bf16[128,1024]{1,0:T(8,128)(2,1)S(1)}, bf16[128,1024]{1,0:T(8,128)(2,1)S(1)}, u32[]{:S(2)}, u32[]{:S(2)}) %collective-permute-start.8) | collective-permute-done | bytes 262176 | tf_op jit(solution)/shard_map/ppermute | solution.py:466
  30.8 3.5 %collective-permute-start.13 = (bf16[128,2048]{1,0:T(8,128)(2,1)S(1)}, bf16[128,2048]{1,0:T(8,128)(2,1)S(1)}, u32[]{:S(2)}, u32[]{:S(2)}) collective-permute-start(bf16[128,2048]{1,0:T(8,128)(2,1)S(1)} %collective-permute-done.6.refs_7_.refs_1_), channel_id=1, source_target_pairs={{8,16},{16,8},{9,17},{17,9},{10,18},{18,10},{11,19},{19,11},{12,20... | collective-permute-start | bytes 1572872 | tf_op jit(solution)/shard_map/ppermute | solution.py:463
  35.2 1.3 %collective-permute-start.14 = (bf16[128,2048]{1,0:T(8,128)(2,1)S(1)}, bf16[128,2048]{1,0:T(8,128)(2,1)S(1)}, u32[]{:S(2)}, u32[]{:S(2)}) collective-permute-start(bf16[128,2048]{1,0:T(8,128)(2,1)S(1)} %collective-permute-done.12.refs_8_.refs_1_), channel_id=1, source_target_pairs={{8,0},{16,24},{9,1},{17,25},{10,2},{18,26},{11,3},{19,27},{12,4},{... | collective-permute-start | bytes 1572872 | tf_op jit(solution)/shard_map/ppermute | solution.py:463
  36.6 2.5 %back_product.1 = (bf16[512,2048]{1,0:T(8,128)(2,1)S(1)}, bf16[128,2048]{1,0:T(8,128)(2,1)S(1)}, bf16[128,2048]{1,0:T(8,128)(2,1)S(1)}) custom-call(bf16[128,1024]{1,0:T(8,128)(2,1)S(1)} %stack.3.refs_1_.refs_0_, bf16[128,1024]{1,0:T(8,128)(2,1)S(1)} %collective-permute-done.7.refs_0_.refs_1_, bf16[128,1024]{1,0:T(8,128)(2,1)S(1)} %collective-permute-done.8.refs_1_.refs_2_, ...), custom_call_target="tpu_custom_call" | custom-call | flops 865124992 | tf_op jit(solution)/shard_map/back_product/pallas_call | solution.py:40
  39.1 1.3 %collective-permute-start.16 = (bf16[128,2048]{1,0:T(8,128)(2,1)S(1)}, bf16[128,2048]{1,0:T(8,128)(2,1)S(1)}, u32[]{:S(2)}, u32[]{:S(2)}) collective-permute-start(bf16[128,2048]{1,0:T(8,128)(2,1)S(1)} %get-tuple-element.52.refs_3_.refs_0_), channel_id=1, source_target_pairs={{0,8},{24,16},{1,9},{25,17},{2,10},{26,18},{3,11},{27,19},{4,12},{... | collective-permute-start | bytes 1572872 | tf_op jit(solution)/shard_map/ppermute | solution.py:463
  40.4 2.4 %out_product.2 = (bf16[256,1024]{1,0:T(8,128)(2,1)S(1)}, f32[256,1024]{1,0:T(8,128)S(1)}) custom-call(bf16[128,2048]{1,0:T(8,128)(2,1)S(1)} %add_and_pass.6.refs_0_, bf16[128,2048]{1,0:T(8,128)(2,1)S(1)} %collective-permute-done.6.refs_7_.refs_1_, bf16[2048,2048]{1,0:T(8,128)(2,1)S(1)} %masked_weight.3.refs_4_.refs_6_.refs_2_.refs_1_.refs_3_, ...), custom_call_target="tpu_custom_call" | custom-call | flops 830520000 | tf_op jit(solution)/shard_map/out_product/pallas_call | solution.py:40
  42.8 2.4 %back_rest.1 = (bf16[128,2048]{1,0:T(8,128)(2,1)S(1)}, bf16[128,2048]{1,0:T(8,128)(2,1)S(1)}) custom-call(bf16[512,2048]{1,0:T(8,128)(2,1)S(1)} %get-tuple-element.54.refs_0_.c_ref, bf16[2048,2048]{1,0:T(8,128)(2,1)S(1)} %masked_weight.3.refs_4_.refs_6_.refs_2_.refs_1_.refs_3_, f32[256,1024]{1,0:T(8,128)S(1)} %get-tuple-element.53.refs_2_.refs_0_), custom_call_target="tpu_custom_call" | custom-call | flops 830520000 | tf_op jit(solution)/shard_map/back_rest/pallas_call | solution.py:40
  46.3 3.5 %collective-permute-start.15 = (bf16[128,2048]{1,0:T(8,128)(2,1)S(1)}, bf16[128,2048]{1,0:T(8,128)(2,1)S(1)}, u32[]{:S(2)}, u32[]{:S(2)}) collective-permute-start(bf16[128,2048]{1,0:T(8,128)(2,1)S(1)} %add_and_pass.7.refs_0_.refs_2_), channel_id=1, source_target_pairs={{8,0},{16,24},{9,1},{17,25},{10,2},{18,26},{11,3},{19,27},{12,4},{... | collective-permute-start | bytes 1572872 | tf_op jit(solution)/shard_map/ppermute | solution.py:463
  49.9 1.3 %collective-permute-start.29 = (bf16[128,2048]{1,0:T(8,128)(2,1)S(1)}, bf16[128,2048]{1,0:T(8,128)(2,1)S(1)}, u32[]{:S(2)}, u32[]{:S(2)}) collective-permute-start(bf16[128,2048]{1,0:T(8,128)(2,1)S(1)} %get-tuple-element.56.refs_0_), channel_id=1, source_target_pairs={{0,8},{24,16},{1,9},{25,17},{2,10},{26,18},{3,11},{27,19},{4,12},{... | collective-permute-start | bytes 1572872 | tf_op jit(solution)/shard_map/ppermute | solution.py:463
  51.4 2.4 %collective-permute-done.16.refs_1_ = bf16[128,2048]{1,0:T(8,128)(2,1)S(1)} collective-permute-done((bf16[128,2048]{1,0:T(8,128)(2,1)S(1)}, bf16[128,2048]{1,0:T(8,128)(2,1)S(1)}, u32[]{:S(2)}, u32[]{:S(2)}) %collective-permute-start.16) | collective-permute-done | bytes 524320 | tf_op jit(solution)/shard_map/ppermute | solution.py:463
  53.9 3.6 %collective-permute-start.23 = (bf16[128,2048]{1,0:T(8,128)(2,1)S(1)}, bf16[128,2048]{1,0:T(8,128)(2,1)S(1)}, u32[]{:S(2)}, u32[]{:S(2)}) collective-permute-start(bf16[128,2048]{1,0:T(8,128)(2,1)S(1)} %add_and_pass.9.refs_4_), channel_id=1, source_target_pairs={{8,16},{16,8},{9,17},{17,9},{10,18},{18,10},{11,19},{19,11},{12,20... | collective-permute-start | bytes 1572872 | tf_op jit(solution)/shard_map/ppermute | solution.py:463
  57.6 1.4 %collective-permute-done.15.refs_2_ = bf16[128,2048]{1,0:T(8,128)(2,1)S(1)} collective-permute-done((bf16[128,2048]{1,0:T(8,128)(2,1)S(1)}, bf16[128,2048]{1,0:T(8,128)(2,1)S(1)}, u32[]{:S(2)}, u32[]{:S(2)}) %collective-permute-start.15) | collective-permute-done | bytes 524320 | tf_op jit(solution)/shard_map/ppermute | solution.py:463
  58.9 2.4 %out_product.3 = (bf16[256,512]{1,0:T(8,128)(2,1)S(1)}, bf16[256,512]{1,0:T(8,128)(2,1)S(1)}, f32[256,1024]{1,0:T(8,128)S(1)}, bf16[128,2048]{1,0:T(8,128)(2,1)S(1)}) custom-call(bf16[128,2048]{1,0:T(8,128)(2,1)S(1)} %add_and_pass.8.refs_2_.refs_0_, bf16[128,2048]{1,0:T(8,128)(2,1)S(1)} %collective-permute-done.12.refs_8_.refs_1_, ...), custom_call_target="tpu_custom_call" | custom-call | flops 830520000 | tf_op jit(solution)/shard_map/out_product/pallas_call | solution.py:40
  61.9 2.2 %collective-permute-done.29.refs_1_ = bf16[128,2048]{1,0:T(8,128)(2,1)S(1)} collective-permute-done((bf16[128,2048]{1,0:T(8,128)(2,1)S(1)}, bf16[128,2048]{1,0:T(8,128)(2,1)S(1)}, u32[]{:S(2)}, u32[]{:S(2)}) %collective-permute-start.29) | collective-permute-done | bytes 524320 | tf_op jit(solution)/shard_map/ppermute | solution.py:463
  64.2 3.8 %collective-permute-start.30 = (bf16[128,2048]{1,0:T(8,128)(2,1)S(1)}, bf16[128,2048]{1,0:T(8,128)(2,1)S(1)}, u32[]{:S(2)}, u32[]{:S(2)}) collective-permute-start(bf16[128,2048]{1,0:T(8,128)(2,1)S(1)} %add_and_pass.11), channel_id=1, source_target_pairs={{8,16},{16,8},{9,17},{17,9},{10,18},{18,10},{11,19},{19,11},{12,20... | collective-permute-start | bytes 1572872 | tf_op jit(solution)/shard_map/ppermute | solution.py:463
  69.3 1.4 %collective-permute-start.21 = (bf16[128,1024]{1,0:T(8,128)(2,1)S(1)}, bf16[128,1024]{1,0:T(8,128)(2,1)S(1)}, u32[]{:S(2)}, u32[]{:S(2)}) collective-permute-start(bf16[128,1024]{1,0:T(8,128)(2,1)S(1)} %get-tuple-element.63), channel_id=1, source_target_pairs={{0,4},{1,5},{2,6},{3,7},{4,0},{5,1},{6,2},{7,3},{8,12},{9,13},{10,... | collective-permute-start | bytes 786440 | tf_op jit(solution)/shard_map/ppermute | solution.py:466
  72.0 4.1 %down_gradient.2 = (bf16[2048,2048]{1,0:T(8,128)(2,1)}, bf16[16,128]{1,0:T(8,128)(2,1)S(1)}) custom-call(bf16[512,2048]{1,0:T(8,128)(2,1)S(1)} %get-tuple-element.54.refs_0_.c_ref, bf16[128,2048]{1,0:T(8,128)(2,1)S(1)} %add_and_pass.6.refs_0_, bf16[128,2048]{1,0:T(8,128)(2,1)S(1)} %collective-permute-done.6.refs_7_.refs_1_, ...), custom_call_target="tpu_custom_call" | custom-call | flops 1418804992 | tf_op jit(solution)/shard_map/down_gradient/pallas_call | solution.py:441
  76.2 4.1 %down_gradient.3 = (bf16[2048,2048]{1,0:T(8,128)(2,1)}, bf16[16,128]{1,0:T(8,128)(2,1)S(1)}) custom-call(bf16[512,2048]{1,0:T(8,128)(2,1)S(1)} %get-tuple-element.54.refs_0_.c_ref, bf16[128,2048]{1,0:T(8,128)(2,1)S(1)} %add_and_pass.6.refs_0_, bf16[128,2048]{1,0:T(8,128)(2,1)S(1)} %collective-permute-done.6.refs_7_.refs_1_, ...), custom_call_target="tpu_custom_call", output_to_operand_aliasing={{0}: (6, {})} | custom-call | flops 1418804992 | tf_op jit(solution)/shard_map/down_gradient/pallas_call | solution.py:441
  81.9 1.6 %collective-permute-start.26 = (bf16[32,1024]{1,0:T(8,128)(2,1)S(1)}, bf16[32,1024]{1,0:T(8,128)(2,1)S(1)}, u32[]{:S(2)}, u32[]{:S(2)}) collective-permute-start(bf16[32,1024]{1,0:T(8,128)(2,1)S(1)} %get-tuple-element.71), channel_id=1, source_target_pairs={{0,16},{1,17},{2,24},{3,25},{4,0},{5,1},{6,8},{7,9},{8,18},{9,19},... | collective-permute-start | bytes 196616 | tf_op jit(solution)/shard_map/ppermute | solution.py:524
  83.5 3.4 %collective-permute-start.27 = (bf16[32,1024]{1,0:T(8,128)(2,1)S(1)}, bf16[32,1024]{1,0:T(8,128)(2,1)S(1)}, u32[]{:S(2)}, u32[]{:S(2)}) collective-permute-start(bf16[32,1024]{1,0:T(8,128)(2,1)S(1)} %get-tuple-element.72), channel_id=1, source_target_pairs={{0,24},{1,25},{2,16},{3,17},{4,8},{5,9},{6,0},{7,1},{8,26},{9,27},... | collective-permute-start | bytes 196616 | tf_op jit(solution)/shard_map/ppermute | solution.py:524
  86.9 3.2 %collective-permute-start.24 = (bf16[32,1024]{1,0:T(8,128)(2,1)S(1)}, bf16[32,1024]{1,0:T(8,128)(2,1)S(1)}, u32[]{:S(2)}, u32[]{:S(2)}) collective-permute-start(bf16[32,1024]{1,0:T(8,128)(2,1)S(1)} %get-tuple-element.69.refs_5_), channel_id=1, source_target_pairs={{0,0},{1,1},{2,8},{3,9},{4,16},{5,17},{6,24},{7,25},{8,2},{9,3},{1... | collective-permute-start | bytes 196616 | tf_op jit(solution)/shard_map/ppermute | solution.py:524
  90.2 1.7 %gradients.1 = (bf16[128,2048]{1,0:T(8,128)(2,1)}, bf16[128,2048]{1,0:T(8,128)(2,1)}, bf16[16,128]{1,0:T(8,128)(2,1)S(1)}) custom-call(bf16[128,2048]{1,0:T(8,128)(2,1)S(1)} %get-tuple-element.73.refs_0_, bf16[128,2048]{1,0:T(8,128)(2,1)S(1)} %collective-permute-done.28.refs_1_, bf16[128,2048]{1,0:T(8,128)(2,1)S(1)} %collective-permute-done.30.refs_2_, ...), custom_call_target="tpu_custom_call" | custom-call | flops 588284992 | tf_op jit(solution)/shard_map/gradients/pallas_call | solution.py:148
  91.8 3.1 %collective-permute-done.24.refs_0_ = bf16[32,1024]{1,0:T(8,128)(2,1)S(1)} collective-permute-done((bf16[32,1024]{1,0:T(8,128)(2,1)S(1)}, bf16[32,1024]{1,0:T(8,128)(2,1)S(1)}, u32[]{:S(2)}, u32[]{:S(2)}) %collective-permute-start.24) | collective-permute-done | bytes 65568 | tf_op jit(solution)/shard_map/ppermute | solution.py:524
  (54 shorter events, 17.8 us)
Async XLA Ops:
  1.6 7.6 %collective-permute-start = (bf16[32,1024]{1,0:T(8,128)(2,1)S(1)}, bf16[32,1024]{1,0:T(8,128)(2,1)S(1)}, u32[]{:S(2)}, u32[]{:S(2)}) collective-permute-start(bf16[32,1024]{1,0:T(8,128)(2,1)S(1)} %get-tuple-element.44), channel_id=1, source_target_pairs={{0,2},{1,3},{2,0},{3,1},{4,6},{5,7},{6,4},{7,5},{8,10},{9,11},{10,... | collective-permute-start | bytes 196616 | tf_op jit(solution)/shard_map/ppermute | solution.py:466
  3.2 6.0 %collective-permute-start.1 = (bf16[32,1024]{1,0:T(8,128)(2,1)S(1)}, bf16[32,1024]{1,0:T(8,128)(2,1)S(1)}, u32[]{:S(2)}, u32[]{:S(2)}) collective-permute-start(bf16[32,1024]{1,0:T(8,128)(2,1)S(1)} %get-tuple-element.45), channel_id=1, source_target_pairs={{0,4},{1,5},{2,6},{3,7},{4,0},{5,1},{6,2},{7,3},{8,12},{9,13},{10,... | collective-permute-start | bytes 196616 | tf_op jit(solution)/shard_map/ppermute | solution.py:466
  4.7 5.2 %collective-permute-start.2 = (bf16[32,1024]{1,0:T(8,128)(2,1)S(1)}, bf16[32,1024]{1,0:T(8,128)(2,1)S(1)}, u32[]{:S(2)}, u32[]{:S(2)}) collective-permute-start(bf16[32,1024]{1,0:T(8,128)(2,1)S(1)} %get-tuple-element.46), channel_id=1, source_target_pairs={{0,6},{1,7},{2,4},{3,5},{4,2},{5,3},{6,0},{7,1},{8,14},{9,15},{10,... | collective-permute-start | bytes 196616 | tf_op jit(solution)/shard_map/ppermute | solution.py:466
  9.9 5.8 %collective-permute-start.3 = (bf16[32,1024]{1,0:T(8,128)(2,1)S(1)}, bf16[32,1024]{1,0:T(8,128)(2,1)S(1)}, u32[]{:S(2)}, u32[]{:S(2)}) collective-permute-start(bf16[32,1024]{1,0:T(8,128)(2,1)S(1)} %get-tuple-element.49), channel_id=1, source_target_pairs={{0,8},{8,0},{16,24},{24,16},{1,9},{9,1},{17,25},{25,17},{2,10},{10... | collective-permute-start | bytes 196616 | tf_op jit(solution)/shard_map/ppermute | solution.py:463
  11.6 5.3 %collective-permute-start.4 = (bf16[32,1024]{1,0:T(8,128)(2,1)S(1)}, bf16[32,1024]{1,0:T(8,128)(2,1)S(1)}, u32[]{:S(2)}, u32[]{:S(2)}) collective-permute-start(bf16[32,1024]{1,0:T(8,128)(2,1)S(1)} %get-tuple-element.50), channel_id=1, source_target_pairs={{0,16},{8,24},{16,0},{24,8},{1,17},{9,25},{17,1},{25,9},{2,18},{10... | collective-permute-start | bytes 196616 | tf_op jit(solution)/shard_map/ppermute | solution.py:463
  11.9 6.2 %collective-permute-start.5 = (bf16[32,1024]{1,0:T(8,128)(2,1)S(1)}, bf16[32,1024]{1,0:T(8,128)(2,1)S(1)}, u32[]{:S(2)}, u32[]{:S(2)}) collective-permute-start(bf16[32,1024]{1,0:T(8,128)(2,1)S(1)} %get-tuple-element.51.refs_1_), channel_id=1, source_target_pairs={{0,24},{8,16},{16,8},{24,0},{1,25},{9,17},{17,9},{25,1},{2,26},{10... | collective-permute-start | bytes 196616 | tf_op jit(solution)/shard_map/ppermute | solution.py:463
  18.1 9.7 %collective-permute-start.9 = (bf16[128,1024]{1,0:T(8,128)(2,1)S(1)}, bf16[128,1024]{1,0:T(8,128)(2,1)S(1)}, u32[]{:S(2)}, u32[]{:S(2)}) collective-permute-start(bf16[128,1024]{1,0:T(8,128)(2,1)S(1)} %stack.3.refs_1_.refs_0_), channel_id=1, source_target_pairs={{0,6},{1,7},{2,4},{3,5},{4,2},{5,3},{6,0},{7,1},{8,14},{9,15},{10,... | collective-permute-start | bytes 786440 | tf_op jit(solution)/shard_map/ppermute | solution.py:466
  20.4 10.4 %collective-permute-start.6 = (bf16[128,2048]{1,0:T(8,128)(2,1)S(1)}, bf16[128,2048]{1,0:T(8,128)(2,1)S(1)}, u32[]{:S(2)}, u32[]{:S(2)}) collective-permute-start(bf16[128,2048]{1,0:T(8,128)(2,1)S(1)} %add_and_pass.6.refs_0_), channel_id=1, source_target_pairs={{0,8},{8,0},{16,24},{24,16},{1,9},{9,1},{17,25},{25,17},{2,10},{10... | collective-permute-start | bytes 1572872 | tf_op jit(solution)/shard_map/ppermute | solution.py:463
  21.2 8.2 %collective-permute-start.8 = (bf16[128,1024]{1,0:T(8,128)(2,1)S(1)}, bf16[128,1024]{1,0:T(8,128)(2,1)S(1)}, u32[]{:S(2)}, u32[]{:S(2)}) collective-permute-start(bf16[128,1024]{1,0:T(8,128)(2,1)S(1)} %stack.3.refs_1_.refs_0_), channel_id=1, source_target_pairs={{0,4},{1,5},{2,6},{3,7},{4,0},{5,1},{6,2},{7,3},{8,12},{9,13},{10,... | collective-permute-start | bytes 786440 | tf_op jit(solution)/shard_map/ppermute | solution.py:466
  21.7 8.0 %collective-permute-start.7 = (bf16[128,1024]{1,0:T(8,128)(2,1)S(1)}, bf16[128,1024]{1,0:T(8,128)(2,1)S(1)}, u32[]{:S(2)}, u32[]{:S(2)}) collective-permute-start(bf16[128,1024]{1,0:T(8,128)(2,1)S(1)} %stack.3.refs_1_.refs_0_), channel_id=1, source_target_pairs={{0,2},{1,3},{2,0},{3,1},{4,6},{5,7},{6,4},{7,5},{8,10},{9,11},{10,... | collective-permute-start | bytes 786440 | tf_op jit(solution)/shard_map/ppermute | solution.py:466
  22.7 12.6 %collective-permute-start.12 = (bf16[128,2048]{1,0:T(8,128)(2,1)S(1)}, bf16[128,2048]{1,0:T(8,128)(2,1)S(1)}, u32[]{:S(2)}, u32[]{:S(2)}) collective-permute-start(bf16[128,2048]{1,0:T(8,128)(2,1)S(1)} %add_and_pass.6.refs_0_), channel_id=1, source_target_pairs={{8,16},{16,8},{9,17},{17,9},{10,18},{18,10},{11,19},{19,11},{12,20... | collective-permute-start | bytes 1572872 | tf_op jit(solution)/shard_map/ppermute | solution.py:463
  27.9 8.7 %collective-permute-start.10 = (bf16[256,1024]{1,0:T(8,128)(2,1)S(1)}, bf16[256,1024]{1,0:T(8,128)(2,1)S(1)}, u32[]{:S(2)}, u32[]{:S(2)}) collective-permute-start(bf16[256,1024]{1,0:T(8,128)(2,1)S(1)} %stack.4), channel_id=1, source_target_pairs={{0,1},{1,0},{2,3},{3,2},{4,5},{5,4},{6,7},{7,6},{8,9},{9,8},{10,11... | collective-permute-start | bytes 1572872 | tf_op jit(solution)/shard_map/ppermute | solution.py:469
  29.7 6.8 %collective-permute-start.11 = (bf16[256,1024]{1,0:T(8,128)(2,1)S(1)}, bf16[256,1024]{1,0:T(8,128)(2,1)S(1)}, u32[]{:S(2)}, u32[]{:S(2)}) collective-permute-start(bf16[256,1024]{1,0:T(8,128)(2,1)S(1)} %stack.5), channel_id=1, source_target_pairs={{0,1},{1,0},{2,3},{3,2},{4,5},{5,4},{6,7},{7,6},{8,9},{9,8},{10,11... | collective-permute-start | bytes 1572872 | tf_op jit(solution)/shard_map/ppermute | solution.py:469
  30.8 15.5 %collective-permute-start.13 = (bf16[128,2048]{1,0:T(8,128)(2,1)S(1)}, bf16[128,2048]{1,0:T(8,128)(2,1)S(1)}, u32[]{:S(2)}, u32[]{:S(2)}) collective-permute-start(bf16[128,2048]{1,0:T(8,128)(2,1)S(1)} %collective-permute-done.6.refs_7_.refs_1_), channel_id=1, source_target_pairs={{8,16},{16,8},{9,17},{17,9},{10,18},{18,10},{11,19},{19,11},{12,20... | collective-permute-start | bytes 1572872 | tf_op jit(solution)/shard_map/ppermute | solution.py:463
  35.2 16.0 %collective-permute-start.14 = (bf16[128,2048]{1,0:T(8,128)(2,1)S(1)}, bf16[128,2048]{1,0:T(8,128)(2,1)S(1)}, u32[]{:S(2)}, u32[]{:S(2)}) collective-permute-start(bf16[128,2048]{1,0:T(8,128)(2,1)S(1)} %collective-permute-done.12.refs_8_.refs_1_), channel_id=1, source_target_pairs={{8,0},{16,24},{9,1},{17,25},{10,2},{18,26},{11,3},{19,27},{12,4},{... | collective-permute-start | bytes 1572872 | tf_op jit(solution)/shard_map/ppermute | solution.py:463
  39.1 14.7 %collective-permute-start.16 = (bf16[128,2048]{1,0:T(8,128)(2,1)S(1)}, bf16[128,2048]{1,0:T(8,128)(2,1)S(1)}, u32[]{:S(2)}, u32[]{:S(2)}) collective-permute-start(bf16[128,2048]{1,0:T(8,128)(2,1)S(1)} %get-tuple-element.52.refs_3_.refs_0_), channel_id=1, source_target_pairs={{0,8},{24,16},{1,9},{25,17},{2,10},{26,18},{3,11},{27,19},{4,12},{... | collective-permute-start | bytes 1572872 | tf_op jit(solution)/shard_map/ppermute | solution.py:463
  46.3 12.6 %collective-permute-start.15 = (bf16[128,2048]{1,0:T(8,128)(2,1)S(1)}, bf16[128,2048]{1,0:T(8,128)(2,1)S(1)}, u32[]{:S(2)}, u32[]{:S(2)}) collective-permute-start(bf16[128,2048]{1,0:T(8,128)(2,1)S(1)} %add_and_pass.7.refs_0_.refs_2_), channel_id=1, source_target_pairs={{8,0},{16,24},{9,1},{17,25},{10,2},{18,26},{11,3},{19,27},{12,4},{... | collective-permute-start | bytes 1572872 | tf_op jit(solution)/shard_map/ppermute | solution.py:463
  49.9 14.2 %collective-permute-start.29 = (bf16[128,2048]{1,0:T(8,128)(2,1)S(1)}, bf16[128,2048]{1,0:T(8,128)(2,1)S(1)}, u32[]{:S(2)}, u32[]{:S(2)}) collective-permute-start(bf16[128,2048]{1,0:T(8,128)(2,1)S(1)} %get-tuple-element.56.refs_0_), channel_id=1, source_target_pairs={{0,8},{24,16},{1,9},{25,17},{2,10},{26,18},{3,11},{27,19},{4,12},{... | collective-permute-start | bytes 1572872 | tf_op jit(solution)/shard_map/ppermute | solution.py:463
  51.2 16.9 %collective-permute-start.17 = (bf16[256,1024]{1,0:T(8,128)(2,1)S(1)}, bf16[256,1024]{1,0:T(8,128)(2,1)S(1)}, u32[]{:S(2)}, u32[]{:S(2)}) collective-permute-start(bf16[256,1024]{1,0:T(8,128)(2,1)S(1)} %get-tuple-element.58), channel_id=1, source_target_pairs={{0,1},{1,0},{2,3},{3,2},{4,5},{5,4},{6,7},{7,6},{8,9},{9,8},{10,11... | collective-permute-start | bytes 1572872 | tf_op jit(solution)/shard_map/ppermute | solution.py:469
  53.9 17.9 %collective-permute-start.23 = (bf16[128,2048]{1,0:T(8,128)(2,1)S(1)}, bf16[128,2048]{1,0:T(8,128)(2,1)S(1)}, u32[]{:S(2)}, u32[]{:S(2)}) collective-permute-start(bf16[128,2048]{1,0:T(8,128)(2,1)S(1)} %add_and_pass.9.refs_4_), channel_id=1, source_target_pairs={{8,16},{16,8},{9,17},{17,9},{10,18},{18,10},{11,19},{19,11},{12,20... | collective-permute-start | bytes 1572872 | tf_op jit(solution)/shard_map/ppermute | solution.py:463
  61.3 6.8 %collective-permute-start.18 = (bf16[256,512]{1,0:T(8,128)(2,1)S(1)}, bf16[256,512]{1,0:T(8,128)(2,1)S(1)}, u32[]{:S(2)}, u32[]{:S(2)}) collective-permute-start(bf16[256,512]{1,0:T(8,128)(2,1)S(1)} %get-tuple-element.59), channel_id=1, source_target_pairs={{0,1},{1,0},{2,3},{3,2},{4,5},{5,4},{6,7},{7,6},{8,9},{9,8},{10,11... | collective-permute-start | bytes 786440 | tf_op jit(solution)/shard_map/ppermute | solution.py:469
  61.4 6.7 %collective-permute-start.19 = (bf16[256,512]{1,0:T(8,128)(2,1)S(1)}, bf16[256,512]{1,0:T(8,128)(2,1)S(1)}, u32[]{:S(2)}, u32[]{:S(2)}) collective-permute-start(bf16[256,512]{1,0:T(8,128)(2,1)S(1)} %get-tuple-element.60), channel_id=1, source_target_pairs={{0,1},{1,0},{2,3},{3,2},{4,5},{5,4},{6,7},{7,6},{8,9},{9,8},{10,11... | collective-permute-start | bytes 786440 | tf_op jit(solution)/shard_map/ppermute | solution.py:469
  64.2 22.7 %collective-permute-start.30 = (bf16[128,2048]{1,0:T(8,128)(2,1)S(1)}, bf16[128,2048]{1,0:T(8,128)(2,1)S(1)}, u32[]{:S(2)}, u32[]{:S(2)}) collective-permute-start(bf16[128,2048]{1,0:T(8,128)(2,1)S(1)} %add_and_pass.11), channel_id=1, source_target_pairs={{8,16},{16,8},{9,17},{17,9},{10,18},{18,10},{11,19},{19,11},{12,20... | collective-permute-start | bytes 1572872 | tf_op jit(solution)/shard_map/ppermute | solution.py:463
  68.3 12.0 %collective-permute-start.20 = (bf16[128,1024]{1,0:T(8,128)(2,1)S(1)}, bf16[128,1024]{1,0:T(8,128)(2,1)S(1)}, u32[]{:S(2)}, u32[]{:S(2)}) collective-permute-start(bf16[128,1024]{1,0:T(8,128)(2,1)S(1)} %get-tuple-element.62), channel_id=1, source_target_pairs={{0,2},{1,3},{2,0},{3,1},{4,6},{5,7},{6,4},{7,5},{8,10},{9,11},{10,... | collective-permute-start | bytes 786440 | tf_op jit(solution)/shard_map/ppermute | solution.py:466
  69.3 11.1 %collective-permute-start.21 = (bf16[128,1024]{1,0:T(8,128)(2,1)S(1)}, bf16[128,1024]{1,0:T(8,128)(2,1)S(1)}, u32[]{:S(2)}, u32[]{:S(2)}) collective-permute-start(bf16[128,1024]{1,0:T(8,128)(2,1)S(1)} %get-tuple-element.63), channel_id=1, source_target_pairs={{0,4},{1,5},{2,6},{3,7},{4,0},{5,1},{6,2},{7,3},{8,12},{9,13},{10,... | collective-permute-start | bytes 786440 | tf_op jit(solution)/shard_map/ppermute | solution.py:466
  70.8 9.7 %collective-permute-start.22 = (bf16[128,1024]{1,0:T(8,128)(2,1)S(1)}, bf16[128,1024]{1,0:T(8,128)(2,1)S(1)}, u32[]{:S(2)}, u32[]{:S(2)}) collective-permute-start(bf16[128,1024]{1,0:T(8,128)(2,1)S(1)} %get-tuple-element.64), channel_id=1, source_target_pairs={{0,6},{1,7},{2,4},{3,5},{4,2},{5,3},{6,0},{7,1},{8,14},{9,15},{10,... | collective-permute-start | bytes 786440 | tf_op jit(solution)/shard_map/ppermute | solution.py:466
  72.0 18.2 %collective-permute-start.28 = (bf16[128,2048]{1,0:T(8,128)(2,1)S(1)}, bf16[128,2048]{1,0:T(8,128)(2,1)S(1)}, u32[]{:S(2)}, u32[]{:S(2)}) collective-permute-start(bf16[128,2048]{1,0:T(8,128)(2,1)S(1)} %add_and_pass.10.refs_5_), channel_id=1, source_target_pairs={{0,8},{8,0},{16,24},{24,16},{1,9},{9,1},{17,25},{25,17},{2,10},{10... | collective-permute-start | bytes 1572872 | tf_op jit(solution)/shard_map/ppermute | solution.py:463
  80.7 11.1 %collective-permute-start.25 = (bf16[32,1024]{1,0:T(8,128)(2,1)S(1)}, bf16[32,1024]{1,0:T(8,128)(2,1)S(1)}, u32[]{:S(2)}, u32[]{:S(2)}) collective-permute-start(bf16[32,1024]{1,0:T(8,128)(2,1)S(1)} %get-tuple-element.70), channel_id=1, source_target_pairs={{0,8},{1,9},{2,0},{3,1},{4,24},{5,25},{6,16},{7,17},{8,10},{9,11},... | collective-permute-start | bytes 196616 | tf_op jit(solution)/shard_map/ppermute | solution.py:524
  81.9 9.9 %collective-permute-start.26 = (bf16[32,1024]{1,0:T(8,128)(2,1)S(1)}, bf16[32,1024]{1,0:T(8,128)(2,1)S(1)}, u32[]{:S(2)}, u32[]{:S(2)}) collective-permute-start(bf16[32,1024]{1,0:T(8,128)(2,1)S(1)} %get-tuple-element.71), channel_id=1, source_target_pairs={{0,16},{1,17},{2,24},{3,25},{4,0},{5,1},{6,8},{7,9},{8,18},{9,19},... | collective-permute-start | bytes 196616 | tf_op jit(solution)/shard_map/ppermute | solution.py:524
  83.5 8.3 %collective-permute-start.27 = (bf16[32,1024]{1,0:T(8,128)(2,1)S(1)}, bf16[32,1024]{1,0:T(8,128)(2,1)S(1)}, u32[]{:S(2)}, u32[]{:S(2)}) collective-permute-start(bf16[32,1024]{1,0:T(8,128)(2,1)S(1)} %get-tuple-element.72), channel_id=1, source_target_pairs={{0,24},{1,25},{2,16},{3,17},{4,8},{5,9},{6,0},{7,1},{8,26},{9,27},... | collective-permute-start | bytes 196616 | tf_op jit(solution)/shard_map/ppermute | solution.py:524
  86.9 8.0 %collective-permute-start.24 = (bf16[32,1024]{1,0:T(8,128)(2,1)S(1)}, bf16[32,1024]{1,0:T(8,128)(2,1)S(1)}, u32[]{:S(2)}, u32[]{:S(2)}) collective-permute-start(bf16[32,1024]{1,0:T(8,128)(2,1)S(1)} %get-tuple-element.69.refs_5_), channel_id=1, source_target_pairs={{0,0},{1,1},{2,8},{3,9},{4,16},{5,17},{6,24},{7,25},{8,2},{9,3},{1... | collective-permute-start | bytes 196616 | tf_op jit(solution)/shard_map/ppermute | solution.py:524

commit v6 on v5

--- a/solution.py
+++ b/solution.py
@@ -509,7 +509,7 @@
     received.append([over_core(x) for x in sent])
     (to_inner,) = add_and_pass([(back3, first2)], after=[own23])
     across = over_row(to_inner, 3, inner)
-    pieces = pair_sum([own01, own23], received, tok, chips)
+    pieces = pair_sum([own01, own23], received, tok, chips, after=[to_inner])
     pieces = [pieces[0]] + [over_chips(pieces[u], u) for u in range(1, chips)]
     (to_near,) = add_and_pass([(back1, second)], after=[pieces[0]])
     beside = over_row(to_near, 1)

time: 96.7 us -> 96.7 us (level)
  no operation moved by 1% of the time
where the time goes in v6:
time: 96.7 us; the launch traced here: 95.7 us
  starting transfers between devices  47.8 us (49%)
  Pallas kernels  28.7 us (30%)
  waiting for transfers between devices  18.2 us (19%)
    ppermute x13, starting transfers between devices, over_row(): return lax.ppermute(x, 'row', [(i, i ^ t) for i in senders])  26.8 us
    pallas_call x18, Pallas kernels, call(): pl.pallas_call(body, in_specs=(specs or [VMEM] * n) + [pl.BlockSpec(memor...  13.5 us
    ppermute x13, waiting for transfers between devices, over_row(): return lax.ppermute(x, 'row', [(i, i ^ t) for i in senders])  11.4 us
    ppermute x9, starting transfers between devices, over_chips(): return lax.ppermute(x, 'col', [(j, j ^ 2 * u) for j in range(2 * chips)])  10.8 us
    ppermute x4, starting transfers between devices, fast_body(): lax.ppermute(ready[k], ('row', 'col'), [(r * width + 2 * a + h, (a ^ k) *...  9.47 us
    pallas_call x2, Pallas kernels, down_gradient(): pl.pallas_call(kernel, grid=(2,), in_specs=[pl.BlockSpec((tokens, step),...  8.28 us
    pallas_call x2, Pallas kernels, masked_weight(): pl.pallas_call(kernel, in_specs=[ANY, VMEM] + [VMEM] * len(extra) + [ANY]...  4.52 us
    ppermute x9, waiting for transfers between devices, over_chips(): return lax.ppermute(x, 'col', [(j, j ^ 2 * u) for j in range(2 * chips)])  3.67 us
  transfers between devices with their start and end apart: 31, of which 14 were waited for; matrix products, arithmetic and copies ran while one was open for 0% of the time, Pallas kernels for 28%

profile of v6, /device:TPU:16, one launch (start us, length us, event | category | flops | bytes accessed | tf_op | source)
XLA Modules:
  0.0 95.7 jit_solution(16179961024744790088)
XLA Ops:
  1.6 1.6 %collective-permute-start = (bf16[32,1024]{1,0:T(8,128)(2,1)S(1)}, bf16[32,1024]{1,0:T(8,128)(2,1)S(1)}, u32[]{:S(2)}, u32[]{:S(2)}) collective-permute-start(bf16[32,1024]{1,0:T(8,128)(2,1)S(1)} %get-tuple-element.44), channel_id=1, source_target_pairs={{0,2},{1,3},{2,0},{3,1},{4,6},{5,7},{6,4},{7,5},{8,10},{9,11},{10,... | collective-permute-start | bytes 196616 | tf_op jit(solution)/shard_map/ppermute | solution.py:466
  3.2 1.5 %collective-permute-start.1 = (bf16[32,1024]{1,0:T(8,128)(2,1)S(1)}, bf16[32,1024]{1,0:T(8,128)(2,1)S(1)}, u32[]{:S(2)}, u32[]{:S(2)}) collective-permute-start(bf16[32,1024]{1,0:T(8,128)(2,1)S(1)} %get-tuple-element.45), channel_id=1, source_target_pairs={{0,4},{1,5},{2,6},{3,7},{4,0},{5,1},{6,2},{7,3},{8,12},{9,13},{10,... | collective-permute-start | bytes 196616 | tf_op jit(solution)/shard_map/ppermute | solution.py:466
  5.2 1.8 %gated.1 = (bf16[128,2048]{1,0:T(8,128)(2,1)S(1)}, f32[128,2048]{1,0:T(8,128)S(1)}, f32[128,2048]{1,0:T(8,128)S(1)}, s32[16,2048]{1,0:T(8,128)S(1)}) custom-call(bf16[128,2048]{1,0:T(8,128)(2,1)} %refs_0_.3, bf16[128,2048]{1,0:T(8,128)(2,1)} %refs_1_.1, s32[16,16]{1,0:T(8,128)} %refs_2_.1, bf16[32,1024]{1,0:T(8,128)(2,1)S(1)} %get-tuple-element.42.refs_3_.refs_0_), custom_call_target="tpu_custom_call" | custom-call | flops 588284992 | tf_op jit(solution)/shard_map/gated/pallas_call | solution.py:40
  6.9 2.3 %masked_weight.2.refs_4_.refs_0_ = bf16[2048,2048]{1,0:T(8,128)(2,1)S(1)} custom-call(bf16[2048,2048]{1,0:T(8,128)(2,1)} %w_ref.3, s32[16,2048]{1,0:T(8,128)S(1)} %get-tuple-element.47.m_ref.refs_4_, bf16[128,2048]{1,0:T(8,128)(2,1)S(1)} %get-tuple-element.43.refs_0_), custom_call_target="tpu_custom_call" | custom-call | flops 761310016 | tf_op jit(solution)/shard_map/masked_weight/pallas_call | solution.py:73
  9.9 1.6 %collective-permute-start.3 = (bf16[32,1024]{1,0:T(8,128)(2,1)S(1)}, bf16[32,1024]{1,0:T(8,128)(2,1)S(1)}, u32[]{:S(2)}, u32[]{:S(2)}) collective-permute-start(bf16[32,1024]{1,0:T(8,128)(2,1)S(1)} %get-tuple-element.49), channel_id=1, source_target_pairs={{0,8},{8,0},{16,24},{24,16},{1,9},{9,1},{17,25},{25,17},{2,10},{10... | collective-permute-start | bytes 196616 | tf_op jit(solution)/shard_map/ppermute | solution.py:463
  11.9 1.6 %collective-permute-start.5 = (bf16[32,1024]{1,0:T(8,128)(2,1)S(1)}, bf16[32,1024]{1,0:T(8,128)(2,1)S(1)}, u32[]{:S(2)}, u32[]{:S(2)}) collective-permute-start(bf16[32,1024]{1,0:T(8,128)(2,1)S(1)} %get-tuple-element.51.refs_1_), channel_id=1, source_target_pairs={{0,24},{8,16},{16,8},{24,0},{1,25},{9,17},{17,9},{25,1},{2,26},{10... | collective-permute-start | bytes 196616 | tf_op jit(solution)/shard_map/ppermute | solution.py:463
  13.5 2.3 %masked_weight.3.refs_4_.refs_6_.refs_2_.refs_1_.refs_3_ = bf16[2048,2048]{1,0:T(8,128)(2,1)S(1)} custom-call(bf16[2048,2048]{1,0:T(8,128)(2,1)} %w_ref.3, s32[16,2048]{1,0:T(8,128)S(1)} %get-tuple-element.47.m_ref.refs_4_, bf16[2048,2048]{1,0:T(8,128)(2,1)S(1)} %masked_weight.2.refs_4_.refs_0_, ...), custom_call_target="tpu_custom_call", output_to_operand_aliasing={{}: (2, {})} | custom-call | flops 761310016 | tf_op jit(solution)/shard_map/masked_weight/pallas_call | solution.py:73
  18.1 2.2 %collective-permute-start.9 = (bf16[128,1024]{1,0:T(8,128)(2,1)S(1)}, bf16[128,1024]{1,0:T(8,128)(2,1)S(1)}, u32[]{:S(2)}, u32[]{:S(2)}) collective-permute-start(bf16[128,1024]{1,0:T(8,128)(2,1)S(1)} %stack.3.refs_1_.refs_0_), channel_id=1, source_target_pairs={{0,6},{1,7},{2,4},{3,5},{4,2},{5,3},{6,0},{7,1},{8,14},{9,15},{10,... | collective-permute-start | bytes 786440 | tf_op jit(solution)/shard_map/ppermute | solution.py:466
  22.7 4.0 %collective-permute-start.12 = (bf16[128,2048]{1,0:T(8,128)(2,1)S(1)}, bf16[128,2048]{1,0:T(8,128)(2,1)S(1)}, u32[]{:S(2)}, u32[]{:S(2)}) collective-permute-start(bf16[128,2048]{1,0:T(8,128)(2,1)S(1)} %add_and_pass.6.refs_0_), channel_id=1, source_target_pairs={{8,16},{16,8},{9,17},{17,9},{10,18},{18,10},{11,19},{19,11},{12,20... | collective-permute-start | bytes 1572872 | tf_op jit(solution)/shard_map/ppermute | solution.py:463
  28.0 1.5 %collective-permute-done.8.refs_1_.refs_2_ = bf16[128,1024]{1,0:T(8,128)(2,1)S(1)} collective-permute-done((bf16[128,1024]{1,0:T(8,128)(2,1)S(1)}, bf16[128,1024]{1,0:T(8,128)(2,1)S(1)}, u32[]{:S(2)}, u32[]{:S(2)}) %collective-permute-start.8) | collective-permute-done | bytes 262176 | tf_op jit(solution)/shard_map/ppermute | solution.py:466
  30.8 3.5 %collective-permute-start.13 = (bf16[128,2048]{1,0:T(8,128)(2,1)S(1)}, bf16[128,2048]{1,0:T(8,128)(2,1)S(1)}, u32[]{:S(2)}, u32[]{:S(2)}) collective-permute-start(bf16[128,2048]{1,0:T(8,128)(2,1)S(1)} %collective-permute-done.6.refs_7_.refs_1_), channel_id=1, source_target_pairs={{8,16},{16,8},{9,17},{17,9},{10,18},{18,10},{11,19},{19,11},{12,20... | collective-permute-start | bytes 1572872 | tf_op jit(solution)/shard_map/ppermute | solution.py:463
  35.2 1.3 %collective-permute-start.14 = (bf16[128,2048]{1,0:T(8,128)(2,1)S(1)}, bf16[128,2048]{1,0:T(8,128)(2,1)S(1)}, u32[]{:S(2)}, u32[]{:S(2)}) collective-permute-start(bf16[128,2048]{1,0:T(8,128)(2,1)S(1)} %collective-permute-done.12.refs_8_.refs_1_), channel_id=1, source_target_pairs={{8,0},{16,24},{9,1},{17,25},{10,2},{18,26},{11,3},{19,27},{12,4},{... | collective-permute-start | bytes 1572872 | tf_op jit(solution)/shard_map/ppermute | solution.py:463
  36.6 2.5 %back_product.1 = (bf16[512,2048]{1,0:T(8,128)(2,1)S(1)}, bf16[128,2048]{1,0:T(8,128)(2,1)S(1)}, bf16[128,2048]{1,0:T(8,128)(2,1)S(1)}) custom-call(bf16[128,1024]{1,0:T(8,128)(2,1)S(1)} %stack.3.refs_1_.refs_0_, bf16[128,1024]{1,0:T(8,128)(2,1)S(1)} %collective-permute-done.7.refs_0_.refs_1_, bf16[128,1024]{1,0:T(8,128)(2,1)S(1)} %collective-permute-done.8.refs_1_.refs_2_, ...), custom_call_target="tpu_custom_call" | custom-call | flops 865124992 | tf_op jit(solution)/shard_map/back_product/pallas_call | solution.py:40
  39.1 1.3 %collective-permute-start.16 = (bf16[128,2048]{1,0:T(8,128)(2,1)S(1)}, bf16[128,2048]{1,0:T(8,128)(2,1)S(1)}, u32[]{:S(2)}, u32[]{:S(2)}) collective-permute-start(bf16[128,2048]{1,0:T(8,128)(2,1)S(1)} %get-tuple-element.52.refs_3_.refs_0_), channel_id=1, source_target_pairs={{0,8},{24,16},{1,9},{25,17},{2,10},{26,18},{3,11},{27,19},{4,12},{... | collective-permute-start | bytes 1572872 | tf_op jit(solution)/shard_map/ppermute | solution.py:463
  40.4 2.4 %out_product.2 = (bf16[256,1024]{1,0:T(8,128)(2,1)S(1)}, f32[256,1024]{1,0:T(8,128)S(1)}) custom-call(bf16[128,2048]{1,0:T(8,128)(2,1)S(1)} %add_and_pass.6.refs_0_, bf16[128,2048]{1,0:T(8,128)(2,1)S(1)} %collective-permute-done.6.refs_7_.refs_1_, bf16[2048,2048]{1,0:T(8,128)(2,1)S(1)} %masked_weight.3.refs_4_.refs_6_.refs_2_.refs_1_.refs_3_, ...), custom_call_target="tpu_custom_call" | custom-call | flops 830520000 | tf_op jit(solution)/shard_map/out_product/pallas_call | solution.py:40
  42.8 2.4 %back_rest.1 = (bf16[128,2048]{1,0:T(8,128)(2,1)S(1)}, bf16[128,2048]{1,0:T(8,128)(2,1)S(1)}) custom-call(bf16[512,2048]{1,0:T(8,128)(2,1)S(1)} %get-tuple-element.54.refs_0_.c_ref, bf16[2048,2048]{1,0:T(8,128)(2,1)S(1)} %masked_weight.3.refs_4_.refs_6_.refs_2_.refs_1_.refs_3_, f32[256,1024]{1,0:T(8,128)S(1)} %get-tuple-element.53.refs_2_.refs_0_), custom_call_target="tpu_custom_call" | custom-call | flops 830520000 | tf_op jit(solution)/shard_map/back_rest/pallas_call | solution.py:40
  46.3 3.5 %collective-permute-start.15 = (bf16[128,2048]{1,0:T(8,128)(2,1)S(1)}, bf16[128,2048]{1,0:T(8,128)(2,1)S(1)}, u32[]{:S(2)}, u32[]{:S(2)}) collective-permute-start(bf16[128,2048]{1,0:T(8,128)(2,1)S(1)} %add_and_pass.7.refs_0_.refs_2_), channel_id=1, source_target_pairs={{8,0},{16,24},{9,1},{17,25},{10,2},{18,26},{11,3},{19,27},{12,4},{... | collective-permute-start | bytes 1572872 | tf_op jit(solution)/shard_map/ppermute | solution.py:463
  49.9 1.3 %collective-permute-start.20 = (bf16[128,2048]{1,0:T(8,128)(2,1)S(1)}, bf16[128,2048]{1,0:T(8,128)(2,1)S(1)}, u32[]{:S(2)}, u32[]{:S(2)}) collective-permute-start(bf16[128,2048]{1,0:T(8,128)(2,1)S(1)} %get-tuple-element.56.refs_0_), channel_id=1, source_target_pairs={{0,8},{24,16},{1,9},{25,17},{2,10},{26,18},{3,11},{27,19},{4,12},{... | collective-permute-start | bytes 1572872 | tf_op jit(solution)/shard_map/ppermute | solution.py:463
  51.4 2.4 %collective-permute-done.16.refs_1_ = bf16[128,2048]{1,0:T(8,128)(2,1)S(1)} collective-permute-done((bf16[128,2048]{1,0:T(8,128)(2,1)S(1)}, bf16[128,2048]{1,0:T(8,128)(2,1)S(1)}, u32[]{:S(2)}, u32[]{:S(2)}) %collective-permute-start.16) | collective-permute-done | bytes 524320 | tf_op jit(solution)/shard_map/ppermute | solution.py:463
  53.9 3.6 %collective-permute-start.24 = (bf16[128,2048]{1,0:T(8,128)(2,1)S(1)}, bf16[128,2048]{1,0:T(8,128)(2,1)S(1)}, u32[]{:S(2)}, u32[]{:S(2)}) collective-permute-start(bf16[128,2048]{1,0:T(8,128)(2,1)S(1)} %add_and_pass.9.refs_4_), channel_id=1, source_target_pairs={{8,16},{16,8},{9,17},{17,9},{10,18},{18,10},{11,19},{19,11},{12,20... | collective-permute-start | bytes 1572872 | tf_op jit(solution)/shard_map/ppermute | solution.py:463
  57.6 1.4 %collective-permute-done.15.refs_2_ = bf16[128,2048]{1,0:T(8,128)(2,1)S(1)} collective-permute-done((bf16[128,2048]{1,0:T(8,128)(2,1)S(1)}, bf16[128,2048]{1,0:T(8,128)(2,1)S(1)}, u32[]{:S(2)}, u32[]{:S(2)}) %collective-permute-start.15) | collective-permute-done | bytes 524320 | tf_op jit(solution)/shard_map/ppermute | solution.py:463
  58.9 2.4 %out_product.3 = (bf16[256,512]{1,0:T(8,128)(2,1)S(1)}, bf16[256,512]{1,0:T(8,128)(2,1)S(1)}, f32[256,1024]{1,0:T(8,128)S(1)}, bf16[128,2048]{1,0:T(8,128)(2,1)S(1)}) custom-call(bf16[128,2048]{1,0:T(8,128)(2,1)S(1)} %add_and_pass.8.refs_2_.refs_0_, bf16[128,2048]{1,0:T(8,128)(2,1)S(1)} %collective-permute-done.12.refs_8_.refs_1_, ...), custom_call_target="tpu_custom_call" | custom-call | flops 830520000 | tf_op jit(solution)/shard_map/out_product/pallas_call | solution.py:40
  61.9 2.2 %collective-permute-done.20.refs_1_ = bf16[128,2048]{1,0:T(8,128)(2,1)S(1)} collective-permute-done((bf16[128,2048]{1,0:T(8,128)(2,1)S(1)}, bf16[128,2048]{1,0:T(8,128)(2,1)S(1)}, u32[]{:S(2)}, u32[]{:S(2)}) %collective-permute-start.20) | collective-permute-done | bytes 524320 | tf_op jit(solution)/shard_map/ppermute | solution.py:463
  64.2 3.8 %collective-permute-start.30 = (bf16[128,2048]{1,0:T(8,128)(2,1)S(1)}, bf16[128,2048]{1,0:T(8,128)(2,1)S(1)}, u32[]{:S(2)}, u32[]{:S(2)}) collective-permute-start(bf16[128,2048]{1,0:T(8,128)(2,1)S(1)} %add_and_pass.10.refs_5_), channel_id=1, source_target_pairs={{8,16},{16,8},{9,17},{17,9},{10,18},{18,10},{11,19},{19,11},{12,20... | collective-permute-start | bytes 1572872 | tf_op jit(solution)/shard_map/ppermute | solution.py:463
  69.4 1.4 %collective-permute-start.22 = (bf16[128,1024]{1,0:T(8,128)(2,1)S(1)}, bf16[128,1024]{1,0:T(8,128)(2,1)S(1)}, u32[]{:S(2)}, u32[]{:S(2)}) collective-permute-start(bf16[128,1024]{1,0:T(8,128)(2,1)S(1)} %get-tuple-element.63), channel_id=1, source_target_pairs={{0,4},{1,5},{2,6},{3,7},{4,0},{5,1},{6,2},{7,3},{8,12},{9,13},{10,... | collective-permute-start | bytes 786440 | tf_op jit(solution)/shard_map/ppermute | solution.py:466
  72.1 4.1 %down_gradient.2 = (bf16[2048,2048]{1,0:T(8,128)(2,1)}, bf16[16,128]{1,0:T(8,128)(2,1)S(1)}) custom-call(bf16[512,2048]{1,0:T(8,128)(2,1)S(1)} %get-tuple-element.54.refs_0_.c_ref, bf16[128,2048]{1,0:T(8,128)(2,1)S(1)} %add_and_pass.6.refs_0_, bf16[128,2048]{1,0:T(8,128)(2,1)S(1)} %collective-permute-done.6.refs_7_.refs_1_, ...), custom_call_target="tpu_custom_call" | custom-call | flops 1418804992 | tf_op jit(solution)/shard_map/down_gradient/pallas_call | solution.py:441
  76.2 4.1 %down_gradient.3 = (bf16[2048,2048]{1,0:T(8,128)(2,1)}, bf16[16,128]{1,0:T(8,128)(2,1)S(1)}) custom-call(bf16[512,2048]{1,0:T(8,128)(2,1)S(1)} %get-tuple-element.54.refs_0_.c_ref, bf16[128,2048]{1,0:T(8,128)(2,1)S(1)} %add_and_pass.6.refs_0_, bf16[128,2048]{1,0:T(8,128)(2,1)S(1)} %collective-permute-done.6.refs_7_.refs_1_, ...), custom_call_target="tpu_custom_call", output_to_operand_aliasing={{0}: (6, {})} | custom-call | flops 1418804992 | tf_op jit(solution)/shard_map/down_gradient/pallas_call | solution.py:441
  82.0 1.6 %collective-permute-start.27 = (bf16[32,1024]{1,0:T(8,128)(2,1)S(1)}, bf16[32,1024]{1,0:T(8,128)(2,1)S(1)}, u32[]{:S(2)}, u32[]{:S(2)}) collective-permute-start(bf16[32,1024]{1,0:T(8,128)(2,1)S(1)} %get-tuple-element.71), channel_id=1, source_target_pairs={{0,16},{1,17},{2,24},{3,25},{4,0},{5,1},{6,8},{7,9},{8,18},{9,19},... | collective-permute-start | bytes 196616 | tf_op jit(solution)/shard_map/ppermute | solution.py:524
  83.6 3.4 %collective-permute-start.28 = (bf16[32,1024]{1,0:T(8,128)(2,1)S(1)}, bf16[32,1024]{1,0:T(8,128)(2,1)S(1)}, u32[]{:S(2)}, u32[]{:S(2)}) collective-permute-start(bf16[32,1024]{1,0:T(8,128)(2,1)S(1)} %get-tuple-element.72), channel_id=1, source_target_pairs={{0,24},{1,25},{2,16},{3,17},{4,8},{5,9},{6,0},{7,1},{8,26},{9,27},... | collective-permute-start | bytes 196616 | tf_op jit(solution)/shard_map/ppermute | solution.py:524
  87.0 3.2 %collective-permute-start.25 = (bf16[32,1024]{1,0:T(8,128)(2,1)S(1)}, bf16[32,1024]{1,0:T(8,128)(2,1)S(1)}, u32[]{:S(2)}, u32[]{:S(2)}) collective-permute-start(bf16[32,1024]{1,0:T(8,128)(2,1)S(1)} %get-tuple-element.69.refs_5_), channel_id=1, source_target_pairs={{0,0},{1,1},{2,8},{3,9},{4,16},{5,17},{6,24},{7,25},{8,2},{9,3},{1... | collective-permute-start | bytes 196616 | tf_op jit(solution)/shard_map/ppermute | solution.py:524
  90.2 1.7 %gradients.1 = (bf16[128,2048]{1,0:T(8,128)(2,1)}, bf16[128,2048]{1,0:T(8,128)(2,1)}, bf16[16,128]{1,0:T(8,128)(2,1)S(1)}) custom-call(bf16[128,2048]{1,0:T(8,128)(2,1)S(1)} %get-tuple-element.73.refs_0_, bf16[128,2048]{1,0:T(8,128)(2,1)S(1)} %collective-permute-done.29.refs_1_, bf16[128,2048]{1,0:T(8,128)(2,1)S(1)} %collective-permute-done.30.refs_2_, ...), custom_call_target="tpu_custom_call" | custom-call | flops 588284992 | tf_op jit(solution)/shard_map/gradients/pallas_call | solution.py:148
  91.9 3.1 %collective-permute-done.25.refs_0_ = bf16[32,1024]{1,0:T(8,128)(2,1)S(1)} collective-permute-done((bf16[32,1024]{1,0:T(8,128)(2,1)S(1)}, bf16[32,1024]{1,0:T(8,128)(2,1)S(1)}, u32[]{:S(2)}, u32[]{:S(2)}) %collective-permute-start.25) | collective-permute-done | bytes 65568 | tf_op jit(solution)/shard_map/ppermute | solution.py:524
  (54 shorter events, 17.8 us)
Async XLA Ops:
  1.6 7.6 %collective-permute-start = (bf16[32,1024]{1,0:T(8,128)(2,1)S(1)}, bf16[32,1024]{1,0:T(8,128)(2,1)S(1)}, u32[]{:S(2)}, u32[]{:S(2)}) collective-permute-start(bf16[32,1024]{1,0:T(8,128)(2,1)S(1)} %get-tuple-element.44), channel_id=1, source_target_pairs={{0,2},{1,3},{2,0},{3,1},{4,6},{5,7},{6,4},{7,5},{8,10},{9,11},{10,... | collective-permute-start | bytes 196616 | tf_op jit(solution)/shard_map/ppermute | solution.py:466
  3.2 6.0 %collective-permute-start.1 = (bf16[32,1024]{1,0:T(8,128)(2,1)S(1)}, bf16[32,1024]{1,0:T(8,128)(2,1)S(1)}, u32[]{:S(2)}, u32[]{:S(2)}) collective-permute-start(bf16[32,1024]{1,0:T(8,128)(2,1)S(1)} %get-tuple-element.45), channel_id=1, source_target_pairs={{0,4},{1,5},{2,6},{3,7},{4,0},{5,1},{6,2},{7,3},{8,12},{9,13},{10,... | collective-permute-start | bytes 196616 | tf_op jit(solution)/shard_map/ppermute | solution.py:466
  4.7 5.2 %collective-permute-start.2 = (bf16[32,1024]{1,0:T(8,128)(2,1)S(1)}, bf16[32,1024]{1,0:T(8,128)(2,1)S(1)}, u32[]{:S(2)}, u32[]{:S(2)}) collective-permute-start(bf16[32,1024]{1,0:T(8,128)(2,1)S(1)} %get-tuple-element.46), channel_id=1, source_target_pairs={{0,6},{1,7},{2,4},{3,5},{4,2},{5,3},{6,0},{7,1},{8,14},{9,15},{10,... | collective-permute-start | bytes 196616 | tf_op jit(solution)/shard_map/ppermute | solution.py:466
  9.9 5.8 %collective-permute-start.3 = (bf16[32,1024]{1,0:T(8,128)(2,1)S(1)}, bf16[32,1024]{1,0:T(8,128)(2,1)S(1)}, u32[]{:S(2)}, u32[]{:S(2)}) collective-permute-start(bf16[32,1024]{1,0:T(8,128)(2,1)S(1)} %get-tuple-element.49), channel_id=1, source_target_pairs={{0,8},{8,0},{16,24},{24,16},{1,9},{9,1},{17,25},{25,17},{2,10},{10... | collective-permute-start | bytes 196616 | tf_op jit(solution)/shard_map/ppermute | solution.py:463
  11.6 5.3 %collective-permute-start.4 = (bf16[32,1024]{1,0:T(8,128)(2,1)S(1)}, bf16[32,1024]{1,0:T(8,128)(2,1)S(1)}, u32[]{:S(2)}, u32[]{:S(2)}) collective-permute-start(bf16[32,1024]{1,0:T(8,128)(2,1)S(1)} %get-tuple-element.50), channel_id=1, source_target_pairs={{0,16},{8,24},{16,0},{24,8},{1,17},{9,25},{17,1},{25,9},{2,18},{10... | collective-permute-start | bytes 196616 | tf_op jit(solution)/shard_map/ppermute | solution.py:463
  11.9 6.2 %collective-permute-start.5 = (bf16[32,1024]{1,0:T(8,128)(2,1)S(1)}, bf16[32,1024]{1,0:T(8,128)(2,1)S(1)}, u32[]{:S(2)}, u32[]{:S(2)}) collective-permute-start(bf16[32,1024]{1,0:T(8,128)(2,1)S(1)} %get-tuple-element.51.refs_1_), channel_id=1, source_target_pairs={{0,24},{8,16},{16,8},{24,0},{1,25},{9,17},{17,9},{25,1},{2,26},{10... | collective-permute-start | bytes 196616 | tf_op jit(solution)/shard_map/ppermute | solution.py:463
  18.1 9.7 %collective-permute-start.9 = (bf16[128,1024]{1,0:T(8,128)(2,1)S(1)}, bf16[128,1024]{1,0:T(8,128)(2,1)S(1)}, u32[]{:S(2)}, u32[]{:S(2)}) collective-permute-start(bf16[128,1024]{1,0:T(8,128)(2,1)S(1)} %stack.3.refs_1_.refs_0_), channel_id=1, source_target_pairs={{0,6},{1,7},{2,4},{3,5},{4,2},{5,3},{6,0},{7,1},{8,14},{9,15},{10,... | collective-permute-start | bytes 786440 | tf_op jit(solution)/shard_map/ppermute | solution.py:466
  20.4 10.4 %collective-permute-start.6 = (bf16[128,2048]{1,0:T(8,128)(2,1)S(1)}, bf16[128,2048]{1,0:T(8,128)(2,1)S(1)}, u32[]{:S(2)}, u32[]{:S(2)}) collective-permute-start(bf16[128,2048]{1,0:T(8,128)(2,1)S(1)} %add_and_pass.6.refs_0_), channel_id=1, source_target_pairs={{0,8},{8,0},{16,24},{24,16},{1,9},{9,1},{17,25},{25,17},{2,10},{10... | collective-permute-start | bytes 1572872 | tf_op jit(solution)/shard_map/ppermute | solution.py:463
  21.2 8.2 %collective-permute-start.8 = (bf16[128,1024]{1,0:T(8,128)(2,1)S(1)}, bf16[128,1024]{1,0:T(8,128)(2,1)S(1)}, u32[]{:S(2)}, u32[]{:S(2)}) collective-permute-start(bf16[128,1024]{1,0:T(8,128)(2,1)S(1)} %stack.3.refs_1_.refs_0_), channel_id=1, source_target_pairs={{0,4},{1,5},{2,6},{3,7},{4,0},{5,1},{6,2},{7,3},{8,12},{9,13},{10,... | collective-permute-start | bytes 786440 | tf_op jit(solution)/shard_map/ppermute | solution.py:466
  21.7 8.0 %collective-permute-start.7 = (bf16[128,1024]{1,0:T(8,128)(2,1)S(1)}, bf16[128,1024]{1,0:T(8,128)(2,1)S(1)}, u32[]{:S(2)}, u32[]{:S(2)}) collective-permute-start(bf16[128,1024]{1,0:T(8,128)(2,1)S(1)} %stack.3.refs_1_.refs_0_), channel_id=1, source_target_pairs={{0,2},{1,3},{2,0},{3,1},{4,6},{5,7},{6,4},{7,5},{8,10},{9,11},{10,... | collective-permute-start | bytes 786440 | tf_op jit(solution)/shard_map/ppermute | solution.py:466
  22.7 12.6 %collective-permute-start.12 = (bf16[128,2048]{1,0:T(8,128)(2,1)S(1)}, bf16[128,2048]{1,0:T(8,128)(2,1)S(1)}, u32[]{:S(2)}, u32[]{:S(2)}) collective-permute-start(bf16[128,2048]{1,0:T(8,128)(2,1)S(1)} %add_and_pass.6.refs_0_), channel_id=1, source_target_pairs={{8,16},{16,8},{9,17},{17,9},{10,18},{18,10},{11,19},{19,11},{12,20... | collective-permute-start | bytes 1572872 | tf_op jit(solution)/shard_map/ppermute | solution.py:463
  27.9 8.7 %collective-permute-start.10 = (bf16[256,1024]{1,0:T(8,128)(2,1)S(1)}, bf16[256,1024]{1,0:T(8,128)(2,1)S(1)}, u32[]{:S(2)}, u32[]{:S(2)}) collective-permute-start(bf16[256,1024]{1,0:T(8,128)(2,1)S(1)} %stack.4), channel_id=1, source_target_pairs={{0,1},{1,0},{2,3},{3,2},{4,5},{5,4},{6,7},{7,6},{8,9},{9,8},{10,11... | collective-permute-start | bytes 1572872 | tf_op jit(solution)/shard_map/ppermute | solution.py:469
  29.7 6.8 %collective-permute-start.11 = (bf16[256,1024]{1,0:T(8,128)(2,1)S(1)}, bf16[256,1024]{1,0:T(8,128)(2,1)S(1)}, u32[]{:S(2)}, u32[]{:S(2)}) collective-permute-start(bf16[256,1024]{1,0:T(8,128)(2,1)S(1)} %stack.5), channel_id=1, source_target_pairs={{0,1},{1,0},{2,3},{3,2},{4,5},{5,4},{6,7},{7,6},{8,9},{9,8},{10,11... | collective-permute-start | bytes 1572872 | tf_op jit(solution)/shard_map/ppermute | solution.py:469
  30.8 15.5 %collective-permute-start.13 = (bf16[128,2048]{1,0:T(8,128)(2,1)S(1)}, bf16[128,2048]{1,0:T(8,128)(2,1)S(1)}, u32[]{:S(2)}, u32[]{:S(2)}) collective-permute-start(bf16[128,2048]{1,0:T(8,128)(2,1)S(1)} %collective-permute-done.6.refs_7_.refs_1_), channel_id=1, source_target_pairs={{8,16},{16,8},{9,17},{17,9},{10,18},{18,10},{11,19},{19,11},{12,20... | collective-permute-start | bytes 1572872 | tf_op jit(solution)/shard_map/ppermute | solution.py:463
  35.2 16.0 %collective-permute-start.14 = (bf16[128,2048]{1,0:T(8,128)(2,1)S(1)}, bf16[128,2048]{1,0:T(8,128)(2,1)S(1)}, u32[]{:S(2)}, u32[]{:S(2)}) collective-permute-start(bf16[128,2048]{1,0:T(8,128)(2,1)S(1)} %collective-permute-done.12.refs_8_.refs_1_), channel_id=1, source_target_pairs={{8,0},{16,24},{9,1},{17,25},{10,2},{18,26},{11,3},{19,27},{12,4},{... | collective-permute-start | bytes 1572872 | tf_op jit(solution)/shard_map/ppermute | solution.py:463
  39.1 14.7 %collective-permute-start.16 = (bf16[128,2048]{1,0:T(8,128)(2,1)S(1)}, bf16[128,2048]{1,0:T(8,128)(2,1)S(1)}, u32[]{:S(2)}, u32[]{:S(2)}) collective-permute-start(bf16[128,2048]{1,0:T(8,128)(2,1)S(1)} %get-tuple-element.52.refs_3_.refs_0_), channel_id=1, source_target_pairs={{0,8},{24,16},{1,9},{25,17},{2,10},{26,18},{3,11},{27,19},{4,12},{... | collective-permute-start | bytes 1572872 | tf_op jit(solution)/shard_map/ppermute | solution.py:463
  46.3 12.6 %collective-permute-start.15 = (bf16[128,2048]{1,0:T(8,128)(2,1)S(1)}, bf16[128,2048]{1,0:T(8,128)(2,1)S(1)}, u32[]{:S(2)}, u32[]{:S(2)}) collective-permute-start(bf16[128,2048]{1,0:T(8,128)(2,1)S(1)} %add_and_pass.7.refs_0_.refs_2_), channel_id=1, source_target_pairs={{8,0},{16,24},{9,1},{17,25},{10,2},{18,26},{11,3},{19,27},{12,4},{... | collective-permute-start | bytes 1572872 | tf_op jit(solution)/shard_map/ppermute | solution.py:463
  49.9 14.2 %collective-permute-start.20 = (bf16[128,2048]{1,0:T(8,128)(2,1)S(1)}, bf16[128,2048]{1,0:T(8,128)(2,1)S(1)}, u32[]{:S(2)}, u32[]{:S(2)}) collective-permute-start(bf16[128,2048]{1,0:T(8,128)(2,1)S(1)} %get-tuple-element.56.refs_0_), channel_id=1, source_target_pairs={{0,8},{24,16},{1,9},{25,17},{2,10},{26,18},{3,11},{27,19},{4,12},{... | collective-permute-start | bytes 1572872 | tf_op jit(solution)/shard_map/ppermute | solution.py:463
  51.2 16.9 %collective-permute-start.17 = (bf16[256,1024]{1,0:T(8,128)(2,1)S(1)}, bf16[256,1024]{1,0:T(8,128)(2,1)S(1)}, u32[]{:S(2)}, u32[]{:S(2)}) collective-permute-start(bf16[256,1024]{1,0:T(8,128)(2,1)S(1)} %get-tuple-element.58), channel_id=1, source_target_pairs={{0,1},{1,0},{2,3},{3,2},{4,5},{5,4},{6,7},{7,6},{8,9},{9,8},{10,11... | collective-permute-start | bytes 1572872 | tf_op jit(solution)/shard_map/ppermute | solution.py:469
  53.9 17.9 %collective-permute-start.24 = (bf16[128,2048]{1,0:T(8,128)(2,1)S(1)}, bf16[128,2048]{1,0:T(8,128)(2,1)S(1)}, u32[]{:S(2)}, u32[]{:S(2)}) collective-permute-start(bf16[128,2048]{1,0:T(8,128)(2,1)S(1)} %add_and_pass.9.refs_4_), channel_id=1, source_target_pairs={{8,16},{16,8},{9,17},{17,9},{10,18},{18,10},{11,19},{19,11},{12,20... | collective-permute-start | bytes 1572872 | tf_op jit(solution)/shard_map/ppermute | solution.py:463
  61.3 6.7 %collective-permute-start.18 = (bf16[256,512]{1,0:T(8,128)(2,1)S(1)}, bf16[256,512]{1,0:T(8,128)(2,1)S(1)}, u32[]{:S(2)}, u32[]{:S(2)}) collective-permute-start(bf16[256,512]{1,0:T(8,128)(2,1)S(1)} %get-tuple-element.59), channel_id=1, source_target_pairs={{0,1},{1,0},{2,3},{3,2},{4,5},{5,4},{6,7},{7,6},{8,9},{9,8},{10,11... | collective-permute-start | bytes 786440 | tf_op jit(solution)/shard_map/ppermute | solution.py:469
  61.4 6.7 %collective-permute-start.19 = (bf16[256,512]{1,0:T(8,128)(2,1)S(1)}, bf16[256,512]{1,0:T(8,128)(2,1)S(1)}, u32[]{:S(2)}, u32[]{:S(2)}) collective-permute-start(bf16[256,512]{1,0:T(8,128)(2,1)S(1)} %get-tuple-element.60), channel_id=1, source_target_pairs={{0,1},{1,0},{2,3},{3,2},{4,5},{5,4},{6,7},{7,6},{8,9},{9,8},{10,11... | collective-permute-start | bytes 786440 | tf_op jit(solution)/shard_map/ppermute | solution.py:469
  64.2 22.7 %collective-permute-start.30 = (bf16[128,2048]{1,0:T(8,128)(2,1)S(1)}, bf16[128,2048]{1,0:T(8,128)(2,1)S(1)}, u32[]{:S(2)}, u32[]{:S(2)}) collective-permute-start(bf16[128,2048]{1,0:T(8,128)(2,1)S(1)} %add_and_pass.10.refs_5_), channel_id=1, source_target_pairs={{8,16},{16,8},{9,17},{17,9},{10,18},{18,10},{11,19},{19,11},{12,20... | collective-permute-start | bytes 1572872 | tf_op jit(solution)/shard_map/ppermute | solution.py:463
  68.3 12.0 %collective-permute-start.21 = (bf16[128,1024]{1,0:T(8,128)(2,1)S(1)}, bf16[128,1024]{1,0:T(8,128)(2,1)S(1)}, u32[]{:S(2)}, u32[]{:S(2)}) collective-permute-start(bf16[128,1024]{1,0:T(8,128)(2,1)S(1)} %get-tuple-element.62), channel_id=1, source_target_pairs={{0,2},{1,3},{2,0},{3,1},{4,6},{5,7},{6,4},{7,5},{8,10},{9,11},{10,... | collective-permute-start | bytes 786440 | tf_op jit(solution)/shard_map/ppermute | solution.py:466
  69.4 11.1 %collective-permute-start.22 = (bf16[128,1024]{1,0:T(8,128)(2,1)S(1)}, bf16[128,1024]{1,0:T(8,128)(2,1)S(1)}, u32[]{:S(2)}, u32[]{:S(2)}) collective-permute-start(bf16[128,1024]{1,0:T(8,128)(2,1)S(1)} %get-tuple-element.63), channel_id=1, source_target_pairs={{0,4},{1,5},{2,6},{3,7},{4,0},{5,1},{6,2},{7,3},{8,12},{9,13},{10,... | collective-permute-start | bytes 786440 | tf_op jit(solution)/shard_map/ppermute | solution.py:466
  70.8 9.7 %collective-permute-start.23 = (bf16[128,1024]{1,0:T(8,128)(2,1)S(1)}, bf16[128,1024]{1,0:T(8,128)(2,1)S(1)}, u32[]{:S(2)}, u32[]{:S(2)}) collective-permute-start(bf16[128,1024]{1,0:T(8,128)(2,1)S(1)} %get-tuple-element.64), channel_id=1, source_target_pairs={{0,6},{1,7},{2,4},{3,5},{4,2},{5,3},{6,0},{7,1},{8,14},{9,15},{10,... | collective-permute-start | bytes 786440 | tf_op jit(solution)/shard_map/ppermute | solution.py:466
  72.0 18.2 %collective-permute-start.29 = (bf16[128,2048]{1,0:T(8,128)(2,1)S(1)}, bf16[128,2048]{1,0:T(8,128)(2,1)S(1)}, u32[]{:S(2)}, u32[]{:S(2)}) collective-permute-start(bf16[128,2048]{1,0:T(8,128)(2,1)S(1)} %add_and_pass.11.refs_5_), channel_id=1, source_target_pairs={{0,8},{8,0},{16,24},{24,16},{1,9},{9,1},{17,25},{25,17},{2,10},{10... | collective-permute-start | bytes 1572872 | tf_op jit(solution)/shard_map/ppermute | solution.py:463
  80.7 11.2 %collective-permute-start.26 = (bf16[32,1024]{1,0:T(8,128)(2,1)S(1)}, bf16[32,1024]{1,0:T(8,128)(2,1)S(1)}, u32[]{:S(2)}, u32[]{:S(2)}) collective-permute-start(bf16[32,1024]{1,0:T(8,128)(2,1)S(1)} %get-tuple-element.70), channel_id=1, source_target_pairs={{0,8},{1,9},{2,0},{3,1},{4,24},{5,25},{6,16},{7,17},{8,10},{9,11},... | collective-permute-start | bytes 196616 | tf_op jit(solution)/shard_map/ppermute | solution.py:524
  82.0 9.9 %collective-permute-start.27 = (bf16[32,1024]{1,0:T(8,128)(2,1)S(1)}, bf16[32,1024]{1,0:T(8,128)(2,1)S(1)}, u32[]{:S(2)}, u32[]{:S(2)}) collective-permute-start(bf16[32,1024]{1,0:T(8,128)(2,1)S(1)} %get-tuple-element.71), channel_id=1, source_target_pairs={{0,16},{1,17},{2,24},{3,25},{4,0},{5,1},{6,8},{7,9},{8,18},{9,19},... | collective-permute-start | bytes 196616 | tf_op jit(solution)/shard_map/ppermute | solution.py:524
  83.6 8.3 %collective-permute-start.28 = (bf16[32,1024]{1,0:T(8,128)(2,1)S(1)}, bf16[32,1024]{1,0:T(8,128)(2,1)S(1)}, u32[]{:S(2)}, u32[]{:S(2)}) collective-permute-start(bf16[32,1024]{1,0:T(8,128)(2,1)S(1)} %get-tuple-element.72), channel_id=1, source_target_pairs={{0,24},{1,25},{2,16},{3,17},{4,8},{5,9},{6,0},{7,1},{8,26},{9,27},... | collective-permute-start | bytes 196616 | tf_op jit(solution)/shard_map/ppermute | solution.py:524
  87.0 8.1 %collective-permute-start.25 = (bf16[32,1024]{1,0:T(8,128)(2,1)S(1)}, bf16[32,1024]{1,0:T(8,128)(2,1)S(1)}, u32[]{:S(2)}, u32[]{:S(2)}) collective-permute-start(bf16[32,1024]{1,0:T(8,128)(2,1)S(1)} %get-tuple-element.69.refs_5_), channel_id=1, source_target_pairs={{0,0},{1,1},{2,8},{3,9},{4,16},{5,17},{6,24},{7,25},{8,2},{9,3},{1... | collective-permute-start | bytes 196616 | tf_op jit(solution)/shard_map/ppermute | solution.py:524
